TPU v7x, 32 devices: a whole 2x2x4 slice. The times are simulated.
32 devices in a mesh: prow: 8 (over z, y), pcol: 4 (over x, core).
Axes of the slice: x: 2, y: 2, z: 4, core: 2. Of those that a mesh axis runs over, the one named last changes fastest.
Arguments:
- front: float32 [8, 8, 16, 4, 128, 128], P(None, 'prow', None, 'pcol'), may hold values from -6 to 6, as said below
- child_blocks: float32 [1024, 128, 128], P(('prow', 'pcol')), may hold values from -3 to 3
- owners: int32 [1024, 1], P(('prow', 'pcol')), may hold values from 0 to 31; in each aligned block of 32 rows (0 to 31, 32 to 63, ...) at most 2 rows name the same one
- slots: int32 [1024], P(('prow', 'pcol')), may hold values from 1 to 127
- pattern: int32 [2, 64], replicated, may hold values 0 or 1
Outputs:
- factored: float32 [8, 8, 16, 4, 128, 128], P(None, 'prow', None, 'pcol')
Inputs may be any that keep to these rules, and one draw needn't show every extreme that they name: `front`: in the leading 2 * 256 rows and columns, off-diagonal entries lie within 2 / 512 in magnitude and diagonal entries within 3 to 5. `owners`: among the 32 child blocks of one device no owner is named more than 2 times; some owner is named exactly 2 times. `slots`: slot 0 never occurs.
All inputs are finite; a program needn't handle non-finite values.
Results may differ from a plain program's by a relative error of at most 0.0001.
Values sent between devices are 32-bit elements; how exact they have to be, the bound alone decides.
No kernel may reach another device: no remote copies, remote signals or barrier semaphores. Data moves between devices by JAX's collectives and lax.ppermute only.
A program may use at most 192 MiB of HBM per device.

v0:
```python
import functools

import jax
import jax.numpy as jnp
from jax import lax
from jax.experimental import pallas as pl
from jax.experimental.pallas import tpu as pltpu
from jax.sharding import PartitionSpec as P

ALL = ("prow", "pcol")
HIGHEST = lax.Precision.HIGHEST
VMEM_LIMIT = 56 * 2**20
WHOLE = pl.BlockSpec(memory_space=pltpu.VMEM)
HBM = pl.BlockSpec(memory_space=pl.ANY)


def bits_of(size):
    return size.bit_length() - 1


def xor_send(x, axis, bit):
    size = lax.axis_size(axis)
    return lax.ppermute(x, axis, [(i, i ^ (1 << bit)) for i in range(size)])


def my_bit(axis, bit):
    return (lax.axis_index(axis) >> bit) & 1


def gather_bit(x, axis, bit):
    other = xor_send(x, axis, bit)
    low = my_bit(axis, bit) == 0
    return jnp.stack([jnp.where(low, x, other), jnp.where(low, other, x)])


def spread_high(x, axis, low_bits):
    for bit in range(low_bits, bits_of(lax.axis_size(axis))):
        other = lax.ppermute(x, axis, [(i, i | (1 << bit)) for i in range(1 << bit)])
        x = jnp.where(my_bit(axis, bit) == 1, other, x)
    return x


def nt_dot(a, b):
    return lax.dot_general(a, b, (((1,), (1,)), ((), ())), preferred_element_type=jnp.float32)


def split(x):
    high = x.astype(jnp.bfloat16)
    return high, (x - high.astype(jnp.float32)).astype(jnp.bfloat16)


def nt_dot3(a, b):
    return nt_dot(a[0], b[0]) + (nt_dot(a[1], b[0]) + nt_dot(a[0], b[1]))


def after_kernel(x_ref, *refs):
    pass


def after(x, *others):
    return pl.pallas_call(
        after_kernel,
        out_shape=jax.ShapeDtypeStruct(x.shape, x.dtype),
        in_specs=[HBM] * (1 + len(others)),
        out_specs=HBM,
        input_output_aliases={0: 0},
        name="after",
    )(x, *others)


def pack_kernel(owner_ref, rank_ref, child_ref, first_ref, second_ref, sem):
    count = child_ref.shape[0]

    def to_first(k):
        return pltpu.make_async_copy(child_ref.at[k], first_ref.at[owner_ref[k]], sem.at[k])

    def to_second(k):
        return pltpu.make_async_copy(child_ref.at[k], second_ref.at[owner_ref[k]], sem.at[k])

    for k in range(count):
        pl.when(rank_ref[k] == 0)(lambda k=k: to_first(k).start())
        pl.when(rank_ref[k] != 0)(lambda k=k: to_second(k).start())
    for k in range(count):
        pl.when(rank_ref[k] == 0)(lambda k=k: to_first(k).wait())
        pl.when(rank_ref[k] != 0)(lambda k=k: to_second(k).wait())


def pack(owner_ids, rank, child_blocks, devices):
    count, tile, _ = child_blocks.shape
    shape = jax.ShapeDtypeStruct((devices, tile, tile), jnp.float32)
    return pl.pallas_call(
        pack_kernel,
        out_shape=(shape, shape),
        grid_spec=pltpu.PrefetchScalarGridSpec(
            num_scalar_prefetch=2,
            grid=(),
            in_specs=[WHOLE],
            out_specs=(HBM, HBM),
            scratch_shapes=[pltpu.SemaphoreType.DMA((count,))],
        ),
        compiler_params=pltpu.CompilerParams(vmem_limit_bytes=VMEM_LIMIT),
        name="pack_children",
    )(owner_ids, rank, child_blocks)


def strip_kernel(row_ref, strip_ref, got_ref, earlier_ref, out_ref, buffer, sem):
    sources = got_ref.shape[0]

    def copy(s):
        return pltpu.make_async_copy(got_ref.at[s], buffer.at[s], sem.at[s])

    for s in range(sources):
        pl.when(row_ref[s] >= 0)(lambda s=s: copy(s).start())
    out_ref[...] = strip_ref[...]
    for s in range(sources):

        @pl.when(row_ref[s] >= 0)
        def _(s=s):
            copy(s).wait()
            out_ref[row_ref[s]] = out_ref[row_ref[s]] + buffer[s]


def add_to_strip(panel_row, strip, got, earlier):
    return pl.pallas_call(
        strip_kernel,
        out_shape=jax.ShapeDtypeStruct(strip.shape, jnp.float32),
        grid_spec=pltpu.PrefetchScalarGridSpec(
            num_scalar_prefetch=1,
            grid=(),
            in_specs=[WHOLE, HBM, HBM],
            out_specs=WHOLE,
            scratch_shapes=[
                pltpu.VMEM(got.shape, jnp.float32),
                pltpu.SemaphoreType.DMA((got.shape[0],)),
            ],
        ),
        compiler_params=pltpu.CompilerParams(vmem_limit_bytes=VMEM_LIMIT),
        name="add_panel_children",
    )(panel_row, strip, got, earlier)


def exact_dot(a, b, dims):
    return lax.dot_general(a, b, (dims, ((), ())), precision=HIGHEST, preferred_element_type=jnp.float32)


def inverse_root(x):
    y = lax.rsqrt(x)
    return y * (1.5 - 0.5 * x * y * y)


def eliminate(work_ref, right_ref, t_ref, z_ref):
    n = work_ref.shape[0]
    row = lax.broadcasted_iota(jnp.int32, (n, n), 0)
    col = lax.broadcasted_iota(jnp.int32, (n, n), 1)
    right_ref[...] = jnp.where(row == col, 1.0, 0.0)
    for j in range(0, n, 2):
        lo = j // 8 * 8
        i = j - lo
        a = work_ref[lo:, :]
        z = right_ref[lo:, :]
        col0 = jnp.broadcast_to(a[:, j : j + 1], a.shape)
        col1 = jnp.broadcast_to(a[:, j + 1 : j + 2], a.shape)
        inv0 = inverse_root(col0[i : i + 1, :])
        row0 = a[i : i + 1, :] * inv0
        low0 = col0 * inv0
        cross = low0[i + 1 : i + 2, :]
        low1 = col1 - low0 * cross
        inv1 = inverse_root(low1[i + 1 : i + 2, :])
        row1 = (a[i + 1 : i + 2, :] - cross * row0) * inv1
        low1 = low1 * inv1
        z0 = z[i : i + 1, :] * inv0
        z1 = (z[i + 1 : i + 2, :] - cross * z0) * inv1
        if j + 2 < n:
            work_ref[lo:, :] = a - low0 * row0 - low1 * row1
            right_ref[lo:, :] = z - low0 * z0 - low1 * z1
        t_ref[j : j + 1, :] = row0
        t_ref[j + 1 : j + 2, :] = row1
        z_ref[j : j + 1, :] = z0
        z_ref[j + 1 : j + 2, :] = z1


def lower_of(t):
    n = t.shape[0]
    row = lax.broadcasted_iota(jnp.int32, (n, n), 0)
    col = lax.broadcasted_iota(jnp.int32, (n, n), 1)
    return jnp.where(col <= row, t.T, 0.0)


def symmetric(block):
    n = block.shape[0]
    row = lax.broadcasted_iota(jnp.int32, (n, n), 0)
    col = lax.broadcasted_iota(jnp.int32, (n, n), 1)
    return jnp.where(col <= row, block, block.T)


def factor_panel(g, scratch):
    work, right, t, z = scratch
    nt, nn = ((1,), (1,)), ((1,), (0,))
    work[...] = symmetric(g[0][0])
    eliminate(work, right, t, z)
    l00, z00 = lower_of(t[...]), z[...]
    l10 = exact_dot(g[1][0], z00, nt)
    work[...] = symmetric(g[1][1]) - exact_dot(l10, l10, nt)
    eliminate(work, right, t, z)
    l11, z11 = lower_of(t[...]), z[...]
    z10 = -exact_dot(z11, exact_dot(l10, z00, nn), nn)
    return (l00, l10, l11), (z00, z10, z11)


def store_square(ref, blocks):
    tile = blocks[0].shape[0]
    ref[:tile, :tile] = blocks[0]
    ref[:tile, tile:] = jnp.zeros((tile, tile), ref.dtype)
    ref[tile:, :tile] = blocks[1]
    ref[tile:, tile:] = blocks[2]


def leading_block(ref, i, j):
    return ref[j % 2, j // 2, i % 2, i // 2]


def panel0_kernel(corner_ref, l_ref, zh_ref, zl_ref, *scratch):
    g = [[leading_block(corner_ref, i, j) for j in range(2)] for i in range(2)]
    lower, inverse = factor_panel(g, scratch)
    store_square(l_ref, lower)
    parts = [split(block) for block in inverse]
    store_square(zh_ref, [part[0] for part in parts])
    store_square(zl_ref, [part[1] for part in parts])


def panel1_kernel(keep_ref, corner_ref, z0h_ref, z0l_ref, earlier_ref, a_ref, ah_ref, al_ref, l_ref, zh_ref, zl_ref, *scratch):
    tile = corner_ref.shape[-1]
    z0 = (z0h_ref[...], z0l_ref[...])
    rows = [jnp.concatenate([leading_block(corner_ref, 2 + i, j) for j in range(2)], axis=1) for i in range(2)]
    a = jnp.concatenate([nt_dot3(split(rows[i]), z0) * keep_ref[i].astype(jnp.float32) for i in range(2)], axis=0)
    a_ref[...] = a
    ah_ref[...], al_ref[...] = split(a)
    update = exact_dot(a, a, ((1,), (1,)))
    g = [
        [leading_block(corner_ref, 2 + i, 2 + j) - update[i * tile : (i + 1) * tile, j * tile : (j + 1) * tile] for j in range(2)]
        for i in range(2)
    ]
    lower, inverse = factor_panel(g, scratch)
    store_square(l_ref, lower)
    parts = [split(block) for block in inverse]
    store_square(zh_ref, [part[0] for part in parts])
    store_square(zl_ref, [part[1] for part in parts])


def factor_panel0(corner):
    tile = corner.shape[-1]
    full = jax.ShapeDtypeStruct((2 * tile, 2 * tile), jnp.float32)
    part = jax.ShapeDtypeStruct((2 * tile, 2 * tile), jnp.bfloat16)
    return pl.pallas_call(
        panel0_kernel,
        out_shape=(full, part, part),
        in_specs=[WHOLE],
        out_specs=(WHOLE,) * 3,
        scratch_shapes=[pltpu.VMEM((tile, tile), jnp.float32)] * 4,
        compiler_params=pltpu.CompilerParams(vmem_limit_bytes=VMEM_LIMIT),
        name="factor_panel0",
    )(corner)


def factor_panel1(corner, keep, z0, earlier):
    tile = corner.shape[-1]
    full = jax.ShapeDtypeStruct((2 * tile, 2 * tile), jnp.float32)
    part = jax.ShapeDtypeStruct((2 * tile, 2 * tile), jnp.bfloat16)
    return pl.pallas_call(
        panel1_kernel,
        out_shape=(full, part, part, full, part, part),
        grid_spec=pltpu.PrefetchScalarGridSpec(
            num_scalar_prefetch=1,
            grid=(),
            in_specs=[WHOLE] * 3 + [HBM],
            out_specs=(WHOLE,) * 6,
            scratch_shapes=[pltpu.VMEM((tile, tile), jnp.float32)] * 4,
        ),
        compiler_params=pltpu.CompilerParams(vmem_limit_bytes=VMEM_LIMIT),
        name="factor_panel1",
    )(keep, corner, *z0, earlier)


def solve_kernel(with_panel, keep0_ref, keep1_ref, place_ref, *refs):
    x_refs, factor_refs, rest = refs[:4], refs[4:10], refs[10:]
    high_ref, low_ref, xs = rest[0], rest[1], rest[-1]
    n = pl.program_id(0)
    depth, tile, _ = x_refs[0].shape
    for m in range(4):
        xs[place_ref[0] ^ m] = x_refs[m][...].reshape(depth * tile, tile)
    z0, a, z1 = [(factor_refs[2 * i][...], factor_refs[2 * i + 1][...]) for i in range(3)]

    def masked(q, keep_ref):
        return jnp.concatenate(
            [q[i * tile : (i + 1) * tile] * keep_ref[n * depth + i].astype(jnp.float32) for i in range(depth)], axis=0
        )

    x0 = jnp.concatenate([xs[0], xs[1]], axis=1)
    x1 = jnp.concatenate([xs[2], xs[3]], axis=1)
    q0 = masked(nt_dot3(split(x0), z0), keep0_ref)
    q0_parts = split(q0)
    q1 = masked(nt_dot3(split(x1 - nt_dot3(q0_parts, a)), z1), keep1_ref)
    q1_parts = split(q1)
    width = 2 * tile
    for ref, index in ((high_ref, 0), (low_ref, 1)):
        ref[:, :width] = q0_parts[index]
        ref[:, width:] = q1_parts[index]
    if with_panel:
        xs[0] = q0[:, :tile]
        xs[1] = q0[:, tile:]
        xs[2] = q1[:, :tile]
        xs[3] = q1[:, tile:]
        rest[2][...] = xs[place_ref[0]].reshape(depth, tile, tile)


def solve(strips, keep0, keep1, place, factors, with_panel):
    rows, tile, _ = strips[0].shape
    depth = rows // 2
    part = jax.ShapeDtypeStruct((rows * tile, 4 * tile), jnp.bfloat16)
    row_spec = pl.BlockSpec((depth * tile, 4 * tile), lambda n, *_: (n, 0))
    strip_spec = pl.BlockSpec((depth, tile, tile), lambda n, *_: (n, 0, 0))
    out_shape, out_specs = [part, part], [row_spec, row_spec]
    if with_panel:
        out_shape.append(jax.ShapeDtypeStruct((rows, tile, tile), jnp.float32))
        out_specs.append(strip_spec)
    return pl.pallas_call(
        functools.partial(solve_kernel, with_panel),
        out_shape=tuple(out_shape),
        grid_spec=pltpu.PrefetchScalarGridSpec(
            num_scalar_prefetch=3,
            grid=(rows // depth,),
            in_specs=[strip_spec] * 4 + [WHOLE] * 6,
            out_specs=tuple(out_specs),
            scratch_shapes=[pltpu.VMEM((4, depth * tile, tile), jnp.float32)],
        ),
        compiler_params=pltpu.CompilerParams(vmem_limit_bytes=VMEM_LIMIT),
        name="solve_rows" if with_panel else "solve_columns",
    )(keep0, keep1, place, *strips, *factors)


def final_kernel(panel_blocks, first_ref, second_ref, place_ref, front_ref, got1_ref, got2_ref, high_ref, low_ref,
                 panel_ref, l0_ref, a_ref, l1_ref, *rest):
    cols, out_ref = rest[:-1], rest[-1]
    step = pl.program_id(0)
    depth, _, bcols, _, tile, _ = front_ref.shape
    my_row, my_col, grid_rows, my_high = place_ref[0], place_ref[1], place_ref[2], place_ref[3]
    highs = len(cols) // 2
    rows = (high_ref[...], low_ref[...])
    for index in range(highs):
        col_high, col_low = cols[2 * index], cols[2 * index + 1]
        for at in range(0, bcols // highs, 2):
            piece = slice(at * tile, (at + 2) * tile)
            update = nt_dot3(rows, (col_high[piece, :], col_low[piece, :]))
            for k in range(2):
                b = (at + k) * highs + (my_high ^ index)
                for a in range(depth):
                    out_ref[a, 0, b, 0] = (
                        front_ref[a, 0, b, 0] - update[a * tile : (a + 1) * tile, k * tile : (k + 1) * tile]
                    )

    def add(list_ref, got_ref):
        def body(k, carry):
            slot = list_ref[1, k]
            a, b = slot // bcols - step * depth, slot % bcols
            out_ref[a, 0, b, 0] = out_ref[a, 0, b, 0] + got_ref[list_ref[0, k]]
            return carry

        lax.fori_loop(list_ref[2, step], list_ref[2, step + 1], body, 0)

    add(first_ref, got1_ref)
    add(second_ref, got2_ref)

    for a in range(depth):
        block_row = (step * depth + a) * grid_rows + my_row

        @pl.when(block_row < panel_blocks)
        def _(a=a):
            out_ref[a] = jnp.zeros(out_ref.shape[1:], jnp.float32)

        @pl.when(my_col < panel_blocks)
        def _(a=a):
            out_ref[a, 0, 0, 0] = panel_ref[a]

        for i in range(panel_blocks):
            for j in range(panel_blocks):

                @pl.when((block_row == i) & (my_col == j))
                def _(a=a, i=i, j=j):
                    ref = (l0_ref, None, a_ref, l1_ref)[i // 2 * 2 + j // 2]
                    rows_at, cols_at = i % 2 * tile, j % 2 * tile
                    if ref is None:
                        out_ref[a, 0, 0, 0] = jnp.zeros((tile, tile), jnp.float32)
                    else:
                        out_ref[a, 0, 0, 0] = ref[rows_at : rows_at + tile, cols_at : cols_at + tile]


def finish(depth, first, second, place, front, got1, got2, row_high, row_low, panel, corners, cols, panel_blocks):
    brows, _, bcols, _, tile, _ = front.shape
    big = pl.BlockSpec((depth, 1, bcols, 1, tile, tile), lambda i, *_: (i, 0, 0, 0, 0, 0))
    rows = pl.BlockSpec((depth * tile, row_high.shape[1]), lambda i, *_: (i, 0))
    return pl.pallas_call(
        functools.partial(final_kernel, panel_blocks),
        out_shape=jax.ShapeDtypeStruct(front.shape, jnp.float32),
        grid_spec=pltpu.PrefetchScalarGridSpec(
            num_scalar_prefetch=3,
            grid=(brows // depth,),
            in_specs=[big, WHOLE, WHOLE, rows, rows, pl.BlockSpec((depth, tile, tile), lambda i, *_: (i, 0, 0))]
            + [WHOLE] * (3 + len(cols)),
            out_specs=big,
        ),
        compiler_params=pltpu.CompilerParams(vmem_limit_bytes=VMEM_LIMIT),
        name="schur_update",
    )(first, second, place, front, got1, got2, row_high, row_low, panel, *corners, *cols)


def by_slot(slots, per_step, steps):
    count = slots.shape[0]
    index = jnp.arange(count, dtype=jnp.int32)
    key = jnp.where(slots > 0, slots, per_step * steps) * count + index
    place = jnp.sum((key[None, :] < key[:, None]).astype(jnp.int32), axis=1)
    at = place[None, :] == index[:, None]
    sources = jnp.sum(jnp.where(at, index[None, :], 0), axis=1)
    ordered = jnp.sum(jnp.where(at, slots[None, :], 0), axis=1)
    bound = jnp.minimum(index, steps) * per_step
    starts = jnp.sum(((slots > 0)[None, :] & (slots[None, :] < bound[:, None])).astype(jnp.int32), axis=1)
    return jnp.stack([sources, ordered, starts])


def local(front, child_blocks, owners, slots, pattern):
    grid_rows = lax.axis_size("prow")
    grid_cols = lax.axis_size("pcol")
    devices = grid_rows * grid_cols
    rank_r = lax.axis_index("prow")
    rank_c = lax.axis_index("pcol")
    me = rank_r * grid_cols + rank_c
    brows, _, bcols, _, tile, _ = front.shape
    row_bits, col_bits = bits_of(grid_rows), bits_of(grid_cols)
    panel_blocks = 2 * pattern.shape[0]
    panel_bits = bits_of(panel_blocks)
    owner_ids = owners[:, 0]
    children = owner_ids.shape[0]

    index = jnp.arange(children, dtype=jnp.int32)
    is_panel = (slots % bcols == 0) & (owner_ids % grid_cols < panel_blocks)
    same = owner_ids[:, None] == owner_ids[None, :]
    ahead = jnp.where(is_panel[:, None] == is_panel[None, :], index[None, :] < index[:, None], is_panel[None, :])
    rank = jnp.sum((same & ahead).astype(jnp.int32), axis=1)
    late = is_panel & (rank == 1)

    to = owner_ids[None, :] == jnp.arange(devices, dtype=jnp.int32)[:, None]
    lane = jnp.arange(tile, dtype=jnp.int32)[None, :]
    slot1 = jnp.sum(jnp.where(to & (rank == 0)[None, :], slots[None, :], 0), axis=1, keepdims=True)
    slot2 = jnp.sum(jnp.where(to & (rank == 1)[None, :], slots[None, :], 0), axis=1, keepdims=True)
    late_count = jnp.sum(late.astype(jnp.int32))
    notes = jnp.where(lane == 0, slot1, jnp.where(lane == 1, slot2, late_count))
    got_notes = lax.all_to_all(notes[:, None, :], ALL, 0, 0, tiled=True)[:, 0]

    send1, send2 = pack(owner_ids, rank, child_blocks, devices)
    got1 = lax.all_to_all(send1, ALL, 0, 0, tiled=True)

    corner = front[0, 0, 0, 0]
    corner = spread_high(corner, "prow", panel_bits)
    corner = spread_high(corner, "pcol", panel_bits)
    for bit in reversed(range(panel_bits)):
        corner = gather_bit(corner, "prow", bit)
    for bit in reversed(range(panel_bits)):
        corner = gather_bit(corner, "pcol", bit)
    l0, *z0 = factor_panel0(corner)

    first_slots, second_slots = got_notes[:, 0], got_notes[:, 1]

    def panel_here(slot):
        return (slot % bcols == 0) & (slot > 0) & (rank_c < panel_blocks)

    panel_row = jnp.where(panel_here(first_slots), first_slots // bcols, -1)
    depth = brows // 4
    lists = [by_slot(jnp.where(panel_here(s), 0, s), depth * bcols, brows // depth) for s in (first_slots, second_slots)]

    strip = front[:, 0, 0, 0]
    rounds = jnp.max(got_notes[:, 2])
    order = jnp.cumsum(late.astype(jnp.int32))

    def deliver(turn, strip):
        chosen = late & (order == turn + 1)
        block = child_blocks[jnp.argmax(chosen)]
        note = jnp.where(lane == 0, jnp.sum(jnp.where(chosen, owner_ids + 1, 0)), jnp.sum(jnp.where(chosen, slots, 0)))
        block = jnp.concatenate([block, jnp.broadcast_to(note, (8, tile)).astype(jnp.float32)], axis=0)
        for axis, bits in (("prow", row_bits), ("pcol", col_bits)):
            for bit in reversed(range(bits)):
                block = gather_bit(block, axis, bit)
        blocks = block.reshape(devices, tile + 8, tile)
        note = blocks[:, tile, :2].astype(jnp.int32)
        here = note[:, 0] == me + 1
        rows = jnp.where(here, note[:, 1] // bcols, 0)
        return strip.at[rows].add(jnp.where(here[:, None, None], blocks[:, :tile], 0.0))

    strip = lax.fori_loop(0, rounds, deliver, strip)
    strip = add_to_strip(panel_row, strip, got1, l0)
    strip = spread_high(strip, "pcol", panel_bits)

    across = xor_send(strip, "pcol", 1)
    row_strips = [strip, xor_send(strip, "pcol", 0), across, xor_send(across, "pcol", 0)]
    a, ah, al, l1, *z1 = factor_panel1(corner, pattern[0, 2:4], z0, strip)
    factors = (*z0, ah, al, *z1)
    parts = [strip]
    for bit in range(col_bits, row_bits):
        parts = parts + [after(xor_send(part, "prow", bit), l1) for part in parts]
    highs = len(parts)

    def to_columns(part, m):
        pairs = [
            ((h * grid_cols + low) * grid_cols + c, (h * grid_cols + (c ^ m)) * grid_cols + low)
            for h in range(highs)
            for low in range(grid_cols)
            for c in range(grid_cols)
        ]
        return lax.ppermute(part, ALL, pairs)

    col_strips = [[to_columns(part, m) for m in range(panel_blocks)] for part in parts]
    got2 = lax.all_to_all(after(send2, l1), ALL, 0, 0, tiled=True)

    keep0, keep1 = pattern[0], jnp.maximum(pattern[0], pattern[1])
    my_high = rank_r // grid_cols
    rows_of = jnp.arange(brows, dtype=jnp.int32) * grid_rows
    blocks = rows_of + rank_r
    row_high, row_low, panel = solve(
        row_strips, keep0[blocks], keep1[blocks], (rank_c % panel_blocks)[None], factors, True
    )
    cols = []
    for high, strips in enumerate(col_strips):
        blocks = rows_of + (my_high ^ high) * grid_cols + rank_c
        cols += solve(strips, keep0[blocks], keep1[blocks], (rank_r % panel_blocks)[None], factors, False)
    place = jnp.stack([rank_r, rank_c, jnp.int32(grid_rows), my_high])
    return finish(
        depth, *lists, place, front, got1, got2, row_high, row_low, panel, (l0, a, l1), cols, panel_blocks
    )


def solution(mesh):
    placed = (
        P(None, "prow", None, "pcol", None, None),
        P(("prow", "pcol"), None, None),
        P(("prow", "pcol"), None),
        P(("prow", "pcol")),
        P(),
    )
    return jax.shard_map(
        local,
        mesh=mesh,
        in_specs=placed,
        out_specs=P(None, "prow", None, "pcol", None, None),
        check_vma=False,
    )
```

profile of v0, /device:TPU:9, one launch (start us, length us, event | category | flops | bytes accessed | tf_op | source)
XLA Modules:
  0.0 253.9 jit_solution(2788481580362474459)
XLA Ops:
  0.0 0.8 slice_bitcast_fusion.1
  0.8 4.2 %collective-permute-start.5 = (f32[128,128]{1,0:T(8,128)S(1)}, f32[128,128]{1,0:T(8,128)S(1)}, u32[]{:S(2)}, u32[]{:S(2)}) collective-permute-start(f32[128,128]{1,0:T(8,128)S(1)} %slice_bitcast_fusion.1), channel_id=1, source_target_pairs={{0,16},{4,20},{8,24},{12,28},{1,17},{5,21},{9,25},{13,29},{2,18},{... | collective-permute-start | bytes 196616 | tf_op jit(solution)/shard_map/ppermute | solution.py:38
  5.7 0.9 convert_reduce_fusion.4.rank_ref
  6.7 1.0 collective-permute-done.5
  7.6 0.8 broadcast_select_fusion
  9.2 2.5 collective-permute-done.6
  11.7 1.3 collective-permute-start.7
  13.0 0.8 select_reduce_fusion.6
  13.8 1.8 collective-permute-done.7
  15.6 1.3 collective-permute-start.8
  16.9 1.4 broadcast_select_fusion.2
  18.3 9.1 %all-to-all-start = ((s32[32,1,128]{2,1,0:T(1,128)}), s32[32,1,128]{2,1,0:T(1,128)S(1)}, u32[]{:S(2)}, u32[]{:S(2)}) async-start(s32[32,1,128]{2,1,0:T(1,128)} %broadcast_select_fusion.2), calls=%async_computation | async-start | bytes 32768 | tf_op jit(solution)/shard_map/all_to_all | solution.py:456
  27.4 1.1 slice_bitcast_fusion
  28.5 1.0 select_bitcast_fusion.13
  29.5 0.8 pad_maximum_fusion.7
  31.6 2.2 pack_children.1
  33.9 5.7 %all-to-all-start.1 = ((f32[32,128,128]{2,1,0:T(8,128)}), f32[32,128,128]{2,1,0:T(8,128)}, u32[]{:S(2)}, u32[]{:S(2)}) async-start(f32[32,128,128]{2,1,0:T(8,128)} %get-tuple-element.155), calls=%async_computation.1 | async-start | bytes 4194304 | tf_op jit(solution)/shard_map/all_to_all | solution.py:459
  39.6 0.8 slice_reduce_fusion
  41.0 1.1 select_bitcast_fusion.11
  42.1 1.1 pad_maximum_fusion.6.corner_ref
  43.2 17.4 %factor_panel0.1 = (f32[256,256]{1,0:T(8,128)}, bf16[256,256]{1,0:T(8,128)(2,1)}, bf16[256,256]{1,0:T(8,128)(2,1)}) custom-call(f32[2,2,2,2,128,128]{5,4,3,2,1,0:T(8,128)} %pad_maximum_fusion.6.corner_ref), custom_call_target="tpu_custom_call" | custom-call | tf_op jit(solution)/shard_map/factor_panel0/pallas_call | solution.py:254
  61.4 25.4 %all-to-all-done.1.got_ref.got1_ref = f32[32,128,128]{2,1,0:T(8,128)} async-done(((f32[32,128,128]{2,1,0:T(8,128)}), f32[32,128,128]{2,1,0:T(8,128)}, u32[]{:S(2)}, u32[]{:S(2)}) %all-to-all-start.1) | async-done | bytes 2097184 | tf_op jit(solution)/shard_map/all_to_all | solution.py:459
  86.8 2.8 %add_panel_children.1.earlier_ref.refs_0_ = f32[8,128,128]{2,1,0:T(8,128)} custom-call(s32[32]{0:T(128)} %get-tuple-element.232.row_ref, f32[8,128,128]{2,1,0:T(8,128)S(1)} %get-tuple-element.412, f32[32,128,128]{2,1,0:T(8,128)} %all-to-all-done.1.got_ref.got1_ref, f32[256,256]{1,0:T(8,128)} %get-tuple-element.160.earlier_ref.l0_ref), custom_call_target="tpu_custom_call" | custom-call | tf_op jit(solution)/shard_map/add_panel_children/pallas_call | solution.py:124
  89.6 19.0 %factor_panel1.1 = (f32[256,256]{1,0:T(8,128)}, bf16[256,256]{1,0:T(8,128)(2,1)}, bf16[256,256]{1,0:T(8,128)(2,1)}, f32[256,256]{1,0:T(8,128)}, bf16[256,256]{1,0:T(8,128)(2,1)}, /*index=5*/bf16[256,256]{1,0:T(8,128)(2,1)}) custom-call(s32[2]{0:T(128)} %slice_bitcast_fusion.3.keep_ref, f32[2,2,2,2,128,128]{5,4,3,2,1,0:T(8,128)} %pad_maximum_fusion.6.corner_ref, ...), custom_call_target="tpu_custom_call" | custom-call | tf_op jit(solution)/shard_map/factor_panel1/pallas_call | solution.py:269
  108.6 5.8 %all-to-all-start.2 = ((f32[32,128,128]{2,1,0:T(8,128)}), f32[32,128,128]{2,1,0:T(8,128)S(1)}, u32[]{:S(2)}, u32[]{:S(2)}) async-start(f32[32,128,128]{2,1,0:T(8,128)} %after.2), calls=%async_computation.2 | async-start | bytes 4194304 | tf_op jit(solution)/shard_map/all_to_all | solution.py:520
  114.5 1.2 gather_fusion.1
  115.7 1.1 gather_fusion
  116.8 1.2 gather_fusion.3
  118.0 1.2 gather_fusion.2
  119.2 2.1 collective-permute-start.17
  121.4 1.7 collective-permute-start.16
  123.1 1.2 gather_fusion.5
  124.3 1.2 gather_fusion.4
  126.1 1.0 collective-permute-start.15
  127.1 2.0 collective-permute-start.14
  129.1 2.2 collective-permute-start.13
  131.3 51.6 %collective-permute-done.17.x_ref = f32[8,128,128]{2,1,0:T(8,128)S(1)} collective-permute-done((f32[8,128,128]{2,1,0:T(8,128)S(1)}, f32[8,128,128]{2,1,0:T(8,128)S(1)}, u32[]{:S(2)}, u32[]{:S(2)}) %collective-permute-start.17) | collective-permute-done | bytes 524320 | tf_op jit(solution)/shard_map/ppermute | solution.py:23
  183.3 1.2 collective-permute-start.10
  185.5 4.1 %collective-permute-start.20 = (f32[8,128,128]{2,1,0:T(8,128)}, f32[8,128,128]{2,1,0:T(8,128)S(1)}, u32[]{:S(2)}, u32[]{:S(2)}) collective-permute-start(f32[8,128,128]{2,1,0:T(8,128)} %after.3), channel_id=1, source_target_pairs={{0,8},{1,12},{2,0},{3,4},{4,9},{5,13},{6,1},{7,5},{8,10},{9,14},{1... | collective-permute-start | bytes 1572872 | tf_op jit(solution)/shard_map/ppermute | solution.py:517
  189.6 1.3 collective-permute-start.19
  190.9 20.0 %collective-permute-done.11.refs_2_ = f32[8,128,128]{2,1,0:T(8,128)} collective-permute-done((f32[8,128,128]{2,1,0:T(8,128)S(1)}, f32[8,128,128]{2,1,0:T(8,128)}, u32[]{:S(2)}, u32[]{:S(2)}) %collective-permute-start.11) | collective-permute-done | bytes 524320 | tf_op jit(solution)/shard_map/ppermute | solution.py:23
  211.0 4.3 %collective-permute-start.18 = (f32[8,128,128]{2,1,0:T(8,128)}, f32[8,128,128]{2,1,0:T(8,128)S(1)}, u32[]{:S(2)}, u32[]{:S(2)}) collective-permute-start(f32[8,128,128]{2,1,0:T(8,128)} %after.3), channel_id=1, source_target_pairs={{0,0},{1,4},{2,8},{3,12},{4,1},{5,5},{6,9},{7,13},{8,2},{9,6},{10,... | collective-permute-start | bytes 1572872 | tf_op jit(solution)/shard_map/ppermute | solution.py:517
  217.0 5.7 %solve_columns.2 = (bf16[1024,512]{1,0:T(8,128)(2,1)}, bf16[1024,512]{1,0:T(8,128)(2,1)}) custom-call(s32[8]{0:T(128)} %gather_fusion.2, s32[8]{0:T(128)} %gather_fusion.3, s32[1]{0:T(128)} %bitcast.28.place_ref, f32[8,128,128]{2,1,0:T(8,128)} %collective-permute-done.13.refs_0_, f32[8,128,128]{2,1,0:T(8,128)} %collective-permute-done.14.refs_1_, ...), custom_call_target="tpu_custom_call" | custom-call | tf_op jit(solution)/shard_map/solve_columns/pallas_call | solution.py:326
  223.5 5.8 %solve_rows.1 = (bf16[1024,512]{1,0:T(8,128)(2,1)}, bf16[1024,512]{1,0:T(8,128)(2,1)}, f32[8,128,128]{2,1,0:T(8,128)}) custom-call(s32[8]{0:T(128)} %gather_fusion, s32[8]{0:T(128)} %gather_fusion.1, s32[1]{0:T(128)} %bitcast.26.place_ref, f32[8,128,128]{2,1,0:T(8,128)} %add_panel_children.1.earlier_ref.refs_0_, ...), custom_call_target="tpu_custom_call" | custom-call | tf_op jit(solution)/shard_map/solve_rows/pallas_call | solution.py:326
  230.5 0.8 copy-done.8
  231.2 5.7 %solve_columns.3 = (bf16[1024,512]{1,0:T(8,128)(2,1)}, bf16[1024,512]{1,0:T(8,128)(2,1)}) custom-call(s32[8]{0:T(128)} %gather_fusion.4, s32[8]{0:T(128)} %gather_fusion.5, s32[1]{0:T(128)} %bitcast.28.place_ref, f32[8,128,128]{2,1,0:T(8,128)} %copy-done.8, f32[8,128,128]{2,1,0:T(8,128)} %copy-done.7, f32[8,128,128]{2,1,0:T(8,128)} %copy-done.6, ...), custom_call_target="tpu_custom_call" | custom-call | tf_op jit(solution)/shard_map/solve_columns/pallas_call | solution.py:326
  237.0 1.3 copy-done
  238.3 15.7 %schur_update.1 = f32[8,1,16,1,128,128]{5,4,3,2,1,0:T(8,128)} custom-call(s32[3,32]{1,0:T(4,128)} %pad_add_fusion.first_ref, s32[3,32]{1,0:T(4,128)} %pad_add_fusion.1.second_ref, s32[4]{0:T(128)} %pad_add_fusion.2.place_ref, f32[8,1,16,1,128,128]{5,4,3,2,1,0:T(8,128)} %front_ref.1, f32[32,128,128]{2,1,0:T(8,128)} %all-to-all-done.1.got_ref.got1_ref, ...), custom_call_target="tpu_custom_call" | custom-call | tf_op jit(solution)/shard_map/schur_update/pallas_call | solution.py:401
  (77 shorter events, 9.7 us)
Async XLA Ops:
  0.8 6.8 %collective-permute-start.5 = (f32[128,128]{1,0:T(8,128)S(1)}, f32[128,128]{1,0:T(8,128)S(1)}, u32[]{:S(2)}, u32[]{:S(2)}) collective-permute-start(f32[128,128]{1,0:T(8,128)S(1)} %slice_bitcast_fusion.1), channel_id=1, source_target_pairs={{0,16},{4,20},{8,24},{12,28},{1,17},{5,21},{9,25},{13,29},{2,18},{... | collective-permute-start | bytes 196616 | tf_op jit(solution)/shard_map/ppermute | solution.py:38
  6.7 23.7 %copy-start.12 = (s32[32]{0:T(128)}, s32[32]{0:T(128)S(1)}, u32[]{:S(2)}) copy-start(s32[32]{0:T(128)S(1)} %convert_reduce_fusion.4.rank_ref) | copy-start | bytes 388
  8.5 3.2 %collective-permute-start.6 = (f32[128,128]{1,0:T(8,128)S(1)}, f32[128,128]{1,0:T(8,128)S(1)}, u32[]{:S(2)}, u32[]{:S(2)}) collective-permute-start(f32[128,128]{1,0:T(8,128)S(1)} %broadcast_select_fusion), channel_id=1, source_target_pairs={{0,8},{4,12},{8,0},{12,4},{16,24},{20,28},{24,16},{28,20},{1,9},{5... | collective-permute-start | bytes 196616 | tf_op jit(solution)/shard_map/ppermute | solution.py:23
  11.7 3.9 %collective-permute-start.7 = (f32[2,128,128]{2,1,0:T(8,128)S(1)}, f32[2,128,128]{2,1,0:T(8,128)S(1)}, u32[]{:S(2)}, u32[]{:S(2)}) collective-permute-start(f32[2,128,128]{2,1,0:T(8,128)S(1)} %pad_maximum_fusion.9), channel_id=1, source_target_pairs={{0,4},{4,0},{8,12},{12,8},{16,20},{20,16},{24,28},{28,24},{1,5},{5... | collective-permute-start | bytes 393224 | tf_op jit(solution)/shard_map/ppermute | solution.py:23
  13.8 16.9 %copy-start.13 = (s32[2,64]{1,0:T(2,128)S(1)}, s32[2,64]{1,0:T(2,128)}, u32[]{:S(2)}) copy-start(s32[2,64]{1,0:T(2,128)} %param.11) | copy-start | bytes 1540
  13.8 17.8 %copy-start.2 = (f32[32,128,128]{2,1,0:T(8,128)S(1)}, f32[32,128,128]{2,1,0:T(8,128)}, u32[]{:S(2)}) copy-start(f32[32,128,128]{2,1,0:T(8,128)} %child_ref.1) | copy-start | bytes 6291460
  13.8 17.8 %copy-start.10 = (s32[32,1]{0,1:T(1,128)S(1)}, s32[32,1]{0,1:T(1,128)}, u32[]{:S(2)}) copy-start(s32[32,1]{0,1:T(1,128)} %param.9) | copy-start | bytes 388
  15.6 12.9 %collective-permute-start.8 = (f32[2,2,128,128]{3,2,1,0:T(8,128)S(1)}, f32[2,2,128,128]{3,2,1,0:T(8,128)}, u32[]{:S(2)}, u32[]{:S(2)}) collective-permute-start(f32[2,2,128,128]{3,2,1,0:T(8,128)S(1)} %pad_maximum_fusion.8), channel_id=1, source_target_pairs={{0,2},{1,3},{2,0},{3,1},{4,6},{5,7},{6,4},{7,5},{8,10},{9,11},{10,... | collective-permute-start | bytes 786440 | tf_op jit(solution)/shard_map/ppermute | solution.py:23
  18.3 15.6 %all-to-all-start = ((s32[32,1,128]{2,1,0:T(1,128)}), s32[32,1,128]{2,1,0:T(1,128)S(1)}, u32[]{:S(2)}, u32[]{:S(2)}) async-start(s32[32,1,128]{2,1,0:T(1,128)} %broadcast_select_fusion.2), calls=%async_computation | async-start | bytes 32768 | tf_op jit(solution)/shard_map/all_to_all | solution.py:456
  30.3 10.6 %collective-permute-start.9 = (f32[2,2,2,128,128]{4,3,2,1,0:T(8,128)}, f32[2,2,2,128,128]{4,3,2,1,0:T(8,128)}, u32[]{:S(2)}, u32[]{:S(2)}) collective-permute-start(f32[2,2,2,128,128]{4,3,2,1,0:T(8,128)} %pad_maximum_fusion.7), channel_id=1, source_target_pairs={{0,1},{1,0},{2,3},{3,2},{4,5},{5,4},{6,7},{7,6},{8,9},{9,8},{10,11... | collective-permute-start | bytes 1572872 | tf_op jit(solution)/shard_map/ppermute | solution.py:23
  33.9 52.9 %all-to-all-start.1 = ((f32[32,128,128]{2,1,0:T(8,128)}), f32[32,128,128]{2,1,0:T(8,128)}, u32[]{:S(2)}, u32[]{:S(2)}) async-start(f32[32,128,128]{2,1,0:T(8,128)} %get-tuple-element.155), calls=%async_computation.1 | async-start | bytes 4194304 | tf_op jit(solution)/shard_map/all_to_all | solution.py:459
  42.1 18.5 %copy-start.11 = (s32[32]{0:T(128)S(1)}, s32[32]{0:T(128)}, u32[]{:S(2)}) copy-start(s32[32]{0:T(128)} %param.10) | copy-start | bytes 388
  108.6 128.3 %all-to-all-start.2 = ((f32[32,128,128]{2,1,0:T(8,128)}), f32[32,128,128]{2,1,0:T(8,128)S(1)}, u32[]{:S(2)}, u32[]{:S(2)}) async-start(f32[32,128,128]{2,1,0:T(8,128)} %after.2), calls=%async_computation.2 | async-start | bytes 4194304 | tf_op jit(solution)/shard_map/all_to_all | solution.py:520
  114.4 4.8 %copy-start.1 = (f32[8,128,128]{2,1,0:T(8,128)S(1)}, f32[8,128,128]{2,1,0:T(8,128)}, u32[]{:S(2)}) copy-start(f32[8,128,128]{2,1,0:T(8,128)} %add_panel_children.1.earlier_ref.refs_0_) | copy-start | bytes 1572868
  119.2 63.7 %collective-permute-start.17 = (f32[8,128,128]{2,1,0:T(8,128)S(1)}, f32[8,128,128]{2,1,0:T(8,128)S(1)}, u32[]{:S(2)}, u32[]{:S(2)}) collective-permute-start(f32[8,128,128]{2,1,0:T(8,128)S(1)} %copy-done.1), channel_id=1, source_target_pairs={{0,16},{4,20},{8,24},{12,28},{16,0},{20,4},{24,8},{28,12},{1,17},{... | collective-permute-start | bytes 1572872 | tf_op jit(solution)/shard_map/ppermute | solution.py:23
  121.4 62.0 %collective-permute-start.16 = (f32[8,128,128]{2,1,0:T(8,128)S(1)}, f32[8,128,128]{2,1,0:T(8,128)}, u32[]{:S(2)}, u32[]{:S(2)}) collective-permute-start(f32[8,128,128]{2,1,0:T(8,128)S(1)} %copy-done.1), channel_id=1, source_target_pairs={{0,12},{1,8},{2,4},{3,0},{4,13},{5,9},{6,5},{7,1},{8,14},{9,10},{1... | collective-permute-start | bytes 1572872 | tf_op jit(solution)/shard_map/ppermute | solution.py:517
  126.1 58.8 %collective-permute-start.15 = (f32[8,128,128]{2,1,0:T(8,128)S(1)}, f32[8,128,128]{2,1,0:T(8,128)}, u32[]{:S(2)}, u32[]{:S(2)}) collective-permute-start(f32[8,128,128]{2,1,0:T(8,128)S(1)} %copy-done.1), channel_id=1, source_target_pairs={{0,8},{1,12},{2,0},{3,4},{4,9},{5,13},{6,1},{7,5},{8,10},{9,14},{1... | collective-permute-start | bytes 1572872 | tf_op jit(solution)/shard_map/ppermute | solution.py:517
  127.1 58.4 %collective-permute-start.14 = (f32[8,128,128]{2,1,0:T(8,128)S(1)}, f32[8,128,128]{2,1,0:T(8,128)}, u32[]{:S(2)}, u32[]{:S(2)}) collective-permute-start(f32[8,128,128]{2,1,0:T(8,128)S(1)} %copy-done.1), channel_id=1, source_target_pairs={{0,4},{1,0},{2,12},{3,8},{4,5},{5,1},{6,13},{7,9},{8,6},{9,2},{10,... | collective-permute-start | bytes 1572872 | tf_op jit(solution)/shard_map/ppermute | solution.py:517
  129.1 60.5 %collective-permute-start.13 = (f32[8,128,128]{2,1,0:T(8,128)S(1)}, f32[8,128,128]{2,1,0:T(8,128)}, u32[]{:S(2)}, u32[]{:S(2)}) collective-permute-start(f32[8,128,128]{2,1,0:T(8,128)S(1)} %copy-done.1), channel_id=1, source_target_pairs={{0,0},{1,4},{2,8},{3,12},{4,1},{5,5},{6,9},{7,13},{8,2},{9,6},{10,... | collective-permute-start | bytes 1572872 | tf_op jit(solution)/shard_map/ppermute | solution.py:517
  182.9 2.0 copy-start.4
  182.9 28.1 %collective-permute-start.11 = (f32[8,128,128]{2,1,0:T(8,128)S(1)}, f32[8,128,128]{2,1,0:T(8,128)}, u32[]{:S(2)}, u32[]{:S(2)}) collective-permute-start(f32[8,128,128]{2,1,0:T(8,128)S(1)} %copy-done.1), channel_id=1, source_target_pairs={{0,2},{1,3},{2,0},{3,1},{4,6},{5,7},{6,4},{7,5},{8,10},{9,11},{10,... | collective-permute-start | bytes 1572872 | tf_op jit(solution)/shard_map/ppermute | solution.py:23
  183.3 31.9 %collective-permute-start.10 = (f32[8,128,128]{2,1,0:T(8,128)S(1)}, f32[8,128,128]{2,1,0:T(8,128)}, u32[]{:S(2)}, u32[]{:S(2)}) collective-permute-start(f32[8,128,128]{2,1,0:T(8,128)S(1)} %copy-done.1), channel_id=1, source_target_pairs={{0,1},{1,0},{2,3},{3,2},{4,5},{5,4},{6,7},{7,6},{8,9},{9,8},{10,11... | collective-permute-start | bytes 1572872 | tf_op jit(solution)/shard_map/ppermute | solution.py:23
  184.9 44.4 %collective-permute-start.21 = (f32[8,128,128]{2,1,0:T(8,128)}, f32[8,128,128]{2,1,0:T(8,128)S(1)}, u32[]{:S(2)}, u32[]{:S(2)}) collective-permute-start(f32[8,128,128]{2,1,0:T(8,128)} %after.3), channel_id=1, source_target_pairs={{0,12},{1,8},{2,4},{3,0},{4,13},{5,9},{6,5},{7,1},{8,14},{9,10},{1... | collective-permute-start | bytes 1572872 | tf_op jit(solution)/shard_map/ppermute | solution.py:517
  185.5 43.8 %collective-permute-start.20 = (f32[8,128,128]{2,1,0:T(8,128)}, f32[8,128,128]{2,1,0:T(8,128)S(1)}, u32[]{:S(2)}, u32[]{:S(2)}) collective-permute-start(f32[8,128,128]{2,1,0:T(8,128)} %after.3), channel_id=1, source_target_pairs={{0,8},{1,12},{2,0},{3,4},{4,9},{5,13},{6,1},{7,5},{8,10},{9,14},{1... | collective-permute-start | bytes 1572872 | tf_op jit(solution)/shard_map/ppermute | solution.py:517
  189.6 39.7 %collective-permute-start.19 = (f32[8,128,128]{2,1,0:T(8,128)}, f32[8,128,128]{2,1,0:T(8,128)S(1)}, u32[]{:S(2)}, u32[]{:S(2)}) collective-permute-start(f32[8,128,128]{2,1,0:T(8,128)} %after.3), channel_id=1, source_target_pairs={{0,4},{1,0},{2,12},{3,8},{4,5},{5,1},{6,13},{7,9},{8,6},{9,2},{10,... | collective-permute-start | bytes 1572872 | tf_op jit(solution)/shard_map/ppermute | solution.py:517
  211.0 18.4 %collective-permute-start.18 = (f32[8,128,128]{2,1,0:T(8,128)}, f32[8,128,128]{2,1,0:T(8,128)S(1)}, u32[]{:S(2)}, u32[]{:S(2)}) collective-permute-start(f32[8,128,128]{2,1,0:T(8,128)} %after.3), channel_id=1, source_target_pairs={{0,0},{1,4},{2,8},{3,12},{4,1},{5,5},{6,9},{7,13},{8,2},{9,6},{10,... | collective-permute-start | bytes 1572872 | tf_op jit(solution)/shard_map/ppermute | solution.py:517
  215.3 7.4 %collective-permute-start.12 = (f32[8,128,128]{2,1,0:T(8,128)}, f32[8,128,128]{2,1,0:T(8,128)S(1)}, u32[]{:S(2)}, u32[]{:S(2)}) collective-permute-start(f32[8,128,128]{2,1,0:T(8,128)} %collective-permute-done.11.refs_2_), channel_id=1, source_target_pairs={{0,1},{1,0},{2,3},{3,2},{4,5},{5,4},{6,7},{7,6},{8,9},{9,8},{10,11... | collective-permute-start | bytes 1572872 | tf_op jit(solution)/shard_map/ppermute | solution.py:23
  222.7 0.8 copy-start.9
  229.3 0.8 copy-start.5
  229.3 0.9 copy-start.6
  229.3 1.1 copy-start.7
  230.5 0.8 copy-start.8
  237.0 1.3 copy-start
where the time goes:
time: 255 us; the launch traced here: 254 us
  waiting for transfers between devices  102 us (40%)
  Pallas kernels  74.4 us (29%)
  starting transfers between devices  49.1 us (19%)
  local copies, waits for them, and re-layouts  13.7 us (5%)
  other arithmetic  13.4 us (5%)
    ppermute x8, waiting for transfers between devices, xor_send(): return lax.ppermute(x, axis, [(i, i ^ 1 << bit) for i in range(size)])  75.9 us
    all_to_all x1, waiting for transfers between devices, local(): got1 = lax.all_to_all(send1, ALL, 0, 0, tiled=True)  25.4 us
    pallas_call x1, Pallas kernels, factor_panel1(): pl.pallas_call(panel1_kernel, out_shape=(full, part, part, full, part, pa...  19 us
    pallas_call x1, Pallas kernels, factor_panel0(): pl.pallas_call(panel0_kernel, out_shape=(full, part, part), in_specs=[WHO...  17.4 us
    ppermute x8, starting transfers between devices, to_columns(): return lax.ppermute(part, ALL, pairs)  17.3 us
    pallas_call x3, Pallas kernels, solve(): pl.pallas_call(functools.partial(solve_kernel, with_panel), out_shape=tup...  17.2 us
    pallas_call x1, Pallas kernels, finish(): pl.pallas_call(functools.partial(final_kernel, panel_blocks), out_shape=j...  15.7 us
    all_to_all x1, starting transfers between devices, local(): got_notes = lax.all_to_all(notes[:, None, :], ALL, 0, 0, tiled=True)[:, 0]  9.11 us
  transfers between devices with their start and end apart: 20, of which 6 were waited for; matrix products, arithmetic and copies ran while one was open for 8% of the time, Pallas kernels for 15%

commit v1 on v0

--- a/solution.py
+++ b/solution.py
@@ -68,7 +68,7 @@
     )(x, *others)
 
 
-def pack_kernel(owner_ref, rank_ref, child_ref, first_ref, second_ref, sem):
+def pack_kernel(owner_ref, rank_ref, child_ref, earlier_ref, first_ref, second_ref, sem):
     count = child_ref.shape[0]
 
     def to_first(k):
@@ -85,7 +85,7 @@
         pl.when(rank_ref[k] != 0)(lambda k=k: to_second(k).wait())
 
 
-def pack(owner_ids, rank, child_blocks, devices):
+def pack(owner_ids, rank, child_blocks, devices, earlier):
     count, tile, _ = child_blocks.shape
     shape = jax.ShapeDtypeStruct((devices, tile, tile), jnp.float32)
     return pl.pallas_call(
@@ -94,13 +94,13 @@
         grid_spec=pltpu.PrefetchScalarGridSpec(
             num_scalar_prefetch=2,
             grid=(),
-            in_specs=[WHOLE],
+            in_specs=[WHOLE, HBM],
             out_specs=(HBM, HBM),
             scratch_shapes=[pltpu.SemaphoreType.DMA((count,))],
         ),
         compiler_params=pltpu.CompilerParams(vmem_limit_bytes=VMEM_LIMIT),
         name="pack_children",
-    )(owner_ids, rank, child_blocks)
+    )(owner_ids, rank, child_blocks, earlier)
 
 
 def strip_kernel(row_ref, strip_ref, got_ref, earlier_ref, out_ref, buffer, sem):
@@ -228,11 +228,11 @@
     store_square(zl_ref, [part[1] for part in parts])
 
 
-def panel1_kernel(keep_ref, corner_ref, z0h_ref, z0l_ref, earlier_ref, a_ref, ah_ref, al_ref, l_ref, zh_ref, zl_ref, *scratch):
+def panel1_kernel(pattern_ref, corner_ref, z0h_ref, z0l_ref, earlier_ref, a_ref, ah_ref, al_ref, l_ref, zh_ref, zl_ref, *scratch):
     tile = corner_ref.shape[-1]
     z0 = (z0h_ref[...], z0l_ref[...])
     rows = [jnp.concatenate([leading_block(corner_ref, 2 + i, j) for j in range(2)], axis=1) for i in range(2)]
-    a = jnp.concatenate([nt_dot3(split(rows[i]), z0) * keep_ref[i].astype(jnp.float32) for i in range(2)], axis=0)
+    a = jnp.concatenate([nt_dot3(split(rows[i]), z0) * pattern_ref[0, 2 + i].astype(jnp.float32) for i in range(2)], axis=0)
     a_ref[...] = a
     ah_ref[...], al_ref[...] = split(a)
     update = exact_dot(a, a, ((1,), (1,)))
@@ -262,7 +262,7 @@
     )(corner)
 
 
-def factor_panel1(corner, keep, z0, earlier):
+def factor_panel1(corner, pattern, z0, earlier):
     tile = corner.shape[-1]
     full = jax.ShapeDtypeStruct((2 * tile, 2 * tile), jnp.float32)
     part = jax.ShapeDtypeStruct((2 * tile, 2 * tile), jnp.bfloat16)
@@ -278,10 +278,10 @@
         ),
         compiler_params=pltpu.CompilerParams(vmem_limit_bytes=VMEM_LIMIT),
         name="factor_panel1",
-    )(keep, corner, *z0, earlier)
-
-
-def solve_kernel(with_panel, keep0_ref, keep1_ref, place_ref, *refs):
+    )(pattern, corner, *z0, earlier)
+
+
+def solve_kernel(with_panel, pattern_ref, place_ref, *refs):
     x_refs, factor_refs, rest = refs[:4], refs[4:10], refs[10:]
     high_ref, low_ref, xs = rest[0], rest[1], rest[-1]
     n = pl.program_id(0)
@@ -290,16 +290,21 @@
         xs[place_ref[0] ^ m] = x_refs[m][...].reshape(depth * tile, tile)
     z0, a, z1 = [(factor_refs[2 * i][...], factor_refs[2 * i + 1][...]) for i in range(3)]
 
-    def masked(q, keep_ref):
-        return jnp.concatenate(
-            [q[i * tile : (i + 1) * tile] * keep_ref[n * depth + i].astype(jnp.float32) for i in range(depth)], axis=0
-        )
+    def masked(q, panel):
+        parts = []
+        for i in range(depth):
+            block_row = (n * depth + i) * place_ref[2] + place_ref[1]
+            keep = pattern_ref[0, block_row]
+            if panel == 1:
+                keep = jnp.maximum(keep, pattern_ref[1, block_row])
+            parts.append(q[i * tile : (i + 1) * tile] * keep.astype(jnp.float32))
+        return jnp.concatenate(parts, axis=0)
 
     x0 = jnp.concatenate([xs[0], xs[1]], axis=1)
     x1 = jnp.concatenate([xs[2], xs[3]], axis=1)
-    q0 = masked(nt_dot3(split(x0), z0), keep0_ref)
+    q0 = masked(nt_dot3(split(x0), z0), 0)
     q0_parts = split(q0)
-    q1 = masked(nt_dot3(split(x1 - nt_dot3(q0_parts, a)), z1), keep1_ref)
+    q1 = masked(nt_dot3(split(x1 - nt_dot3(q0_parts, a)), z1), 1)
     q1_parts = split(q1)
     width = 2 * tile
     for ref, index in ((high_ref, 0), (low_ref, 1)):
@@ -313,7 +318,7 @@
         rest[2][...] = xs[place_ref[0]].reshape(depth, tile, tile)
 
 
-def solve(strips, keep0, keep1, place, factors, with_panel):
+def solve(strips, pattern, place, factors, with_panel):
     rows, tile, _ = strips[0].shape
     depth = rows // 2
     part = jax.ShapeDtypeStruct((rows * tile, 4 * tile), jnp.bfloat16)
@@ -327,7 +332,7 @@
         functools.partial(solve_kernel, with_panel),
         out_shape=tuple(out_shape),
         grid_spec=pltpu.PrefetchScalarGridSpec(
-            num_scalar_prefetch=3,
+            num_scalar_prefetch=2,
             grid=(rows // depth,),
             in_specs=[strip_spec] * 4 + [WHOLE] * 6,
             out_specs=tuple(out_specs),
@@ -335,7 +340,7 @@
         ),
         compiler_params=pltpu.CompilerParams(vmem_limit_bytes=VMEM_LIMIT),
         name="solve_rows" if with_panel else "solve_columns",
-    )(keep0, keep1, place, *strips, *factors)
+    )(pattern, place, *strips, *factors)
 
 
 def final_kernel(panel_blocks, first_ref, second_ref, place_ref, front_ref, got1_ref, got2_ref, high_ref, low_ref,
@@ -440,96 +445,112 @@
     owner_ids = owners[:, 0]
     children = owner_ids.shape[0]
 
+    corner = front[0, 0, 0, 0]
+    every = jnp.stack([owner_ids, slots])
+    for bit in reversed(range(panel_bits, row_bits)):
+        every = gather_bit(every, "prow", bit)
+    corner = spread_high(corner, "prow", panel_bits)
+    first_corner = corner
+
     index = jnp.arange(children, dtype=jnp.int32)
-    is_panel = (slots % bcols == 0) & (owner_ids % grid_cols < panel_blocks)
-    same = owner_ids[:, None] == owner_ids[None, :]
-    ahead = jnp.where(is_panel[:, None] == is_panel[None, :], index[None, :] < index[:, None], is_panel[None, :])
-    rank = jnp.sum((same & ahead).astype(jnp.int32), axis=1)
-    late = is_panel & (rank == 1)
-
-    to = owner_ids[None, :] == jnp.arange(devices, dtype=jnp.int32)[:, None]
-    lane = jnp.arange(tile, dtype=jnp.int32)[None, :]
-    slot1 = jnp.sum(jnp.where(to & (rank == 0)[None, :], slots[None, :], 0), axis=1, keepdims=True)
-    slot2 = jnp.sum(jnp.where(to & (rank == 1)[None, :], slots[None, :], 0), axis=1, keepdims=True)
-    late_count = jnp.sum(late.astype(jnp.int32))
-    notes = jnp.where(lane == 0, slot1, jnp.where(lane == 1, slot2, late_count))
-    got_notes = lax.all_to_all(notes[:, None, :], ALL, 0, 0, tiled=True)[:, 0]
-
-    send1, send2 = pack(owner_ids, rank, child_blocks, devices)
+
+    def ranked(owner, slot):
+        panel = (slot % bcols == 0) & (owner % grid_cols < panel_blocks)
+        same = owner[..., :, None] == owner[..., None, :]
+        ahead = jnp.where(
+            panel[..., :, None] == panel[..., None, :], index[None, :] < index[:, None], panel[..., None, :]
+        )
+        return jnp.sum((same & ahead).astype(jnp.int32), axis=-1), panel
+
+    rank, panel = ranked(owner_ids, slots)
+    late = panel & (rank == 1)
+    send1, send2 = pack(owner_ids, rank, child_blocks, devices, first_corner)
     got1 = lax.all_to_all(send1, ALL, 0, 0, tiled=True)
 
-    corner = front[0, 0, 0, 0]
-    corner = spread_high(corner, "prow", panel_bits)
-    corner = spread_high(corner, "pcol", panel_bits)
     for bit in reversed(range(panel_bits)):
         corner = gather_bit(corner, "prow", bit)
+        every = gather_bit(every, "prow", bit)
+    corner = spread_high(corner, "pcol", panel_bits)
+    for bit in reversed(range(panel_bits, col_bits)):
+        every = gather_bit(every, "pcol", bit)
     for bit in reversed(range(panel_bits)):
         corner = gather_bit(corner, "pcol", bit)
+        every = gather_bit(every, "pcol", bit)
     l0, *z0 = factor_panel0(corner)
 
-    first_slots, second_slots = got_notes[:, 0], got_notes[:, 1]
-
-    def panel_here(slot):
-        return (slot % bcols == 0) & (slot > 0) & (rank_c < panel_blocks)
-
-    panel_row = jnp.where(panel_here(first_slots), first_slots // bcols, -1)
+    bits = row_bits + col_bits
+    every = jnp.transpose(every, tuple(reversed(range(bits))) + (bits, bits + 1)).reshape(devices, 2, children)
+    every_owner, every_slot = every[:, 0], every[:, 1]
+    every_rank, every_panel = ranked(every_owner, every_slot)
+    mine = every_owner == me
+    trailing = jnp.where(mine & ~every_panel, every_slot, 0)
+    first_slots = jnp.sum(jnp.where(every_rank == 0, trailing, 0), axis=1)
+    second_slots = jnp.sum(jnp.where(every_rank == 1, trailing, 0), axis=1)
+    panel_row = jnp.sum(jnp.where(mine & every_panel & (every_rank == 0), every_slot // bcols + 1, 0), axis=1) - 1
     depth = brows // 4
-    lists = [by_slot(jnp.where(panel_here(s), 0, s), depth * bcols, brows // depth) for s in (first_slots, second_slots)]
+    lists = [by_slot(slot, depth * bcols, brows // depth) for slot in (first_slots, second_slots)]
 
     strip = front[:, 0, 0, 0]
-    rounds = jnp.max(got_notes[:, 2])
-    order = jnp.cumsum(late.astype(jnp.int32))
+    every_late = every_panel & (every_rank == 1)
+    turns = jnp.cumsum(every_late.astype(jnp.int32), axis=1)
+    rounds = jnp.max(turns)
+    own_turns = jnp.cumsum(late.astype(jnp.int32))
 
     def deliver(turn, strip):
-        chosen = late & (order == turn + 1)
-        block = child_blocks[jnp.argmax(chosen)]
-        note = jnp.where(lane == 0, jnp.sum(jnp.where(chosen, owner_ids + 1, 0)), jnp.sum(jnp.where(chosen, slots, 0)))
-        block = jnp.concatenate([block, jnp.broadcast_to(note, (8, tile)).astype(jnp.float32)], axis=0)
-        for axis, bits in (("prow", row_bits), ("pcol", col_bits)):
-            for bit in reversed(range(bits)):
+        block = child_blocks[jnp.argmax(late & (own_turns == turn + 1))]
+        for axis, count in (("prow", row_bits), ("pcol", col_bits)):
+            for bit in reversed(range(count)):
                 block = gather_bit(block, axis, bit)
-        blocks = block.reshape(devices, tile + 8, tile)
-        note = blocks[:, tile, :2].astype(jnp.int32)
-        here = note[:, 0] == me + 1
-        rows = jnp.where(here, note[:, 1] // bcols, 0)
-        return strip.at[rows].add(jnp.where(here[:, None, None], blocks[:, :tile], 0.0))
+        blocks = jnp.transpose(block, tuple(reversed(range(bits))) + (bits, bits + 1)).reshape(devices, tile, tile)
+        chosen = every_late & (turns == turn + 1) & mine
+        rows = jnp.sum(jnp.where(chosen, every_slot // bcols, 0), axis=1)
+        return strip.at[rows].add(jnp.where(jnp.any(chosen, axis=1)[:, None, None], blocks, 0.0))
 
     strip = lax.fori_loop(0, rounds, deliver, strip)
     strip = add_to_strip(panel_row, strip, got1, l0)
     strip = spread_high(strip, "pcol", panel_bits)
 
+    parts = {0: strip}
+    for bit in reversed(range(1, row_bits)):
+        parts |= {key | (1 << bit): xor_send(part, "prow", bit) for key, part in parts.items()}
     across = xor_send(strip, "pcol", 1)
     row_strips = [strip, xor_send(strip, "pcol", 0), across, xor_send(across, "pcol", 0)]
-    a, ah, al, l1, *z1 = factor_panel1(corner, pattern[0, 2:4], z0, strip)
+    a, ah, al, l1, *z1 = factor_panel1(corner, pattern, z0, row_strips[1])
     factors = (*z0, ah, al, *z1)
-    parts = [strip]
-    for bit in range(col_bits, row_bits):
-        parts = parts + [after(xor_send(part, "prow", bit), l1) for part in parts]
-    highs = len(parts)
-
-    def to_columns(part, m):
+    got2 = lax.all_to_all(after(send2, parts[1 << (row_bits - 1)]), ALL, 0, 0, tiled=True)
+
+    def to_column(part, flip, turn):
         pairs = [
-            ((h * grid_cols + low) * grid_cols + c, (h * grid_cols + (c ^ m)) * grid_cols + low)
-            for h in range(highs)
-            for low in range(grid_cols)
+            (r * grid_cols + c, ((r & ~1) | ((c & 1) ^ turn)) * grid_cols + (((c & ~1) ^ (flip << 1)) | (r & 1)))
+            for r in range(grid_rows)
             for c in range(grid_cols)
         ]
         return lax.ppermute(part, ALL, pairs)
 
-    col_strips = [[to_columns(part, m) for m in range(panel_blocks)] for part in parts]
-    got2 = lax.all_to_all(after(send2, l1), ALL, 0, 0, tiled=True)
-
-    keep0, keep1 = pattern[0], jnp.maximum(pattern[0], pattern[1])
+    def wanted(high, flip):
+        chosen = {key: part for key, part in parts.items() if key >> col_bits == high}
+        for bit in range(1, col_bits):
+            differs = my_bit("prow", bit) ^ my_bit("pcol", bit) ^ (flip if bit == 1 else 0)
+            chosen = {
+                key: jnp.where(differs == 1, chosen[key | (1 << bit)], part)
+                for key, part in chosen.items()
+                if not key >> bit & 1
+            }
+        (part,) = chosen.values()
+        return part
+
     my_high = rank_r // grid_cols
-    rows_of = jnp.arange(brows, dtype=jnp.int32) * grid_rows
-    blocks = rows_of + rank_r
-    row_high, row_low, panel = solve(
-        row_strips, keep0[blocks], keep1[blocks], (rank_c % panel_blocks)[None], factors, True
-    )
+    col_strips = []
+    for high in range(grid_rows // grid_cols):
+        sends = [wanted(high, flip) for flip in range(2)]
+        col_strips.append([to_column(sends[flip], flip, turn) for flip in range(2) for turn in range(2)])
+    row_place = jnp.stack([rank_c % panel_blocks, rank_r, jnp.int32(grid_rows)])
+    row_high, row_low, panel = solve(row_strips, pattern, row_place, factors, True)
     cols = []
     for high, strips in enumerate(col_strips):
-        blocks = rows_of + (my_high ^ high) * grid_cols + rank_c
-        cols += solve(strips, keep0[blocks], keep1[blocks], (rank_r % panel_blocks)[None], factors, False)
+        base = my_bit("pcol", 1) * 2 + my_bit("prow", 0)
+        col_place = jnp.stack([base, (my_high ^ high) * grid_cols + rank_c, jnp.int32(grid_rows)])
+        cols += solve(strips, pattern, col_place, factors, False)
     place = jnp.stack([rank_r, rank_c, jnp.int32(grid_rows), my_high])
     return finish(
         depth, *lists, place, front, got1, got2, row_high, row_low, panel, (l0, a, l1), cols, panel_blocks

time: 255 us -> 266 us (1.043)
  waiting for transfers between devices: 102 us -> 120 us
  local copies, waits for them, and re-layouts: 13.7 us -> 5.9 us
    ppermute x8 -> x15, starting transfers between devices: 7.03 us -> 23 us  [xor_send(): return lax.ppermute(x, axis, [(i, i ^ 1 << bit) for i in range(size)])]
    ppermute x8, waiting for transfers between devices: 0.02 us -> 10.9 us  [to_column(): return lax.ppermute(part, ALL, pairs)]
    all_to_all x2 -> x1, starting transfers between devices: 14.9 us -> 5.77 us  [local(): lax.all_to_all(after(send2, parts[1 << row_bits - 1]), ALL, 0, 0, tiled=T...]
    gather x6 -> x0, local copies, waits for them, and re-layouts: 7.08 us -> none  [the longest x3 3.56 us: local(): keep1[blocks]]
    ppermute x8 -> x15, waiting for transfers between devices: 75.9 us -> 81.8 us  [xor_send(): return lax.ppermute(x, axis, [(i, i ^ 1 << bit) for i in range(size)])]
    ppermute x8, starting transfers between devices: 17.3 us -> 12.3 us  [to_column(): return lax.ppermute(part, ALL, pairs)]
    another operation x3 -> x8, other arithmetic: 0.18 us -> 2.9 us  [the longest x2 1.27 us: local(): jnp.stack([base, (my_high ^ high) * grid_cols + rank_c, jnp.int32(grid_ro...]
  transfers between devices with their start and end apart: 20 -> 26, of which waited for: 6 -> 12; matrix products, arithmetic and copies ran while one was open for 8% -> 5% of each run, Pallas kernels for 15% -> 22%
where the time goes in v1:
time: 266 us; the launch traced here: 264 us
  waiting for transfers between devices  120 us (45%)
  Pallas kernels  76.6 us (29%)
  starting transfers between devices  47.6 us (18%)
  other arithmetic  12.3 us (5%)
  local copies, waits for them, and re-layouts  5.9 us (2%)
    ppermute x15, waiting for transfers between devices, xor_send(): return lax.ppermute(x, axis, [(i, i ^ 1 << bit) for i in range(size)])  81.8 us
    all_to_all x1, waiting for transfers between devices, local(): got1 = lax.all_to_all(send1, ALL, 0, 0, tiled=True)  27.8 us
    ppermute x15, starting transfers between devices, xor_send(): return lax.ppermute(x, axis, [(i, i ^ 1 << bit) for i in range(size)])  23 us
    pallas_call x1, Pallas kernels, factor_panel1(): pl.pallas_call(panel1_kernel, out_shape=(full, part, part, full, part, pa...  19.1 us
    pallas_call x3, Pallas kernels, solve(): pl.pallas_call(functools.partial(solve_kernel, with_panel), out_shape=tup...  17.4 us
    pallas_call x1, Pallas kernels, factor_panel0(): pl.pallas_call(panel0_kernel, out_shape=(full, part, part), in_specs=[WHO...  17.4 us
    pallas_call x1, Pallas kernels, finish(): pl.pallas_call(functools.partial(final_kernel, panel_blocks), out_shape=j...  16.2 us
    ppermute x8, starting transfers between devices, to_column(): return lax.ppermute(part, ALL, pairs)  12.3 us
  transfers between devices with their start and end apart: 26, of which 12 were waited for; matrix products, arithmetic and copies ran while one was open for 5% of the time, Pallas kernels for 22%

profile of v1, /device:TPU:9, one launch (start us, length us, event | category | flops | bytes accessed | tf_op | source)
XLA Modules:
  0.0 264.2 jit_solution(12158257302584906264)
XLA Ops:
  0.7 2.3 collective-permute-start.5
  3.0 0.8 slice_bitcast_fusion.1
  3.8 2.0 collective-permute-start.10
  6.7 1.1 slice_bitcast_fusion
  7.8 1.2 collective-permute-done.6
  9.0 1.3 collective-permute-start.7
  11.6 1.3 collective-permute-start.8
  12.8 0.9 convert_reduce_fusion.1.rank_ref
  14.2 4.7 %collective-permute-start.9 = (s32[2,2,2,2,2,32]{5,4,3,2,1,0:T(2,128)S(1)}, s32[2,2,2,2,2,32]{5,4,3,2,1,0:T(2,128)S(1)}, u32[]{:S(2)}, u32[]{:S(2)}) collective-permute-start(s32[2,2,2,2,2,32]{5,4,3,2,1,0:T(2,128)S(1)} %pad_add_fusion), channel_id=1, source_target_pairs={{0,1},{1,0},{2,3},{3,2},{4,5},{5,4},{6,7},{7,6},{8,9},{9,8},{10,11... | collective-permute-start | bytes 12296 | tf_op jit(solution)/shard_map/ppermute | solution.py:23
  19.8 0.9 broadcast_select_fusion.4.earlier_ref
  20.8 3.1 %collective-permute-done.11 = f32[128,128]{1,0:T(8,128)S(1)} collective-permute-done((f32[128,128]{1,0:T(8,128)S(1)}, f32[128,128]{1,0:T(8,128)S(1)}, u32[]{:S(2)}, u32[]{:S(2)}) %collective-permute-start.11) | collective-permute-done | bytes 65568 | tf_op jit(solution)/shard_map/ppermute | solution.py:23
  23.9 1.3 collective-permute-start.12
  25.2 2.6 collective-permute-done.12
  27.8 1.3 collective-permute-start.13
  29.1 0.9 convert_reduce_fusion
  30.1 3.1 %collective-permute-done.13 = f32[2,2,128,128]{3,2,1,0:T(8,128)S(1)} collective-permute-done((f32[2,2,128,128]{3,2,1,0:T(8,128)S(1)}, f32[2,2,128,128]{3,2,1,0:T(8,128)S(1)}, u32[]{:S(2)}, u32[]{:S(2)}) %collective-permute-start.13) | collective-permute-done | bytes 262176 | tf_op jit(solution)/shard_map/ppermute | solution.py:23
  33.2 3.9 %collective-permute-start.14 = (f32[2,2,2,128,128]{4,3,2,1,0:T(8,128)S(1)}, f32[2,2,2,128,128]{4,3,2,1,0:T(8,128)S(1)}, u32[]{:S(2)}, u32[]{:S(2)}) collective-permute-start(f32[2,2,2,128,128]{4,3,2,1,0:T(8,128)S(1)} %pad_maximum_fusion.6), channel_id=1, source_target_pairs={{0,1},{1,0},{2,3},{3,2},{4,5},{5,4},{6,7},{7,6},{8,9},{9,8},{10,11... | collective-permute-start | bytes 1572872 | tf_op jit(solution)/shard_map/ppermute | solution.py:23
  38.6 3.8 %pack_children.1 = (f32[32,128,128]{2,1,0:T(8,128)}, f32[32,128,128]{2,1,0:T(8,128)}) custom-call(s32[32]{0:T(128)} %bitcast.156, s32[32]{0:T(128)} %copy-done.14, f32[32,128,128]{2,1,0:T(8,128)} %child_ref.1, f32[128,128]{1,0:T(8,128)} %copy-done.5), custom_call_target="tpu_custom_call" | custom-call | tf_op jit(solution)/shard_map/pack_children/pallas_call | solution.py:91
  42.5 4.7 %all-to-all-start = ((f32[32,128,128]{2,1,0:T(8,128)}), f32[32,128,128]{2,1,0:T(8,128)}, u32[]{:S(2)}, u32[]{:S(2)}) async-start(f32[32,128,128]{2,1,0:T(8,128)} %get-tuple-element.197), calls=%async_computation | async-start | bytes 4194304 | tf_op jit(solution)/shard_map/all_to_all | solution.py:468
  47.2 1.1 pad_maximum_fusion.5.corner_ref
  48.3 17.4 %factor_panel0.1 = (f32[256,256]{1,0:T(8,128)}, bf16[256,256]{1,0:T(8,128)(2,1)}, bf16[256,256]{1,0:T(8,128)(2,1)}) custom-call(f32[2,2,2,2,128,128]{5,4,3,2,1,0:T(8,128)} %pad_maximum_fusion.5.corner_ref), custom_call_target="tpu_custom_call" | custom-call | tf_op jit(solution)/shard_map/factor_panel0/pallas_call | solution.py:254
  65.7 0.8 while.13
  66.6 27.8 %all-to-all-done.got_ref.got1_ref = f32[32,128,128]{2,1,0:T(8,128)} async-done(((f32[32,128,128]{2,1,0:T(8,128)}), f32[32,128,128]{2,1,0:T(8,128)}, u32[]{:S(2)}, u32[]{:S(2)}) %all-to-all-start) | async-done | bytes 2097184 | tf_op jit(solution)/shard_map/all_to_all | solution.py:468
  94.3 2.6 add_panel_children.1.refs_0_
  97.0 2.0 collective-permute-start.15
  99.0 23.2 %collective-permute-done.15.refs_0_ = f32[8,128,128]{2,1,0:T(8,128)S(1)} collective-permute-done((f32[8,128,128]{2,1,0:T(8,128)}, f32[8,128,128]{2,1,0:T(8,128)S(1)}, u32[]{:S(2)}, u32[]{:S(2)}) %collective-permute-start.15) | collective-permute-done | bytes 524320 | tf_op jit(solution)/shard_map/ppermute | solution.py:23
  122.1 0.8 copy-done.2
  122.9 5.8 %all-to-all-start.1 = ((f32[32,128,128]{2,1,0:T(8,128)}), f32[32,128,128]{2,1,0:T(8,128)S(1)}, u32[]{:S(2)}, u32[]{:S(2)}) async-start(f32[32,128,128]{2,1,0:T(8,128)} %after.1), calls=%async_computation.1 | async-start | bytes 4194304 | tf_op jit(solution)/shard_map/all_to_all | solution.py:520
  131.4 1.4 collective-permute-start.17
  132.8 1.2 collective-permute-start.24
  134.1 1.3 collective-permute-start.16
  135.4 40.0 %collective-permute-done.19 = f32[8,128,128]{2,1,0:T(8,128)S(1)} collective-permute-done((f32[8,128,128]{2,1,0:T(8,128)S(1)}, f32[8,128,128]{2,1,0:T(8,128)S(1)}, u32[]{:S(2)}, u32[]{:S(2)}) %collective-permute-start.19) | collective-permute-done | bytes 524320 | tf_op jit(solution)/shard_map/ppermute | solution.py:23
  175.5 2.0 collective-permute-start.23
  177.5 1.1 collective-permute-start.22
  178.6 0.8 collective-permute-start.21
  179.4 7.2 %collective-permute-done.24 = f32[8,128,128]{2,1,0:T(8,128)S(1)} collective-permute-done((f32[8,128,128]{2,1,0:T(8,128)S(1)}, f32[8,128,128]{2,1,0:T(8,128)S(1)}, u32[]{:S(2)}, u32[]{:S(2)}) %collective-permute-start.24) | collective-permute-done | bytes 524320 | tf_op jit(solution)/shard_map/ppermute | solution.py:23
  187.6 2.7 %collective-permute-start.20 = (f32[8,128,128]{2,1,0:T(8,128)S(1)}, f32[8,128,128]{2,1,0:T(8,128)S(1)}, u32[]{:S(2)}, u32[]{:S(2)}) collective-permute-start(f32[8,128,128]{2,1,0:T(8,128)S(1)} %get-tuple-element.270), channel_id=1, source_target_pairs={{0,0},{1,4},{2,2},{3,6},{4,1},{5,5},{6,3},{7,7},{8,8},{9,12},{10,1... | collective-permute-start | bytes 1572872 | tf_op jit(solution)/shard_map/ppermute | solution.py:528
  190.4 1.0 collective-permute-start.28
  191.4 10.9 %collective-permute-done.22.refs_2_ = f32[8,128,128]{2,1,0:T(8,128)S(1)} collective-permute-done((f32[8,128,128]{2,1,0:T(8,128)S(1)}, f32[8,128,128]{2,1,0:T(8,128)S(1)}, u32[]{:S(2)}, u32[]{:S(2)}) %collective-permute-start.22) | collective-permute-done | bytes 524320 | tf_op jit(solution)/shard_map/ppermute | solution.py:528
  202.3 2.7 %collective-permute-start.26 = (f32[8,128,128]{2,1,0:T(8,128)S(1)}, f32[8,128,128]{2,1,0:T(8,128)}, u32[]{:S(2)}, u32[]{:S(2)}) collective-permute-start(f32[8,128,128]{2,1,0:T(8,128)S(1)} %get-tuple-element.268), channel_id=1, source_target_pairs={{0,4},{1,0},{2,6},{3,2},{4,5},{5,1},{6,7},{7,3},{8,12},{9,8},{10,1... | collective-permute-start | bytes 1572872 | tf_op jit(solution)/shard_map/ppermute | solution.py:528
  205.0 1.9 collective-permute-start.25
  208.4 19.1 %factor_panel1.1 = (f32[256,256]{1,0:T(8,128)}, bf16[256,256]{1,0:T(8,128)(2,1)}, bf16[256,256]{1,0:T(8,128)(2,1)}, f32[256,256]{1,0:T(8,128)}, bf16[256,256]{1,0:T(8,128)(2,1)}, /*index=5*/bf16[256,256]{1,0:T(8,128)(2,1)}) custom-call(s32[2,64]{1,0:T(2,128)} %pattern_ref.7, f32[2,2,2,2,128,128]{5,4,3,2,1,0:T(8,128)} %pad_maximum_fusion.5.corner_ref, ...), custom_call_target="tpu_custom_call" | custom-call | tf_op jit(solution)/shard_map/factor_panel1/pallas_call | solution.py:269
  227.5 6.0 %solve_rows.1 = (bf16[1024,512]{1,0:T(8,128)(2,1)}, bf16[1024,512]{1,0:T(8,128)(2,1)}, f32[8,128,128]{2,1,0:T(8,128)}) custom-call(s32[2,64]{1,0:T(2,128)} %pattern_ref.7, s32[3]{0:T(128)} %pad_add_fusion.9.place_ref, f32[8,128,128]{2,1,0:T(8,128)} %add_panel_children.1.refs_0_, f32[8,128,128]{2,1,0:T(8,128)} %copy-done.4, f32[8,128,128]{2,1,0:T(8,128)} %copy-done.6, ...), custom_call_target="tpu_custom_call" | custom-call | tf_op jit(solution)/shard_map/solve_rows/pallas_call | solution.py:331
  233.6 0.8 copy-done.13
  234.3 5.7 %solve_columns.2 = (bf16[1024,512]{1,0:T(8,128)(2,1)}, bf16[1024,512]{1,0:T(8,128)(2,1)}) custom-call(s32[2,64]{1,0:T(2,128)} %pattern_ref.7, s32[3]{0:T(128)} %pad_add_fusion.8.place_ref, f32[8,128,128]{2,1,0:T(8,128)} %copy-done.13, f32[8,128,128]{2,1,0:T(8,128)} %copy-done.9, f32[8,128,128]{2,1,0:T(8,128)} %copy-done.8, f32[8,128,128]{2,1,0:T(8,128)} %copy-done.7, ...), custom_call_target="tpu_custom_call" | custom-call | tf_op jit(solution)/shard_map/solve_columns/pallas_call | solution.py:331
  241.0 5.7 %solve_columns.3 = (bf16[1024,512]{1,0:T(8,128)(2,1)}, bf16[1024,512]{1,0:T(8,128)(2,1)}) custom-call(s32[2,64]{1,0:T(2,128)} %pattern_ref.7, s32[3]{0:T(128)} %pad_add_fusion.7.place_ref, f32[8,128,128]{2,1,0:T(8,128)} %collective-permute-done.25.refs_0_, f32[8,128,128]{2,1,0:T(8,128)} %collective-permute-done.26.refs_1_, f32[8,128,128]{2,1,0:T(8,128)} %copy-done.11, ...), custom_call_target="tpu_custom_call" | custom-call | tf_op jit(solution)/shard_map/solve_columns/pallas_call | solution.py:331
  246.7 1.3 copy-done
  248.0 16.2 %schur_update.1 = f32[8,1,16,1,128,128]{5,4,3,2,1,0:T(8,128)} custom-call(s32[3,32]{1,0:T(4,128)} %pad_add_fusion.4.first_ref, s32[3,32]{1,0:T(4,128)} %pad_add_fusion.5.second_ref, s32[4]{0:T(128)} %pad_add_fusion.10.place_ref, f32[8,1,16,1,128,128]{5,4,3,2,1,0:T(8,128)} %front_ref.1, f32[32,128,128]{2,1,0:T(8,128)} %all-to-all-done.got_ref.got1_ref, ...), custom_call_target="tpu_custom_call" | custom-call | tf_op jit(solution)/shard_map/schur_update/pallas_call | solution.py:406
  (98 shorter events, 12.2 us)
Async XLA Ops:
  0.7 5.1 %collective-permute-start.5 = (s32[2,32]{1,0:T(2,128)S(1)}, s32[2,32]{1,0:T(2,128)S(1)}, u32[]{:S(2)}, u32[]{:S(2)}) collective-permute-start(s32[2,32]{1,0:T(2,128)S(1)} %pad_add_fusion.6), channel_id=1, source_target_pairs={{0,16},{4,20},{8,24},{12,28},{16,0},{20,4},{24,8},{28,12},{1,17},{... | collective-permute-start | bytes 776 | tf_op jit(solution)/shard_map/ppermute | solution.py:23
  3.8 16.0 %collective-permute-start.10 = (f32[128,128]{1,0:T(8,128)S(1)}, f32[128,128]{1,0:T(8,128)S(1)}, u32[]{:S(2)}, u32[]{:S(2)}) collective-permute-start(f32[128,128]{1,0:T(8,128)S(1)} %slice_bitcast_fusion.1), channel_id=1, source_target_pairs={{0,16},{4,20},{8,24},{12,28},{1,17},{5,21},{9,25},{13,29},{2,18},{... | collective-permute-start | bytes 196616 | tf_op jit(solution)/shard_map/ppermute | solution.py:38
  6.5 2.5 collective-permute-start.6
  9.0 2.5 collective-permute-start.7
  11.6 2.6 collective-permute-start.8
  13.7 19.5 %copy-start.14 = (s32[32]{0:T(128)}, s32[32]{0:T(128)S(1)}, u32[]{:S(2)}) copy-start(s32[32]{0:T(128)S(1)} %convert_reduce_fusion.1.rank_ref) | copy-start | bytes 388
  14.2 5.6 %collective-permute-start.9 = (s32[2,2,2,2,2,32]{5,4,3,2,1,0:T(2,128)S(1)}, s32[2,2,2,2,2,32]{5,4,3,2,1,0:T(2,128)S(1)}, u32[]{:S(2)}, u32[]{:S(2)}) collective-permute-start(s32[2,2,2,2,2,32]{5,4,3,2,1,0:T(2,128)S(1)} %pad_add_fusion), channel_id=1, source_target_pairs={{0,1},{1,0},{2,3},{3,2},{4,5},{5,4},{6,7},{7,6},{8,9},{9,8},{10,11... | collective-permute-start | bytes 12296 | tf_op jit(solution)/shard_map/ppermute | solution.py:23
  20.7 17.9 %copy-start.5 = (f32[128,128]{1,0:T(8,128)}, f32[128,128]{1,0:T(8,128)S(1)}, u32[]{:S(2)}) copy-start(f32[128,128]{1,0:T(8,128)S(1)} %broadcast_select_fusion.4.earlier_ref) | copy-start | bytes 196612
  20.7 3.2 %collective-permute-start.11 = (f32[128,128]{1,0:T(8,128)S(1)}, f32[128,128]{1,0:T(8,128)S(1)}, u32[]{:S(2)}, u32[]{:S(2)}) collective-permute-start(f32[128,128]{1,0:T(8,128)S(1)} %broadcast_select_fusion.4.earlier_ref), channel_id=1, source_target_pairs={{0,8},{4,12},{8,0},{12,4},{16,24},{20,28},{24,16},{28,20},{1,9},{5... | collective-permute-start | bytes 196616 | tf_op jit(solution)/shard_map/ppermute | solution.py:23
  23.9 3.9 %collective-permute-start.12 = (f32[2,128,128]{2,1,0:T(8,128)S(1)}, f32[2,128,128]{2,1,0:T(8,128)S(1)}, u32[]{:S(2)}, u32[]{:S(2)}) collective-permute-start(f32[2,128,128]{2,1,0:T(8,128)S(1)} %pad_maximum_fusion.8), channel_id=1, source_target_pairs={{0,4},{4,0},{8,12},{12,8},{16,20},{20,16},{24,28},{28,24},{1,5},{5... | collective-permute-start | bytes 393224 | tf_op jit(solution)/shard_map/ppermute | solution.py:23
  27.8 5.3 %collective-permute-start.13 = (f32[2,2,128,128]{3,2,1,0:T(8,128)S(1)}, f32[2,2,128,128]{3,2,1,0:T(8,128)S(1)}, u32[]{:S(2)}, u32[]{:S(2)}) collective-permute-start(f32[2,2,128,128]{3,2,1,0:T(8,128)S(1)} %pad_maximum_fusion.7), channel_id=1, source_target_pairs={{0,2},{1,3},{2,0},{3,1},{4,6},{5,7},{6,4},{7,5},{8,10},{9,11},{10,... | collective-permute-start | bytes 786440 | tf_op jit(solution)/shard_map/ppermute | solution.py:23
  33.2 13.9 %collective-permute-start.14 = (f32[2,2,2,128,128]{4,3,2,1,0:T(8,128)S(1)}, f32[2,2,2,128,128]{4,3,2,1,0:T(8,128)S(1)}, u32[]{:S(2)}, u32[]{:S(2)}) collective-permute-start(f32[2,2,2,128,128]{4,3,2,1,0:T(8,128)S(1)} %pad_maximum_fusion.6), channel_id=1, source_target_pairs={{0,1},{1,0},{2,3},{3,2},{4,5},{5,4},{6,7},{7,6},{8,9},{9,8},{10,11... | collective-permute-start | bytes 1572872 | tf_op jit(solution)/shard_map/ppermute | solution.py:23
  42.5 51.9 %all-to-all-start = ((f32[32,128,128]{2,1,0:T(8,128)}), f32[32,128,128]{2,1,0:T(8,128)}, u32[]{:S(2)}, u32[]{:S(2)}) async-start(f32[32,128,128]{2,1,0:T(8,128)} %get-tuple-element.197), calls=%async_computation | async-start | bytes 4194304 | tf_op jit(solution)/shard_map/all_to_all | solution.py:468
  97.0 25.2 %collective-permute-start.15 = (f32[8,128,128]{2,1,0:T(8,128)}, f32[8,128,128]{2,1,0:T(8,128)S(1)}, u32[]{:S(2)}, u32[]{:S(2)}) collective-permute-start(f32[8,128,128]{2,1,0:T(8,128)} %add_panel_children.1.refs_0_), channel_id=1, source_target_pairs={{0,16},{4,20},{8,24},{12,28},{16,0},{20,4},{24,8},{28,12},{1,17},{... | collective-permute-start | bytes 1572872 | tf_op jit(solution)/shard_map/ppermute | solution.py:23
  122.1 0.8 copy-start.2
  122.9 8.4 %copy-start.1 = (f32[8,128,128]{2,1,0:T(8,128)S(1)}, f32[8,128,128]{2,1,0:T(8,128)}, u32[]{:S(2)}) copy-start(f32[8,128,128]{2,1,0:T(8,128)} %add_panel_children.1.refs_0_) | copy-start | bytes 1572868
  122.9 9.8 %copy-start.3 = (f32[8,128,128]{2,1,0:T(8,128)S(1)}, f32[8,128,128]{2,1,0:T(8,128)}, u32[]{:S(2)}) copy-start(f32[8,128,128]{2,1,0:T(8,128)} %copy-done.2) | copy-start | bytes 1572868
  122.9 123.8 %all-to-all-start.1 = ((f32[32,128,128]{2,1,0:T(8,128)}), f32[32,128,128]{2,1,0:T(8,128)S(1)}, u32[]{:S(2)}, u32[]{:S(2)}) async-start(f32[32,128,128]{2,1,0:T(8,128)} %after.1), calls=%async_computation.1 | async-start | bytes 4194304 | tf_op jit(solution)/shard_map/all_to_all | solution.py:520
  131.3 44.1 %collective-permute-start.19 = (f32[8,128,128]{2,1,0:T(8,128)S(1)}, f32[8,128,128]{2,1,0:T(8,128)S(1)}, u32[]{:S(2)}, u32[]{:S(2)}) collective-permute-start(f32[8,128,128]{2,1,0:T(8,128)S(1)} %copy-done.1), channel_id=1, source_target_pairs={{0,8},{4,12},{8,0},{12,4},{16,24},{20,28},{24,16},{28,20},{1,9},{5... | collective-permute-start | bytes 1572872 | tf_op jit(solution)/shard_map/ppermute | solution.py:23
  131.4 47.2 %collective-permute-start.17 = (f32[8,128,128]{2,1,0:T(8,128)S(1)}, f32[8,128,128]{2,1,0:T(8,128)S(1)}, u32[]{:S(2)}, u32[]{:S(2)}) collective-permute-start(f32[8,128,128]{2,1,0:T(8,128)S(1)} %copy-done.1), channel_id=1, source_target_pairs={{0,2},{1,3},{2,0},{3,1},{4,6},{5,7},{6,4},{7,5},{8,10},{9,11},{10,... | collective-permute-start | bytes 1572872 | tf_op jit(solution)/shard_map/ppermute | solution.py:23
  132.8 53.9 %collective-permute-start.24 = (f32[8,128,128]{2,1,0:T(8,128)S(1)}, f32[8,128,128]{2,1,0:T(8,128)S(1)}, u32[]{:S(2)}, u32[]{:S(2)}) collective-permute-start(f32[8,128,128]{2,1,0:T(8,128)S(1)} %copy-done.3), channel_id=1, source_target_pairs={{0,8},{4,12},{8,0},{12,4},{16,24},{20,28},{24,16},{28,20},{1,9},{5... | collective-permute-start | bytes 1572872 | tf_op jit(solution)/shard_map/ppermute | solution.py:23
  134.1 53.5 %collective-permute-start.16 = (f32[8,128,128]{2,1,0:T(8,128)S(1)}, f32[8,128,128]{2,1,0:T(8,128)S(1)}, u32[]{:S(2)}, u32[]{:S(2)}) collective-permute-start(f32[8,128,128]{2,1,0:T(8,128)S(1)} %copy-done.1), channel_id=1, source_target_pairs={{0,1},{1,0},{2,3},{3,2},{4,5},{5,4},{6,7},{7,6},{8,9},{9,8},{10,11... | collective-permute-start | bytes 1572872 | tf_op jit(solution)/shard_map/ppermute | solution.py:23
  175.5 14.9 %collective-permute-start.23 = (f32[8,128,128]{2,1,0:T(8,128)S(1)}, f32[8,128,128]{2,1,0:T(8,128)S(1)}, u32[]{:S(2)}, u32[]{:S(2)}) collective-permute-start(f32[8,128,128]{2,1,0:T(8,128)S(1)} %get-tuple-element.269), channel_id=1, source_target_pairs={{0,6},{1,2},{2,4},{3,0},{4,7},{5,3},{6,5},{7,1},{8,14},{9,10},{10,... | collective-permute-start | bytes 1572872 | tf_op jit(solution)/shard_map/ppermute | solution.py:528
  177.5 24.8 %collective-permute-start.22 = (f32[8,128,128]{2,1,0:T(8,128)S(1)}, f32[8,128,128]{2,1,0:T(8,128)S(1)}, u32[]{:S(2)}, u32[]{:S(2)}) collective-permute-start(f32[8,128,128]{2,1,0:T(8,128)S(1)} %get-tuple-element.269), channel_id=1, source_target_pairs={{0,2},{1,6},{2,0},{3,4},{4,3},{5,7},{6,1},{7,5},{8,10},{9,14},{10,... | collective-permute-start | bytes 1572872 | tf_op jit(solution)/shard_map/ppermute | solution.py:528
  178.6 48.9 %copy-start.6 = (f32[8,128,128]{2,1,0:T(8,128)}, f32[8,128,128]{2,1,0:T(8,128)S(1)}, u32[]{:S(2)}) copy-start(f32[8,128,128]{2,1,0:T(8,128)S(1)} %collective-permute-done.17.refs_2_) | copy-start | bytes 1572868
  178.6 23.7 %collective-permute-start.21 = (f32[8,128,128]{2,1,0:T(8,128)S(1)}, f32[8,128,128]{2,1,0:T(8,128)S(1)}, u32[]{:S(2)}, u32[]{:S(2)}) collective-permute-start(f32[8,128,128]{2,1,0:T(8,128)S(1)} %get-tuple-element.270), channel_id=1, source_target_pairs={{0,4},{1,0},{2,6},{3,2},{4,5},{5,1},{6,7},{7,3},{8,12},{9,8},{10,1... | collective-permute-start | bytes 1572872 | tf_op jit(solution)/shard_map/ppermute | solution.py:528
  186.6 18.4 %collective-permute-start.18 = (f32[8,128,128]{2,1,0:T(8,128)S(1)}, f32[8,128,128]{2,1,0:T(8,128)S(1)}, u32[]{:S(2)}, u32[]{:S(2)}) collective-permute-start(f32[8,128,128]{2,1,0:T(8,128)S(1)} %collective-permute-done.17.refs_2_), channel_id=1, source_target_pairs={{0,1},{1,0},{2,3},{3,2},{4,5},{5,4},{6,7},{7,6},{8,9},{9,8},{10,11... | collective-permute-start | bytes 1572872 | tf_op jit(solution)/shard_map/ppermute | solution.py:23
  187.6 20.8 %copy-start.4 = (f32[8,128,128]{2,1,0:T(8,128)}, f32[8,128,128]{2,1,0:T(8,128)S(1)}, u32[]{:S(2)}) copy-start(f32[8,128,128]{2,1,0:T(8,128)S(1)} %collective-permute-done.16.earlier_ref.refs_1_) | copy-start | bytes 1572868
  187.6 45.9 %collective-permute-start.20 = (f32[8,128,128]{2,1,0:T(8,128)S(1)}, f32[8,128,128]{2,1,0:T(8,128)S(1)}, u32[]{:S(2)}, u32[]{:S(2)}) collective-permute-start(f32[8,128,128]{2,1,0:T(8,128)S(1)} %get-tuple-element.270), channel_id=1, source_target_pairs={{0,0},{1,4},{2,2},{3,6},{4,1},{5,5},{6,3},{7,7},{8,8},{9,12},{10,1... | collective-permute-start | bytes 1572872 | tf_op jit(solution)/shard_map/ppermute | solution.py:528
  190.4 43.1 %copy-start.7 = (f32[8,128,128]{2,1,0:T(8,128)}, f32[8,128,128]{2,1,0:T(8,128)S(1)}, u32[]{:S(2)}) copy-start(f32[8,128,128]{2,1,0:T(8,128)S(1)} %collective-permute-done.23.refs_3_) | copy-start | bytes 1572868
  190.4 49.7 %collective-permute-start.28 = (f32[8,128,128]{2,1,0:T(8,128)S(1)}, f32[8,128,128]{2,1,0:T(8,128)S(1)}, u32[]{:S(2)}, u32[]{:S(2)}) collective-permute-start(f32[8,128,128]{2,1,0:T(8,128)S(1)} %get-tuple-element.267), channel_id=1, source_target_pairs={{0,6},{1,2},{2,4},{3,0},{4,7},{5,3},{6,5},{7,1},{8,14},{9,10},{10,... | collective-permute-start | bytes 1572872 | tf_op jit(solution)/shard_map/ppermute | solution.py:528
  202.3 31.2 %copy-start.8 = (f32[8,128,128]{2,1,0:T(8,128)}, f32[8,128,128]{2,1,0:T(8,128)S(1)}, u32[]{:S(2)}) copy-start(f32[8,128,128]{2,1,0:T(8,128)S(1)} %collective-permute-done.22.refs_2_) | copy-start | bytes 1572868
  202.3 37.8 %collective-permute-start.27 = (f32[8,128,128]{2,1,0:T(8,128)S(1)}, f32[8,128,128]{2,1,0:T(8,128)S(1)}, u32[]{:S(2)}, u32[]{:S(2)}) collective-permute-start(f32[8,128,128]{2,1,0:T(8,128)S(1)} %get-tuple-element.267), channel_id=1, source_target_pairs={{0,2},{1,6},{2,0},{3,4},{4,3},{5,7},{6,1},{7,5},{8,10},{9,14},{10,... | collective-permute-start | bytes 1572872 | tf_op jit(solution)/shard_map/ppermute | solution.py:528
  202.3 31.2 %copy-start.9 = (f32[8,128,128]{2,1,0:T(8,128)}, f32[8,128,128]{2,1,0:T(8,128)S(1)}, u32[]{:S(2)}) copy-start(f32[8,128,128]{2,1,0:T(8,128)S(1)} %collective-permute-done.21.refs_1_) | copy-start | bytes 1572868
  202.3 37.8 %collective-permute-start.26 = (f32[8,128,128]{2,1,0:T(8,128)S(1)}, f32[8,128,128]{2,1,0:T(8,128)}, u32[]{:S(2)}, u32[]{:S(2)}) collective-permute-start(f32[8,128,128]{2,1,0:T(8,128)S(1)} %get-tuple-element.268), channel_id=1, source_target_pairs={{0,4},{1,0},{2,6},{3,2},{4,5},{5,1},{6,7},{7,3},{8,12},{9,8},{10,1... | collective-permute-start | bytes 1572872 | tf_op jit(solution)/shard_map/ppermute | solution.py:528
  205.0 1.9 copy-start.12
  205.0 35.1 %collective-permute-start.25 = (f32[8,128,128]{2,1,0:T(8,128)S(1)}, f32[8,128,128]{2,1,0:T(8,128)}, u32[]{:S(2)}, u32[]{:S(2)}) collective-permute-start(f32[8,128,128]{2,1,0:T(8,128)S(1)} %get-tuple-element.268), channel_id=1, source_target_pairs={{0,0},{1,4},{2,2},{3,6},{4,1},{5,5},{6,3},{7,7},{8,8},{9,12},{10,1... | collective-permute-start | bytes 1572872 | tf_op jit(solution)/shard_map/ppermute | solution.py:528
  233.5 0.8 copy-start.13
  240.1 0.8 copy-start.10
  240.1 0.9 copy-start.11
  246.7 1.3 copy-start

commit v2 on v1

v2 whole, which is shorter than its diff:
```python
import functools

import jax
import jax.numpy as jnp
from jax import lax
from jax.experimental import pallas as pl
from jax.experimental.pallas import tpu as pltpu
from jax.sharding import PartitionSpec as P

ALL = ("prow", "pcol")
CAP = 2
HIGHEST = lax.Precision.HIGHEST
VMEM_LIMIT = 56 * 2**20
WHOLE = pl.BlockSpec(memory_space=pltpu.VMEM)
HBM = pl.BlockSpec(memory_space=pl.ANY)


def bits_of(size):
    return size.bit_length() - 1


def xor_send(x, axis, bit):
    size = lax.axis_size(axis)
    return lax.ppermute(x, axis, [(i, i ^ (1 << bit)) for i in range(size)])


def my_bit(axis, bit):
    return (lax.axis_index(axis) >> bit) & 1


def gather_bit(x, axis, bit):
    other = xor_send(x, axis, bit)
    low = my_bit(axis, bit) == 0
    return jnp.stack([jnp.where(low, x, other), jnp.where(low, other, x)])


def spread_high(x, axis, low_bits):
    for bit in range(low_bits, bits_of(lax.axis_size(axis))):
        other = lax.ppermute(x, axis, [(i, i | (1 << bit)) for i in range(1 << bit)])
        x = jnp.where(my_bit(axis, bit) == 1, other, x)
    return x


def nt_dot(a, b):
    return lax.dot_general(a, b, (((1,), (1,)), ((), ())), preferred_element_type=jnp.float32)


def split(x):
    high = x.astype(jnp.bfloat16)
    return high, (x - high.astype(jnp.float32)).astype(jnp.bfloat16)


def nt_dot3(a, b):
    return nt_dot(a[0], b[0]) + (nt_dot(a[1], b[0]) + nt_dot(a[0], b[1]))


def after_kernel(x_ref, *refs):
    pass


def after(x, *others):
    return pl.pallas_call(
        after_kernel,
        out_shape=jax.ShapeDtypeStruct(x.shape, x.dtype),
        in_specs=[HBM] * (1 + len(others)),
        out_specs=HBM,
        input_output_aliases={0: 0},
        name="after",
    )(x, *others)


def stage(ready, work, *operands):
    shapes = jax.eval_shape(work, *operands)
    return lax.cond(
        ready, work, lambda *_: jax.tree.map(lambda part: jnp.zeros(part.shape, part.dtype), shapes), *operands
    )


def pack_kernel(place_ref, child_ref, out_ref, sem):
    count = child_ref.shape[0]

    def copy(k):
        return pltpu.make_async_copy(child_ref.at[k], out_ref.at[place_ref[k]], sem.at[k])

    for k in range(count):
        copy(k).start()
    for k in range(count):
        copy(k).wait()


def pack(place, child_blocks, places):
    count, tile, _ = child_blocks.shape
    return pl.pallas_call(
        pack_kernel,
        out_shape=jax.ShapeDtypeStruct((places, tile, tile), jnp.float32),
        grid_spec=pltpu.PrefetchScalarGridSpec(
            num_scalar_prefetch=1,
            grid=(),
            in_specs=[WHOLE],
            out_specs=HBM,
            scratch_shapes=[pltpu.SemaphoreType.DMA((count,))],
        ),
        compiler_params=pltpu.CompilerParams(vmem_limit_bytes=VMEM_LIMIT),
        name="pack_children",
    )(place, child_blocks)


def strip_kernel(row_ref, strip_ref, got_ref, out_ref, buffer, sem):
    sources = got_ref.shape[0]

    def copy(s):
        return pltpu.make_async_copy(got_ref.at[s], buffer.at[s], sem.at[s])

    for s in range(sources):
        pl.when(row_ref[s] >= 0)(lambda s=s: copy(s).start())
    out_ref[...] = strip_ref[...]
    for s in range(sources):

        @pl.when(row_ref[s] >= 0)
        def _(s=s):
            copy(s).wait()
            out_ref[row_ref[s]] = out_ref[row_ref[s]] + buffer[s]


def add_to_strip(panel_row, strip, got):
    return pl.pallas_call(
        strip_kernel,
        out_shape=jax.ShapeDtypeStruct(strip.shape, jnp.float32),
        grid_spec=pltpu.PrefetchScalarGridSpec(
            num_scalar_prefetch=1,
            grid=(),
            in_specs=[WHOLE, HBM],
            out_specs=WHOLE,
            scratch_shapes=[
                pltpu.VMEM(got.shape, jnp.float32),
                pltpu.SemaphoreType.DMA((got.shape[0],)),
            ],
        ),
        compiler_params=pltpu.CompilerParams(vmem_limit_bytes=VMEM_LIMIT),
        name="add_panel_children",
    )(panel_row, strip, got)


def exact_dot(a, b, dims):
    return lax.dot_general(a, b, (dims, ((), ())), precision=HIGHEST, preferred_element_type=jnp.float32)


def inverse_root(x):
    y = lax.rsqrt(x)
    return y * (1.5 - 0.5 * x * y * y)


def eliminate(work_ref, right_ref, t_ref, z_ref):
    n = work_ref.shape[0]
    row = lax.broadcasted_iota(jnp.int32, (n, n), 0)
    col = lax.broadcasted_iota(jnp.int32, (n, n), 1)
    right_ref[...] = jnp.where(row == col, 1.0, 0.0)
    for j in range(0, n, 2):
        lo = j // 8 * 8
        i = j - lo
        a = work_ref[lo:, :]
        z = right_ref[lo:, :]
        col0 = jnp.broadcast_to(a[:, j : j + 1], a.shape)
        col1 = jnp.broadcast_to(a[:, j + 1 : j + 2], a.shape)
        inv0 = inverse_root(col0[i : i + 1, :])
        row0 = a[i : i + 1, :] * inv0
        low0 = col0 * inv0
        cross = low0[i + 1 : i + 2, :]
        low1 = col1 - low0 * cross
        inv1 = inverse_root(low1[i + 1 : i + 2, :])
        row1 = (a[i + 1 : i + 2, :] - cross * row0) * inv1
        low1 = low1 * inv1
        z0 = z[i : i + 1, :] * inv0
        z1 = (z[i + 1 : i + 2, :] - cross * z0) * inv1
        if j + 2 < n:
            work_ref[lo:, :] = a - low0 * row0 - low1 * row1
            right_ref[lo:, :] = z - low0 * z0 - low1 * z1
        t_ref[j : j + 1, :] = row0
        t_ref[j + 1 : j + 2, :] = row1
        z_ref[j : j + 1, :] = z0
        z_ref[j + 1 : j + 2, :] = z1


def lower_of(t):
    n = t.shape[0]
    row = lax.broadcasted_iota(jnp.int32, (n, n), 0)
    col = lax.broadcasted_iota(jnp.int32, (n, n), 1)
    return jnp.where(col <= row, t.T, 0.0)


def symmetric(block):
    n = block.shape[0]
    row = lax.broadcasted_iota(jnp.int32, (n, n), 0)
    col = lax.broadcasted_iota(jnp.int32, (n, n), 1)
    return jnp.where(col <= row, block, block.T)


def factor_panel(g, scratch):
    work, right, t, z = scratch
    nt, nn = ((1,), (1,)), ((1,), (0,))
    work[...] = symmetric(g[0][0])
    eliminate(work, right, t, z)
    l00, z00 = lower_of(t[...]), z[...]
    l10 = exact_dot(g[1][0], z00, nt)
    work[...] = symmetric(g[1][1]) - exact_dot(l10, l10, nt)
    eliminate(work, right, t, z)
    l11, z11 = lower_of(t[...]), z[...]
    z10 = -exact_dot(z11, exact_dot(l10, z00, nn), nn)
    return (l00, l10, l11), (z00, z10, z11)


def store_square(ref, blocks):
    tile = blocks[0].shape[0]
    ref[:tile, :tile] = blocks[0]
    ref[:tile, tile:] = jnp.zeros((tile, tile), ref.dtype)
    ref[tile:, :tile] = blocks[1]
    ref[tile:, tile:] = blocks[2]


def leading_block(ref, i, j):
    return ref[j % 2, j // 2, i % 2, i // 2, : ref.shape[-1], :]


def panel0_kernel(corner_ref, l_ref, zh_ref, zl_ref, *scratch):
    g = [[leading_block(corner_ref, i, j) for j in range(2)] for i in range(2)]
    lower, inverse = factor_panel(g, scratch)
    store_square(l_ref, lower)
    parts = [split(block) for block in inverse]
    store_square(zh_ref, [part[0] for part in parts])
    store_square(zl_ref, [part[1] for part in parts])


def panel1_kernel(pattern_ref, corner_ref, z0h_ref, z0l_ref, a_ref, ah_ref, al_ref, l_ref, zh_ref, zl_ref, *scratch):
    tile = corner_ref.shape[-1]
    z0 = (z0h_ref[...], z0l_ref[...])
    rows = [jnp.concatenate([leading_block(corner_ref, 2 + i, j) for j in range(2)], axis=1) for i in range(2)]
    a = jnp.concatenate([nt_dot3(split(rows[i]), z0) * pattern_ref[0, 2 + i].astype(jnp.float32) for i in range(2)], axis=0)
    a_ref[...] = a
    ah_ref[...], al_ref[...] = split(a)
    update = exact_dot(a, a, ((1,), (1,)))
    g = [
        [leading_block(corner_ref, 2 + i, 2 + j) - update[i * tile : (i + 1) * tile, j * tile : (j + 1) * tile] for j in range(2)]
        for i in range(2)
    ]
    lower, inverse = factor_panel(g, scratch)
    store_square(l_ref, lower)
    parts = [split(block) for block in inverse]
    store_square(zh_ref, [part[0] for part in parts])
    store_square(zl_ref, [part[1] for part in parts])


def factor_panel0(corner):
    tile = corner.shape[-1]
    full = jax.ShapeDtypeStruct((2 * tile, 2 * tile), jnp.float32)
    part = jax.ShapeDtypeStruct((2 * tile, 2 * tile), jnp.bfloat16)
    return pl.pallas_call(
        panel0_kernel,
        out_shape=(full, part, part),
        in_specs=[WHOLE],
        out_specs=(WHOLE,) * 3,
        scratch_shapes=[pltpu.VMEM((tile, tile), jnp.float32)] * 4,
        compiler_params=pltpu.CompilerParams(vmem_limit_bytes=VMEM_LIMIT),
        name="factor_panel0",
    )(corner)


def factor_panel1(corner, pattern, z0):
    tile = corner.shape[-1]
    full = jax.ShapeDtypeStruct((2 * tile, 2 * tile), jnp.float32)
    part = jax.ShapeDtypeStruct((2 * tile, 2 * tile), jnp.bfloat16)
    return pl.pallas_call(
        panel1_kernel,
        out_shape=(full, part, part, full, part, part),
        grid_spec=pltpu.PrefetchScalarGridSpec(
            num_scalar_prefetch=1,
            grid=(),
            in_specs=[WHOLE] * 3,
            out_specs=(WHOLE,) * 6,
            scratch_shapes=[pltpu.VMEM((tile, tile), jnp.float32)] * 4,
        ),
        compiler_params=pltpu.CompilerParams(vmem_limit_bytes=VMEM_LIMIT),
        name="factor_panel1",
    )(pattern, corner, *z0)


def solve_strips(x_refs, factors, pattern_ref, first_strip, block_row_of, xs, high_ref, low_ref, size, write):
    rows, tile, _ = x_refs[0].shape
    width = 2 * tile
    z0, a, z1 = factors

    def masked(q, panel, at):
        parts = []
        for i in range(size):
            block_row = block_row_of(at + i)
            keep = pattern_ref[0, block_row]
            if panel == 1:
                keep = jnp.maximum(keep, pattern_ref[1, block_row])
            parts.append(q[i * tile : (i + 1) * tile] * keep.astype(jnp.float32))
        return jnp.concatenate(parts, axis=0)

    for at in range(0, rows, size):
        for m in range(4):
            xs[first_strip ^ m] = x_refs[m][at : at + size].reshape(size * tile, tile)
        x0 = jnp.concatenate([xs[0], xs[1]], axis=1)
        x1 = jnp.concatenate([xs[2], xs[3]], axis=1)
        q0 = masked(nt_dot3(split(x0), z0), 0, at)
        q0_parts = split(q0)
        q1 = masked(nt_dot3(split(x1 - nt_dot3(q0_parts, a)), z1), 1, at)
        q1_parts = split(q1)
        where = slice(at * tile, (at + size) * tile)
        for ref, index in ((high_ref, 0), (low_ref, 1)):
            ref[where, :width] = q0_parts[index]
            ref[where, width:] = q1_parts[index]
        if write is not None:
            for index, q in enumerate((q0, q1)):
                xs[2 * index] = q[:, :tile]
                xs[2 * index + 1] = q[:, tile:]
            write(at)


def factor_pairs(refs):
    return [(refs[2 * i][...], refs[2 * i + 1][...]) for i in range(3)]


def rows_kernel(size, pattern_ref, place_ref, *refs):
    x_refs, factor_refs, (high_ref, low_ref, panel_ref, xs) = refs[:4], refs[4:10], refs[10:]
    tile = x_refs[0].shape[-1]
    strip = place_ref[1] % 4

    def write(at):
        panel_ref[at : at + size] = xs[strip].reshape(size, tile, tile)

    def block_row_of(a):
        return a * place_ref[2] + place_ref[0]

    solve_strips(x_refs, factor_pairs(factor_refs), pattern_ref, strip, block_row_of, xs, high_ref, low_ref, size, write)


def solve_rows(strips, pattern, place, factors):
    rows, tile, _ = strips[0].shape
    size = min(rows, 4)
    part = jax.ShapeDtypeStruct((rows * tile, 4 * tile), jnp.bfloat16)
    return pl.pallas_call(
        functools.partial(rows_kernel, size),
        out_shape=(part, part, jax.ShapeDtypeStruct((rows, tile, tile), jnp.float32)),
        grid_spec=pltpu.PrefetchScalarGridSpec(
            num_scalar_prefetch=2,
            grid=(),
            in_specs=[WHOLE] * 10,
            out_specs=(WHOLE,) * 3,
            scratch_shapes=[pltpu.VMEM((4, size * tile, tile), jnp.float32)],
        ),
        compiler_params=pltpu.CompilerParams(vmem_limit_bytes=VMEM_LIMIT),
        name="solve_rows",
    )(pattern, place, *strips, *factors)


def schur_kernel(size, panel_blocks, list_ref, pattern_ref, place_ref, before_ref, front_ref, got_ref, high_ref, low_ref,
                 panel_ref, l0_ref, a_ref, l1_ref, *refs):
    x_refs, factor_refs, (out_ref, xs, col_high, col_low) = refs[:4], refs[4:10], refs[10:]
    step = pl.program_id(0)
    depth, bcols, _, tile, _ = front_ref.shape
    my_row, my_col, grid_rows, grid_cols, share = [place_ref[i] for i in range(5)]

    @pl.when(step == 0)
    def _():
        def block_row_of(a):
            return a * grid_rows + share * grid_cols + my_col

        solve_strips(
            x_refs, factor_pairs(factor_refs), pattern_ref, my_row % 4, block_row_of, xs, col_high, col_low, size, None
        )

    rows = (high_ref[...], low_ref[...])
    for at in range(0, bcols, 2):
        piece = slice(at * tile, (at + 2) * tile)
        update = nt_dot3(rows, (col_high[piece, :], col_low[piece, :]))
        for k in range(2):
            for a in range(depth):
                out_ref[a, at + k, 0] = (
                    front_ref[a, at + k, 0] - update[a * tile : (a + 1) * tile, k * tile : (k + 1) * tile]
                )

    def body(k, carry):
        slot = list_ref[1, k]
        a, b = slot // bcols - step * depth, slot % bcols
        out_ref[a, b, 0] = out_ref[a, b, 0] + got_ref[list_ref[0, k]]
        return carry

    lax.fori_loop(list_ref[2, step], list_ref[2, step + 1], body, 0)

    for a in range(depth):
        block_row = (step * depth + a) * grid_rows + my_row

        @pl.when(block_row < panel_blocks)
        def _(a=a):
            out_ref[a] = jnp.zeros(out_ref.shape[1:], jnp.float32)

        @pl.when((my_col < panel_blocks) & (share == 0))
        def _(a=a):
            out_ref[a, 0, 0] = panel_ref[a]

        for i in range(panel_blocks):
            for j in range(panel_blocks):

                @pl.when((block_row == i) & (my_col == j) & (share == 0))
                def _(a=a, i=i, j=j):
                    ref = (l0_ref, None, a_ref, l1_ref)[i // 2 * 2 + j // 2]
                    rows_at, cols_at = i % 2 * tile, j % 2 * tile
                    if ref is None:
                        out_ref[a, 0, 0] = jnp.zeros((tile, tile), jnp.float32)
                    else:
                        out_ref[a, 0, 0] = ref[rows_at : rows_at + tile, cols_at : cols_at + tile]


def schur_share(depth, listed, pattern, place, before, front, got, rows, panel, corners, strips, factors, panel_blocks):
    brows, bcols, _, tile, _ = front.shape
    size = min(brows, 4)
    width = 4 * tile
    share = pl.BlockSpec((depth, bcols, 1, tile, tile), lambda i, listed, pattern, place: (i, 0, place[4], 0, 0))
    row_spec = pl.BlockSpec((depth * tile, width), lambda i, *_: (i, 0))
    return pl.pallas_call(
        functools.partial(schur_kernel, size, panel_blocks),
        out_shape=jax.ShapeDtypeStruct(front.shape, jnp.float32),
        grid_spec=pltpu.PrefetchScalarGridSpec(
            num_scalar_prefetch=3,
            grid=(brows // depth,),
            in_specs=[HBM, share, WHOLE, row_spec, row_spec, pl.BlockSpec((depth, tile, tile), lambda i, *_: (i, 0, 0))]
            + [WHOLE] * 13,
            out_specs=share,
            scratch_shapes=[
                pltpu.VMEM((4, size * tile, tile), jnp.float32),
                pltpu.VMEM((brows * tile, width), jnp.bfloat16),
                pltpu.VMEM((brows * tile, width), jnp.bfloat16),
            ],
        ),
        input_output_aliases={3: 0} if before is not front else {},
        compiler_params=pltpu.CompilerParams(vmem_limit_bytes=VMEM_LIMIT),
        name="schur_share",
    )(listed, pattern, place, before, front, got, *rows, panel, *corners, *strips, *factors)


def in_slot_order(slots, valid):
    count = slots.shape[0]
    index = jnp.arange(count, dtype=jnp.int32)
    key = jnp.where(valid, slots, 2**20) * count + index
    place = jnp.sum((key[None, :] < key[:, None]).astype(jnp.int32), axis=1)
    at = place[None, :] == index[:, None]
    return jnp.sum(jnp.where(at, index[None, :], 0), axis=1), jnp.sum(jnp.where(at, slots[None, :], 0), axis=1)


def by_slot(slots, valid, per_step, steps):
    index = jnp.arange(slots.shape[0], dtype=jnp.int32)
    sources, ordered = in_slot_order(slots, valid)
    bound = jnp.minimum(index, steps) * per_step
    starts = jnp.sum((valid[None, :] & (slots[None, :] < bound[:, None])).astype(jnp.int32), axis=1)
    return jnp.stack([sources, ordered, starts])


def local(front, child_blocks, owners, slots, pattern):
    grid_rows = lax.axis_size("prow")
    grid_cols = lax.axis_size("pcol")
    devices = grid_rows * grid_cols
    rank_r = lax.axis_index("prow")
    rank_c = lax.axis_index("pcol")
    me = rank_r * grid_cols + rank_c
    brows, _, bcols, _, tile, _ = front.shape
    row_bits, col_bits = bits_of(grid_rows), bits_of(grid_cols)
    panel_blocks = 2 * pattern.shape[0]
    panel_bits = bits_of(panel_blocks)
    owner_ids = owners[:, 0]
    children = owner_ids.shape[0]

    notes = jnp.zeros((8, tile), jnp.float32)
    notes = notes.at[0, :children].set(owner_ids.astype(jnp.float32)).at[1, :children].set(slots.astype(jnp.float32))
    corner = front[0, 0, 0, 0]

    def spread(corner, notes, axis):
        for bit in range(panel_bits, bits_of(lax.axis_size(axis))):
            other = xor_send(jnp.concatenate([corner, notes], axis=-2), axis, bit)
            high = my_bit(axis, bit) == 1
            corner, others = jnp.where(high, other[..., : corner.shape[-2], :], corner), other[..., corner.shape[-2] :, :]
            notes = jnp.concatenate([jnp.where(high, others, notes), jnp.where(high, notes, others)], axis=-2)
        return corner, notes

    index = jnp.arange(children, dtype=jnp.int32)

    def ranked(owner):
        same = owner[..., :, None] == owner[..., None, :]
        return jnp.sum((same & (index[None, :] < index[:, None])).astype(jnp.int32), axis=-1)

    corner, notes = spread(corner, notes, "prow")
    corner = jnp.concatenate([corner, notes], axis=0)
    for bit in reversed(range(1, panel_bits)):
        corner = gather_bit(corner, "prow", bit)
    send = after(pack(owner_ids * CAP + ranked(owner_ids), child_blocks, devices * CAP), corner)
    got = lax.all_to_all(send, ALL, 0, 0, tiled=True)
    corner = after(corner, send)
    depth = brows // 4
    highs = grid_rows // grid_cols
    my_high = rank_r // grid_cols
    share_cols = bcols // highs
    shares = [my_high ^ high for high in range(highs)]
    ready = owner_ids[0] >= 0

    def beside_children(corner):
        corner = gather_bit(corner, "prow", 0)
        corner, notes = spread(corner[..., :tile, :], corner[..., tile:, :], "pcol")
        corner = jnp.concatenate([corner, notes], axis=-2)
        for bit in reversed(range(panel_bits)):
            corner = gather_bit(corner, "pcol", bit)
        l0, *z0 = factor_panel0(corner)
        a, ah, al, l1, *z1 = factor_panel1(corner, pattern, z0)

        bits = row_bits + col_bits
        noted = corner[..., tile:, :].reshape((2,) * bits + (8, tile))[..., :2, :children].astype(jnp.int32)
        dims = [("col", bit) for bit in range(panel_bits)] + [("row", bit) for bit in range(panel_bits)]
        dims += [("col", bit) for bit in reversed(range(panel_bits, col_bits))]
        dims += [("row", bit) for bit in reversed(range(panel_bits, row_bits))]
        linear = [("row", bit) for bit in reversed(range(row_bits))] + [("col", bit) for bit in reversed(range(col_bits))]
        every = jnp.transpose(noted, [dims.index(dim) for dim in linear] + [bits, bits + 1])
        every = every.reshape(devices, 2, children)
        every_owner, every_slot = every[:, 0], every[:, 1]
        every_rank = ranked(every_owner)
        mine = every_owner == me
        got_slots = jnp.stack(
            [jnp.sum(jnp.where(mine & (every_rank == rank), every_slot, 0), axis=1) for rank in range(CAP)], axis=1
        ).reshape(-1)
        panel_here = (got_slots > 0) & (got_slots % bcols == 0) & (rank_c < panel_blocks)
        panel_row = jnp.where(panel_here, got_slots // bcols, -1)

        def listed(share):
            inside = (got_slots > 0) & ~panel_here & (got_slots % bcols % highs == share)
            slot = got_slots // bcols * share_cols + got_slots % bcols // highs
            return by_slot(slot, inside, depth * share_cols, brows // depth)

        return (l0, a, l1), (*z0, ah, al, *z1), panel_row, [listed(share) for share in shares]

    corners, factors, panel_row, lists = stage(ready, beside_children, corner)
    strip = add_to_strip(panel_row, front[:, 0, 0, 0], got)
    strip = spread_high(strip, "pcol", panel_bits)

    def to_column(part, m):
        pairs = [
            ((high * grid_cols + low) * grid_cols + c, (high * grid_cols + (c ^ m)) * grid_cols + low)
            for high in range(highs)
            for low in range(grid_cols)
            for c in range(grid_cols)
        ]
        return lax.ppermute(part, ALL, pairs)

    parts = {0: strip}
    for bit in reversed(range(col_bits, row_bits)):
        parts |= {key | (1 << (bit - col_bits)): xor_send(part, "prow", bit) for key, part in parts.items()}
    col_strips = [[to_column(parts[high], m) for m in range(panel_blocks)] for high in range(highs)]
    across, beside = xor_send(strip, "pcol", 1), xor_send(strip, "pcol", 0)
    row_strips = [strip, beside, across, xor_send(across, "pcol", 0)]
    place = jnp.stack([rank_r, rank_c, jnp.int32(grid_rows)])
    row_high, row_low, panel = solve_rows(row_strips, pattern, place, factors)
    blocks = front.reshape(brows, share_cols, highs, tile, tile)
    out = blocks
    for high, strips in enumerate(col_strips):
        place = jnp.stack([rank_r, rank_c, jnp.int32(grid_rows), jnp.int32(grid_cols), shares[high]])
        out = schur_share(
            depth, lists[high], pattern, place, out, blocks, got, (row_high, row_low), panel, corners, strips, factors,
            panel_blocks,
        )
    return out.reshape(front.shape)


def solution(mesh):
    placed = (
        P(None, "prow", None, "pcol", None, None),
        P(("prow", "pcol"), None, None),
        P(("prow", "pcol"), None),
        P(("prow", "pcol")),
        P(),
    )
    return jax.shard_map(
        local,
        mesh=mesh,
        in_specs=placed,
        out_specs=P(None, "prow", None, "pcol", None, None),
        check_vma=False,
    )
```

time: 266 us -> 205 us (0.77)
  waiting for transfers between devices: 120 us -> 66.1 us
  other arithmetic: 12.3 us -> 7.65 us
  starting transfers between devices: 47.6 us -> 44.6 us
    ppermute x15 -> x9, waiting for transfers between devices: 81.8 us -> 51.8 us  [xor_send(): return lax.ppermute(x, axis, [(i, i ^ 1 << bit) for i in range(size)])]
    all_to_all x2 -> x1, waiting for transfers between devices: 27.8 us -> 8.76 us  [local(): got = lax.all_to_all(send, ALL, 0, 0, tiled=True)]
    ppermute x8, starting transfers between devices: 12.3 us -> 19.2 us  [to_column(): return lax.ppermute(part, ALL, pairs)]
    ppermute x15 -> x9, starting transfers between devices: 23 us -> 17.4 us  [xor_send(): return lax.ppermute(x, axis, [(i, i ^ 1 << bit) for i in range(size)])]
    ppermute x8, waiting for transfers between devices: 10.9 us -> 5.57 us  [to_column(): return lax.ppermute(part, ALL, pairs)]
    unnamed x30 -> x18, local copies, waits for them, and re-layouts: 3.86 us -> 1.17 us
    all_to_all x2 -> x1, starting transfers between devices: 10.4 us -> 8.03 us  [local(): got = lax.all_to_all(send, ALL, 0, 0, tiled=True)]
    pallas_call x5 -> x4, Pallas kernels: 37.4 us -> 37.1 us  [the longest x2 26.6 us: schur_share(): pl.pallas_call(functools.partial(schur_kernel, size, panel_blocks), out_s...]
  transfers between devices with their start and end apart: 26 -> 18, of which waited for: 12 -> 7; matrix products, arithmetic and copies ran while one was open for 5% -> 4% of each run, Pallas kernels for 22% -> 30%
where the time goes in v2:
time: 205 us; the launch traced here: 202 us
  Pallas kernels  77.1 us (38%)
  waiting for transfers between devices  66.1 us (32%)
  starting transfers between devices  44.6 us (22%)
  other arithmetic  7.65 us (4%)
  local copies, waits for them, and re-layouts  5.62 us (3%)
    ppermute x9, waiting for transfers between devices, xor_send(): return lax.ppermute(x, axis, [(i, i ^ 1 << bit) for i in range(size)])  51.8 us
    pallas_call x2, Pallas kernels, schur_share(): pl.pallas_call(functools.partial(schur_kernel, size, panel_blocks), out_s...  26.6 us
    ppermute x8, starting transfers between devices, to_column(): return lax.ppermute(part, ALL, pairs)  19.2 us
    pallas_call x1, Pallas kernels, factor_panel1(): pl.pallas_call(panel1_kernel, out_shape=(full, part, part, full, part, pa...  18.4 us
    pallas_call x1, Pallas kernels, factor_panel0(): pl.pallas_call(panel0_kernel, out_shape=(full, part, part), in_specs=[WHO...  17.5 us
    ppermute x9, starting transfers between devices, xor_send(): return lax.ppermute(x, axis, [(i, i ^ 1 << bit) for i in range(size)])  17.4 us
    all_to_all x1, waiting for transfers between devices, local(): got = lax.all_to_all(send, ALL, 0, 0, tiled=True)  8.76 us
    all_to_all x1, starting transfers between devices, local(): got = lax.all_to_all(send, ALL, 0, 0, tiled=True)  8.03 us
  transfers between devices with their start and end apart: 18, of which 7 were waited for; matrix products, arithmetic and copies ran while one was open for 4% of the time, Pallas kernels for 30%

profile of v2, /device:TPU:9, one launch (start us, length us, event | category | flops | bytes accessed | tf_op | source)
XLA Modules:
  0.0 201.7 jit_solution(13562692945745099133)
XLA Ops:
  0.0 0.7 convert_bitcast_fusion
  0.7 0.7 convert_bitcast_fusion.1
  1.3 0.8 slice_bitcast_fusion.3
  2.2 0.2 scatter.9
  2.4 2.4 %collective-permute-start.3 = (f32[136,128]{1,0:T(8,128)S(1)}, f32[136,128]{1,0:T(8,128)S(1)}, u32[]{:S(2)}, u32[]{:S(2)}) collective-permute-start(f32[136,128]{1,0:T(8,128)S(1)} %pad_maximum_fusion.5), channel_id=1, source_target_pairs={{0,16},{4,20},{8,24},{12,28},{16,0},{20,4},{24,8},{28,12},{1,17},{... | collective-permute-start | bytes 208904 | tf_op jit(solution)/shard_map/ppermute | solution.py:24
  4.8 0.9 convert_reduce_fusion.5
  5.7 1.9 collective-permute-done.3
  7.6 0.8 slice_select_fusion
  8.5 1.2 multiply_add_fusion.1.place_ref
  9.7 3.8 %pack_children.1.x_ref = f32[64,128,128]{2,1,0:T(8,128)} custom-call(s32[32]{0:T(128)} %multiply_add_fusion.1.place_ref, f32[32,128,128]{2,1,0:T(8,128)} %child_ref.1), custom_call_target="tpu_custom_call" | custom-call | tf_op jit(solution)/shard_map/pack_children/pallas_call | solution.py:93
  13.6 8.0 %all-to-all-start = ((f32[64,128,128]{2,1,0:T(8,128)}), f32[64,128,128]{2,1,0:T(8,128)}, u32[]{:S(2)}, u32[]{:S(2)}) async-start(f32[64,128,128]{2,1,0:T(8,128)} %after.2.refs_0_), calls=%async_computation | async-start | bytes 8388608 | tf_op jit(solution)/shard_map/all_to_all | solution.py:497
  21.7 1.9 slice_bitcast_fusion.2.strip_ref
  23.6 80.6 %conditional.1 = (f32[256,256]{1,0:T(8,128)S(1)}, f32[256,256]{1,0:T(8,128)S(1)}, f32[256,256]{1,0:T(8,128)S(1)}, bf16[256,256]{1,0:T(8,128)(2,1)}, bf16[256,256...) conditional(s32[]{:T(128)} %bitcast.20, () %tuple.22, ...), branch_computations={%region_1.0_spmd, %region_2.14_spmd} | conditional | flops 1527825 | bytes 13772833 | solution.py:74
  23.6 1.2 collective-permute-start
  24.8 20.3 %collective-permute-done = f32[2,144,128]{2,1,0:T(8,128)S(1)} collective-permute-done((f32[2,144,128]{2,1,0:T(8,128)S(1)}, f32[2,144,128]{2,1,0:T(8,128)S(1)}, u32[]{:S(2)}, u32[]{:S(2)}) %collective-permute-start) | collective-permute-done | bytes 147488 | tf_op jit(solution)/shard_map/cond/branch_1_fun/ppermute | solution.py:24
  45.2 6.5 %collective-permute-start.1 = (f32[2,2,144,128]{3,2,1,0:T(8,128)S(1)}, f32[2,2,144,128]{3,2,1,0:T(8,128)S(1)}, u32[]{:S(2)}, u32[]{:S(2)}) collective-permute-start(f32[2,2,144,128]{3,2,1,0:T(8,128)S(1)} %pad_maximum_fusion.2), channel_id=1, source_target_pairs={{0,2},{1,3},{2,0},{3,1},{4,6},{5,7},{6,4},{7,5},{8,10},{9,11},{10,... | collective-permute-start | bytes 884744 | tf_op jit(solution)/shard_map/cond/branch_1_fun/ppermute | solution.py:24
  51.7 10.7 %collective-permute-done.1 = f32[2,2,144,128]{3,2,1,0:T(8,128)S(1)} collective-permute-done((f32[2,2,144,128]{3,2,1,0:T(8,128)S(1)}, f32[2,2,144,128]{3,2,1,0:T(8,128)S(1)}, u32[]{:S(2)}, u32[]{:S(2)}) %collective-permute-start.1) | collective-permute-done | bytes 294944 | tf_op jit(solution)/shard_map/cond/branch_1_fun/ppermute | solution.py:24
  62.5 1.1 collective-permute-start.2
  63.7 1.6 collective-permute-done.2
  65.3 1.1 pad_maximum_fusion.corner_ref
  66.5 0.8 convert_reduce_fusion
  67.6 17.5 %factor_panel0.1 = (f32[256,256]{1,0:T(8,128)S(1)}, bf16[256,256]{1,0:T(8,128)(2,1)}, bf16[256,256]{1,0:T(8,128)(2,1)}) custom-call(f32[2,2,2,2,144,128]{5,4,3,2,1,0:T(8,128)} %pad_maximum_fusion.corner_ref), custom_call_target="tpu_custom_call" | custom-call | tf_op jit(solution)/shard_map/cond/branch_1_fun/factor_panel0/pallas_call | solution.py:256
  85.1 0.2 convert_reduce_fusion.2
  85.3 0.2 select_reduce_fusion.1
  85.6 18.4 %factor_panel1.1 = (f32[256,256]{1,0:T(8,128)S(1)}, bf16[256,256]{1,0:T(8,128)(2,1)S(1)}, bf16[256,256]{1,0:T(8,128)(2,1)S(1)}, f32[256,256]{1,0:T(8,128)S(1)}, ...) custom-call(s32[2,64]{1,0:T(2,128)S(1)} %get-tuple-element.49.pattern_ref, ...), custom_call_target="tpu_custom_call" | custom-call | tf_op jit(solution)/shard_map/cond/branch_1_fun/factor_panel1/pallas_call | solution.py:271
  104.2 8.8 %all-to-all-done.got_ref = f32[64,128,128]{2,1,0:T(8,128)} async-done(((f32[64,128,128]{2,1,0:T(8,128)}), f32[64,128,128]{2,1,0:T(8,128)}, u32[]{:S(2)}, u32[]{:S(2)}) %all-to-all-start) | async-done | bytes 4194336 | tf_op jit(solution)/shard_map/all_to_all | solution.py:497
  113.0 4.2 %add_panel_children.1.refs_0_ = f32[8,128,128]{2,1,0:T(8,128)} custom-call(s32[64]{0:T(128)S(1)} %get-tuple-element.80.row_ref, f32[8,128,128]{2,1,0:T(8,128)} %slice_bitcast_fusion.2.strip_ref, f32[64,128,128]{2,1,0:T(8,128)} %all-to-all-done.got_ref), custom_call_target="tpu_custom_call" | custom-call | tf_op jit(solution)/shard_map/add_panel_children/pallas_call | solution.py:126
  117.1 3.2 %collective-permute-start.12 = (f32[8,128,128]{2,1,0:T(8,128)}, f32[8,128,128]{2,1,0:T(8,128)}, u32[]{:S(2)}, u32[]{:S(2)}) collective-permute-start(f32[8,128,128]{2,1,0:T(8,128)} %add_panel_children.1.refs_0_), channel_id=1, source_target_pairs={{0,16},{4,20},{8,24},{12,28},{16,0},{20,4},{24,8},{28,12},{1,17},{... | collective-permute-start | bytes 1572872 | tf_op jit(solution)/shard_map/ppermute | solution.py:24
  120.4 2.0 collective-permute-start.11
  122.3 0.2 collective-permute-start.10
  122.5 3.4 %collective-permute-start.9 = (f32[8,128,128]{2,1,0:T(8,128)}, f32[8,128,128]{2,1,0:T(8,128)S(1)}, u32[]{:S(2)}, u32[]{:S(2)}) collective-permute-start(f32[8,128,128]{2,1,0:T(8,128)} %add_panel_children.1.refs_0_), channel_id=1, source_target_pairs={{0,4},{1,0},{2,12},{3,8},{4,5},{5,1},{6,13},{7,9},{8,6},{9,2},{10,... | collective-permute-start | bytes 1572872 | tf_op jit(solution)/shard_map/ppermute | solution.py:550
  125.9 17.3 %collective-permute-done.12 = f32[8,128,128]{2,1,0:T(8,128)} collective-permute-done((f32[8,128,128]{2,1,0:T(8,128)}, f32[8,128,128]{2,1,0:T(8,128)}, u32[]{:S(2)}, u32[]{:S(2)}) %collective-permute-start.12) | collective-permute-done | bytes 524320 | tf_op jit(solution)/shard_map/ppermute | solution.py:24
  143.2 0.9 collective-permute-start.5
  144.1 2.0 %collective-permute-start.7 = (f32[8,128,128]{2,1,0:T(8,128)S(1)}, f32[8,128,128]{2,1,0:T(8,128)S(1)}, u32[]{:S(2)}, u32[]{:S(2)}) collective-permute-start(f32[8,128,128]{2,1,0:T(8,128)S(1)} %collective-permute-done.6.refs_2_), channel_id=1, source_target_pairs={{0,1},{1,0},{2,3},{3,2},{4,5},{5,4},{6,7},{7,6},{8,9},{9,8},{10,11... | collective-permute-start | bytes 1572872 | tf_op jit(solution)/shard_map/ppermute | solution.py:24
  146.2 3.6 %collective-permute-start.8 = (f32[8,128,128]{2,1,0:T(8,128)}, f32[8,128,128]{2,1,0:T(8,128)}, u32[]{:S(2)}, u32[]{:S(2)}) collective-permute-start(f32[8,128,128]{2,1,0:T(8,128)} %add_panel_children.1.refs_0_), channel_id=1, source_target_pairs={{0,0},{1,4},{2,8},{3,12},{4,1},{5,5},{6,9},{7,13},{8,2},{9,6},{10,... | collective-permute-start | bytes 1572872 | tf_op jit(solution)/shard_map/ppermute | solution.py:550
  149.8 5.6 %collective-permute-done.10.refs_2_ = f32[8,128,128]{2,1,0:T(8,128)S(1)} collective-permute-done((f32[8,128,128]{2,1,0:T(8,128)}, f32[8,128,128]{2,1,0:T(8,128)S(1)}, u32[]{:S(2)}, u32[]{:S(2)}) %collective-permute-start.10) | collective-permute-done | bytes 524320 | tf_op jit(solution)/shard_map/ppermute | solution.py:550
  155.3 2.0 collective-permute-start.16
  157.3 3.9 %collective-permute-start.15 = (f32[8,128,128]{2,1,0:T(8,128)}, f32[8,128,128]{2,1,0:T(8,128)}, u32[]{:S(2)}, u32[]{:S(2)}) collective-permute-start(f32[8,128,128]{2,1,0:T(8,128)} %collective-permute-done.12), channel_id=1, source_target_pairs={{0,8},{1,12},{2,0},{3,4},{4,9},{5,13},{6,1},{7,5},{8,10},{9,14},{1... | collective-permute-start | bytes 1572872 | tf_op jit(solution)/shard_map/ppermute | solution.py:550
  161.2 0.4 collective-permute-start.14
  161.7 0.3 copy-done.5
  162.0 3.6 %collective-permute-start.13 = (f32[8,128,128]{2,1,0:T(8,128)}, f32[8,128,128]{2,1,0:T(8,128)}, u32[]{:S(2)}, u32[]{:S(2)}) collective-permute-start(f32[8,128,128]{2,1,0:T(8,128)} %collective-permute-done.12), channel_id=1, source_target_pairs={{0,0},{1,4},{2,8},{3,12},{4,1},{5,5},{6,9},{7,13},{8,2},{9,6},{10,... | collective-permute-start | bytes 1572872 | tf_op jit(solution)/shard_map/ppermute | solution.py:550
  165.7 0.7 stack.100.place_ref
  166.3 0.6 stack.102.place_ref
  167.0 0.6 pad_add_fusion.3.place_ref
  167.5 6.6 %solve_rows.1 = (bf16[1024,512]{1,0:T(8,128)(2,1)}, bf16[1024,512]{1,0:T(8,128)(2,1)}, f32[8,128,128]{2,1,0:T(8,128)}) custom-call(s32[2,64]{1,0:T(2,128)S(1)} %copy-done.7, s32[3]{0:T(128)} %pad_add_fusion.3.place_ref, f32[8,128,128]{2,1,0:T(8,128)} %add_panel_children.1.refs_0_, f32[8,128,128]{2,1,0:T(8,128)} %copy-done.5, f32[8,128,128]{2,1,0:T(8,128)} %copy-done.4, ...), custom_call_target="tpu_custom_call" | custom-call | tf_op jit(solution)/shard_map/solve_rows/pallas_call | solution.py:343
  174.2 13.3 %schur_share.2.before_ref = f32[8,8,2,128,128]{4,3,2,1,0:T(8,128)} custom-call(s32[3,64]{1,0:T(4,128)S(1)} %get-tuple-element.79.list_ref, s32[2,64]{1,0:T(2,128)S(1)} %copy-done.7, s32[5]{0:T(128)} %stack.102.place_ref, f32[8,8,2,128,128]{4,3,2,1,0:T(8,128)} %bitcast.63, f32[8,8,2,128,128]{4,3,2,1,0:T(8,128)} %bitcast.64, ...), custom_call_target="tpu_custom_call" | custom-call | tf_op jit(solution)/shard_map/schur_share/pallas_call | solution.py:422
  187.5 0.8 copy-done.2
  188.3 13.3 %schur_share.3 = f32[8,8,2,128,128]{4,3,2,1,0:T(8,128)} custom-call(s32[3,64]{1,0:T(4,128)S(1)} %get-tuple-element.78.list_ref, s32[2,64]{1,0:T(2,128)S(1)} %copy-done.7, s32[5]{0:T(128)} %stack.100.place_ref, f32[8,8,2,128,128]{4,3,2,1,0:T(8,128)} %schur_share.2.before_ref, f32[8,8,2,128,128]{4,3,2,1,0:T(8,128)} %bitcast.65, ...), custom_call_target="tpu_custom_call", output_to_operand_aliasing={{}: (3, {})} | custom-call | tf_op jit(solution)/shard_map/schur_share/pallas_call | solution.py:422
  (57 shorter events, 0.9 us)
Async XLA Ops:
  2.4 5.2 %collective-permute-start.3 = (f32[136,128]{1,0:T(8,128)S(1)}, f32[136,128]{1,0:T(8,128)S(1)}, u32[]{:S(2)}, u32[]{:S(2)}) collective-permute-start(f32[136,128]{1,0:T(8,128)S(1)} %pad_maximum_fusion.5), channel_id=1, source_target_pairs={{0,16},{4,20},{8,24},{12,28},{16,0},{20,4},{24,8},{28,12},{1,17},{... | collective-permute-start | bytes 208904 | tf_op jit(solution)/shard_map/ppermute | solution.py:24
  8.4 5.1 %collective-permute-start.4 = (f32[144,128]{1,0:T(8,128)S(1)}, f32[144,128]{1,0:T(8,128)S(1)}, u32[]{:S(2)}, u32[]{:S(2)}) collective-permute-start(f32[144,128]{1,0:T(8,128)S(1)} %pad_maximum_fusion.4), channel_id=1, source_target_pairs={{0,8},{4,12},{8,0},{12,4},{16,24},{20,28},{24,16},{28,20},{1,9},{5... | collective-permute-start | bytes 221192 | tf_op jit(solution)/shard_map/ppermute | solution.py:24
  13.6 8.1 %copy-start.8 = (s32[32,1]{0,1:T(1,128)S(1)}, s32[32,1]{0,1:T(1,128)}, u32[]{:S(2)}) copy-start(s32[32,1]{0,1:T(1,128)} %param.13) | copy-start | bytes 388
  13.6 99.4 %all-to-all-start = ((f32[64,128,128]{2,1,0:T(8,128)}), f32[64,128,128]{2,1,0:T(8,128)}, u32[]{:S(2)}, u32[]{:S(2)}) async-start(f32[64,128,128]{2,1,0:T(8,128)} %after.2.refs_0_), calls=%async_computation | async-start | bytes 8388608 | tf_op jit(solution)/shard_map/all_to_all | solution.py:497
  21.6 2.0 copy-start.7
  23.6 21.5 %collective-permute-start = (f32[2,144,128]{2,1,0:T(8,128)S(1)}, f32[2,144,128]{2,1,0:T(8,128)S(1)}, u32[]{:S(2)}, u32[]{:S(2)}) collective-permute-start(f32[2,144,128]{2,1,0:T(8,128)S(1)} %get-tuple-element.47), channel_id=1, source_target_pairs={{0,4},{4,0},{8,12},{12,8},{16,20},{20,16},{24,28},{28,24},{1,5},{5... | collective-permute-start | bytes 442376 | tf_op jit(solution)/shard_map/cond/branch_1_fun/ppermute | solution.py:24
  45.2 17.2 %collective-permute-start.1 = (f32[2,2,144,128]{3,2,1,0:T(8,128)S(1)}, f32[2,2,144,128]{3,2,1,0:T(8,128)S(1)}, u32[]{:S(2)}, u32[]{:S(2)}) collective-permute-start(f32[2,2,144,128]{3,2,1,0:T(8,128)S(1)} %pad_maximum_fusion.2), channel_id=1, source_target_pairs={{0,2},{1,3},{2,0},{3,1},{4,6},{5,7},{6,4},{7,5},{8,10},{9,11},{10,... | collective-permute-start | bytes 884744 | tf_op jit(solution)/shard_map/cond/branch_1_fun/ppermute | solution.py:24
  62.5 2.7 %collective-permute-start.2 = (f32[2,2,2,144,128]{4,3,2,1,0:T(8,128)S(1)}, f32[2,2,2,144,128]{4,3,2,1,0:T(8,128)S(1)}, u32[]{:S(2)}, u32[]{:S(2)}) collective-permute-start(f32[2,2,2,144,128]{4,3,2,1,0:T(8,128)S(1)} %pad_maximum_fusion.1), channel_id=1, source_target_pairs={{0,1},{1,0},{2,3},{3,2},{4,5},{5,4},{6,7},{7,6},{8,9},{9,8},{10,11... | collective-permute-start | bytes 1769480 | tf_op jit(solution)/shard_map/cond/branch_1_fun/ppermute | solution.py:24
  117.1 26.1 %collective-permute-start.12 = (f32[8,128,128]{2,1,0:T(8,128)}, f32[8,128,128]{2,1,0:T(8,128)}, u32[]{:S(2)}, u32[]{:S(2)}) collective-permute-start(f32[8,128,128]{2,1,0:T(8,128)} %add_panel_children.1.refs_0_), channel_id=1, source_target_pairs={{0,16},{4,20},{8,24},{12,28},{16,0},{20,4},{24,8},{28,12},{1,17},{... | collective-permute-start | bytes 1572872 | tf_op jit(solution)/shard_map/ppermute | solution.py:24
  120.4 23.7 %collective-permute-start.6 = (f32[8,128,128]{2,1,0:T(8,128)}, f32[8,128,128]{2,1,0:T(8,128)S(1)}, u32[]{:S(2)}, u32[]{:S(2)}) collective-permute-start(f32[8,128,128]{2,1,0:T(8,128)} %add_panel_children.1.refs_0_), channel_id=1, source_target_pairs={{0,2},{1,3},{2,0},{3,1},{4,6},{5,7},{6,4},{7,5},{8,10},{9,11},{10,... | collective-permute-start | bytes 1572872 | tf_op jit(solution)/shard_map/ppermute | solution.py:24
  120.4 25.8 %collective-permute-start.11 = (f32[8,128,128]{2,1,0:T(8,128)}, f32[8,128,128]{2,1,0:T(8,128)S(1)}, u32[]{:S(2)}, u32[]{:S(2)}) collective-permute-start(f32[8,128,128]{2,1,0:T(8,128)} %add_panel_children.1.refs_0_), channel_id=1, source_target_pairs={{0,12},{1,8},{2,4},{3,0},{4,13},{5,9},{6,5},{7,1},{8,14},{9,10},{1... | collective-permute-start | bytes 1572872 | tf_op jit(solution)/shard_map/ppermute | solution.py:550
  122.3 33.0 %collective-permute-start.10 = (f32[8,128,128]{2,1,0:T(8,128)}, f32[8,128,128]{2,1,0:T(8,128)S(1)}, u32[]{:S(2)}, u32[]{:S(2)}) collective-permute-start(f32[8,128,128]{2,1,0:T(8,128)} %add_panel_children.1.refs_0_), channel_id=1, source_target_pairs={{0,8},{1,12},{2,0},{3,4},{4,9},{5,13},{6,1},{7,5},{8,10},{9,14},{1... | collective-permute-start | bytes 1572872 | tf_op jit(solution)/shard_map/ppermute | solution.py:550
  122.5 34.8 %collective-permute-start.9 = (f32[8,128,128]{2,1,0:T(8,128)}, f32[8,128,128]{2,1,0:T(8,128)S(1)}, u32[]{:S(2)}, u32[]{:S(2)}) collective-permute-start(f32[8,128,128]{2,1,0:T(8,128)} %add_panel_children.1.refs_0_), channel_id=1, source_target_pairs={{0,4},{1,0},{2,12},{3,8},{4,5},{5,1},{6,13},{7,9},{8,6},{9,2},{10,... | collective-permute-start | bytes 1572872 | tf_op jit(solution)/shard_map/ppermute | solution.py:550
  143.2 18.0 %collective-permute-start.5 = (f32[8,128,128]{2,1,0:T(8,128)}, f32[8,128,128]{2,1,0:T(8,128)S(1)}, u32[]{:S(2)}, u32[]{:S(2)}) collective-permute-start(f32[8,128,128]{2,1,0:T(8,128)} %add_panel_children.1.refs_0_), channel_id=1, source_target_pairs={{0,1},{1,0},{2,3},{3,2},{4,5},{5,4},{6,7},{7,6},{8,9},{9,8},{10,11... | collective-permute-start | bytes 1572872 | tf_op jit(solution)/shard_map/ppermute | solution.py:24
  144.1 13.2 %copy-start.4 = (f32[8,128,128]{2,1,0:T(8,128)}, f32[8,128,128]{2,1,0:T(8,128)S(1)}, u32[]{:S(2)}) copy-start(f32[8,128,128]{2,1,0:T(8,128)S(1)} %collective-permute-done.6.refs_2_) | copy-start | bytes 1572868
  144.1 17.6 %collective-permute-start.7 = (f32[8,128,128]{2,1,0:T(8,128)S(1)}, f32[8,128,128]{2,1,0:T(8,128)S(1)}, u32[]{:S(2)}, u32[]{:S(2)}) collective-permute-start(f32[8,128,128]{2,1,0:T(8,128)S(1)} %collective-permute-done.6.refs_2_), channel_id=1, source_target_pairs={{0,1},{1,0},{2,3},{3,2},{4,5},{5,4},{6,7},{7,6},{8,9},{9,8},{10,11... | collective-permute-start | bytes 1572872 | tf_op jit(solution)/shard_map/ppermute | solution.py:24
  146.2 28.0 %copy-start = (f32[8,128,128]{2,1,0:T(8,128)}, f32[8,128,128]{2,1,0:T(8,128)S(1)}, u32[]{:S(2)}) copy-start(f32[8,128,128]{2,1,0:T(8,128)S(1)} %collective-permute-done.11.refs_3_) | copy-start | bytes 1572868
  146.2 28.0 %collective-permute-start.8 = (f32[8,128,128]{2,1,0:T(8,128)}, f32[8,128,128]{2,1,0:T(8,128)}, u32[]{:S(2)}, u32[]{:S(2)}) collective-permute-start(f32[8,128,128]{2,1,0:T(8,128)} %add_panel_children.1.refs_0_), channel_id=1, source_target_pairs={{0,0},{1,4},{2,8},{3,12},{4,1},{5,5},{6,9},{7,13},{8,2},{9,6},{10,... | collective-permute-start | bytes 1572872 | tf_op jit(solution)/shard_map/ppermute | solution.py:550
  155.3 18.8 %copy-start.1 = (f32[8,128,128]{2,1,0:T(8,128)}, f32[8,128,128]{2,1,0:T(8,128)S(1)}, u32[]{:S(2)}) copy-start(f32[8,128,128]{2,1,0:T(8,128)S(1)} %collective-permute-done.10.refs_2_) | copy-start | bytes 1572868
  155.3 32.2 %collective-permute-start.16 = (f32[8,128,128]{2,1,0:T(8,128)}, f32[8,128,128]{2,1,0:T(8,128)S(1)}, u32[]{:S(2)}, u32[]{:S(2)}) collective-permute-start(f32[8,128,128]{2,1,0:T(8,128)} %collective-permute-done.12), channel_id=1, source_target_pairs={{0,12},{1,8},{2,4},{3,0},{4,13},{5,9},{6,5},{7,1},{8,14},{9,10},{1... | collective-permute-start | bytes 1572872 | tf_op jit(solution)/shard_map/ppermute | solution.py:550
  157.3 16.9 %copy-start.3 = (f32[8,128,128]{2,1,0:T(8,128)}, f32[8,128,128]{2,1,0:T(8,128)S(1)}, u32[]{:S(2)}) copy-start(f32[8,128,128]{2,1,0:T(8,128)S(1)} %collective-permute-done.9.refs_1_) | copy-start | bytes 1572868
  157.3 30.2 %collective-permute-start.15 = (f32[8,128,128]{2,1,0:T(8,128)}, f32[8,128,128]{2,1,0:T(8,128)}, u32[]{:S(2)}, u32[]{:S(2)}) collective-permute-start(f32[8,128,128]{2,1,0:T(8,128)} %collective-permute-done.12), channel_id=1, source_target_pairs={{0,8},{1,12},{2,0},{3,4},{4,9},{5,13},{6,1},{7,5},{8,10},{9,14},{1... | collective-permute-start | bytes 1572872 | tf_op jit(solution)/shard_map/ppermute | solution.py:550
  161.2 0.8 copy-start.5
  161.2 26.3 %collective-permute-start.14 = (f32[8,128,128]{2,1,0:T(8,128)}, f32[8,128,128]{2,1,0:T(8,128)}, u32[]{:S(2)}, u32[]{:S(2)}) collective-permute-start(f32[8,128,128]{2,1,0:T(8,128)} %collective-permute-done.12), channel_id=1, source_target_pairs={{0,4},{1,0},{2,12},{3,8},{4,5},{5,1},{6,13},{7,9},{8,6},{9,2},{10,... | collective-permute-start | bytes 1572872 | tf_op jit(solution)/shard_map/ppermute | solution.py:550
  162.0 3.6 %copy-start.6 = (f32[8,128,128]{2,1,0:T(8,128)}, f32[8,128,128]{2,1,0:T(8,128)S(1)}, u32[]{:S(2)}) copy-start(f32[8,128,128]{2,1,0:T(8,128)S(1)} %collective-permute-done.7.refs_3_) | copy-start | bytes 1572868
  162.0 25.5 %collective-permute-start.13 = (f32[8,128,128]{2,1,0:T(8,128)}, f32[8,128,128]{2,1,0:T(8,128)}, u32[]{:S(2)}, u32[]{:S(2)}) collective-permute-start(f32[8,128,128]{2,1,0:T(8,128)} %collective-permute-done.12), channel_id=1, source_target_pairs={{0,0},{1,4},{2,8},{3,12},{4,1},{5,5},{6,9},{7,13},{8,2},{9,6},{10,... | collective-permute-start | bytes 1572872 | tf_op jit(solution)/shard_map/ppermute | solution.py:550
  187.5 0.8 copy-start.2

commit v3 on v2

--- a/solution.py
+++ b/solution.py
@@ -9,10 +9,16 @@
 
 ALL = ("prow", "pcol")
 CAP = 2
+DEPTH = 2
 HIGHEST = lax.Precision.HIGHEST
-VMEM_LIMIT = 56 * 2**20
 WHOLE = pl.BlockSpec(memory_space=pltpu.VMEM)
-HBM = pl.BlockSpec(memory_space=pl.ANY)
+HBM = pl.BlockSpec(memory_space=pltpu.HBM)
+ANY = pl.BlockSpec(memory_space=pl.ANY)
+
+
+def vmem(mib, *arrays):
+    held = sum(array.size * array.dtype.itemsize for array in arrays)
+    return pltpu.CompilerParams(vmem_limit_bytes=mib * 2**20 + held)
 
 
 def bits_of(size):
@@ -32,6 +38,18 @@
     other = xor_send(x, axis, bit)
     low = my_bit(axis, bit) == 0
     return jnp.stack([jnp.where(low, x, other), jnp.where(low, other, x)])
+
+
+def gather_bits(x, axis, bits):
+    size = lax.axis_size(axis)
+    masks = [0]
+    for bit in bits:
+        masks = [mask | on for mask in masks for on in (0, 1 << bit)]
+    sent = [lax.ppermute(x, axis, [(i, i ^ mask) for i in range(size)]) if mask else x for mask in masks]
+    whole = jnp.stack(sent).reshape((2,) * len(bits) + x.shape)
+    for dim, bit in enumerate(bits):
+        whole = jnp.where(my_bit(axis, bit) == 0, whole, jnp.flip(whole, dim))
+    return whole
 
 
 def spread_high(x, axis, low_bits):
@@ -62,8 +80,8 @@
     return pl.pallas_call(
         after_kernel,
         out_shape=jax.ShapeDtypeStruct(x.shape, x.dtype),
-        in_specs=[HBM] * (1 + len(others)),
-        out_specs=HBM,
+        in_specs=[ANY] * (1 + len(others)),
+        out_specs=ANY,
         input_output_aliases={0: 0},
         name="after",
     )(x, *others)
@@ -100,7 +118,7 @@
             out_specs=HBM,
             scratch_shapes=[pltpu.SemaphoreType.DMA((count,))],
         ),
-        compiler_params=pltpu.CompilerParams(vmem_limit_bytes=VMEM_LIMIT),
+        compiler_params=vmem(48, child_blocks),
         name="pack_children",
     )(place, child_blocks)
 
@@ -136,7 +154,7 @@
                 pltpu.SemaphoreType.DMA((got.shape[0],)),
             ],
         ),
-        compiler_params=pltpu.CompilerParams(vmem_limit_bytes=VMEM_LIMIT),
+        compiler_params=vmem(8, got),
         name="add_panel_children",
     )(panel_row, strip, got)
 
@@ -259,7 +277,7 @@
         in_specs=[WHOLE],
         out_specs=(WHOLE,) * 3,
         scratch_shapes=[pltpu.VMEM((tile, tile), jnp.float32)] * 4,
-        compiler_params=pltpu.CompilerParams(vmem_limit_bytes=VMEM_LIMIT),
+        compiler_params=vmem(12),
         name="factor_panel0",
     )(corner)
 
@@ -278,62 +296,61 @@
             out_specs=(WHOLE,) * 6,
             scratch_shapes=[pltpu.VMEM((tile, tile), jnp.float32)] * 4,
         ),
-        compiler_params=pltpu.CompilerParams(vmem_limit_bytes=VMEM_LIMIT),
+        compiler_params=vmem(12),
         name="factor_panel1",
     )(pattern, corner, *z0)
 
 
-def solve_strips(x_refs, factors, pattern_ref, first_strip, block_row_of, xs, high_ref, low_ref, size, write):
-    rows, tile, _ = x_refs[0].shape
-    width = 2 * tile
-    z0, a, z1 = factors
+def nn_dot3(a, b):
+    def dot(x, y):
+        return lax.dot_general(x, y, (((1,), (0,)), ((), ())), preferred_element_type=jnp.float32)
+
+    return dot(a[0], b[0]) + (dot(a[1], b[0]) + dot(a[0], b[1]))
+
+
+def rows_kernel(size, pattern_ref, place_ref, *refs):
+    strip_refs, factor_refs, (high_ref, low_ref, panel_ref, xs, x_refs, sem) = refs[:4], refs[4:10], refs[10:]
+    _, rows, tile, _ = x_refs.shape
+    copies = [pltpu.make_async_copy(ref, x_refs.at[m], sem.at[m]) for m, ref in enumerate(strip_refs)]
+    for copy in copies:
+        copy.start()
+    for copy in copies:
+        copy.wait()
+    z0, a, z1 = [(factor_refs[2 * i][...], factor_refs[2 * i + 1][...]) for i in range(3)]
+    strip, base = place_ref[1] % 4, place_ref[0] % 4
 
     def masked(q, panel, at):
         parts = []
         for i in range(size):
-            block_row = block_row_of(at + i)
+            block_row = (at + i) * place_ref[2] + place_ref[0]
             keep = pattern_ref[0, block_row]
             if panel == 1:
                 keep = jnp.maximum(keep, pattern_ref[1, block_row])
             parts.append(q[i * tile : (i + 1) * tile] * keep.astype(jnp.float32))
         return jnp.concatenate(parts, axis=0)
 
+    def spread_out(first, second):
+        for index, whole in enumerate((first, second)):
+            xs[2 * index] = whole[:, :tile]
+            xs[2 * index + 1] = whole[:, tile:]
+
     for at in range(0, rows, size):
         for m in range(4):
-            xs[first_strip ^ m] = x_refs[m][at : at + size].reshape(size * tile, tile)
+            xs[strip ^ m] = x_refs[m, at : at + size].reshape(size * tile, tile)
         x0 = jnp.concatenate([xs[0], xs[1]], axis=1)
         x1 = jnp.concatenate([xs[2], xs[3]], axis=1)
         q0 = masked(nt_dot3(split(x0), z0), 0, at)
         q0_parts = split(q0)
         q1 = masked(nt_dot3(split(x1 - nt_dot3(q0_parts, a)), z1), 1, at)
-        q1_parts = split(q1)
-        where = slice(at * tile, (at + size) * tile)
-        for ref, index in ((high_ref, 0), (low_ref, 1)):
-            ref[where, :width] = q0_parts[index]
-            ref[where, width:] = q1_parts[index]
-        if write is not None:
-            for index, q in enumerate((q0, q1)):
-                xs[2 * index] = q[:, :tile]
-                xs[2 * index + 1] = q[:, tile:]
-            write(at)
-
-
-def factor_pairs(refs):
-    return [(refs[2 * i][...], refs[2 * i + 1][...]) for i in range(3)]
-
-
-def rows_kernel(size, pattern_ref, place_ref, *refs):
-    x_refs, factor_refs, (high_ref, low_ref, panel_ref, xs) = refs[:4], refs[4:10], refs[10:]
-    tile = x_refs[0].shape[-1]
-    strip = place_ref[1] % 4
-
-    def write(at):
+        spread_out(q0, q1)
         panel_ref[at : at + size] = xs[strip].reshape(size, tile, tile)
-
-    def block_row_of(a):
-        return a * place_ref[2] + place_ref[0]
-
-    solve_strips(x_refs, factor_pairs(factor_refs), pattern_ref, strip, block_row_of, xs, high_ref, low_ref, size, write)
+        w1 = nn_dot3(split(q1), z1)
+        w0 = nn_dot3(split(q0 - nn_dot3(split(w1), a)), z0)
+        spread_out(w0, w1)
+        for m in range(4):
+            high_ref[at * tile : (at + size) * tile, m * tile : (m + 1) * tile], low_ref[
+                at * tile : (at + size) * tile, m * tile : (m + 1) * tile
+            ] = split(xs[base ^ m])
 
 
 def solve_rows(strips, pattern, place, factors):
@@ -346,98 +363,145 @@
         grid_spec=pltpu.PrefetchScalarGridSpec(
             num_scalar_prefetch=2,
             grid=(),
-            in_specs=[WHOLE] * 10,
+            in_specs=[ANY] * 4 + [WHOLE] * 6,
             out_specs=(WHOLE,) * 3,
-            scratch_shapes=[pltpu.VMEM((4, size * tile, tile), jnp.float32)],
+            scratch_shapes=[
+                pltpu.VMEM((4, size * tile, tile), jnp.float32),
+                pltpu.VMEM((4, rows, tile, tile), jnp.float32),
+                pltpu.SemaphoreType.DMA((4,)),
+            ],
         ),
-        compiler_params=pltpu.CompilerParams(vmem_limit_bytes=VMEM_LIMIT),
+        compiler_params=vmem(20),
         name="solve_rows",
     )(pattern, place, *strips, *factors)
 
 
-def schur_kernel(size, panel_blocks, list_ref, pattern_ref, place_ref, before_ref, front_ref, got_ref, high_ref, low_ref,
+def schur_kernel(panel_blocks, list_ref, pattern_ref, place_ref, before_ref, front_ref, got_ref, high_ref, low_ref,
                  panel_ref, l0_ref, a_ref, l1_ref, *refs):
-    x_refs, factor_refs, (out_ref, xs, col_high, col_low) = refs[:4], refs[4:10], refs[10:]
-    step = pl.program_id(0)
-    depth, bcols, _, tile, _ = front_ref.shape
+    strip_refs, (out_ref, col_high, col_low, blocks, x_refs, children, child_sem, read_sem, write_sem, x_sem) = refs[:5], refs[5:]
+    brows, bcols, tile, _ = blocks.shape
+    steps = brows // DEPTH
     my_row, my_col, grid_rows, grid_cols, share = [place_ref[i] for i in range(5)]
 
-    @pl.when(step == 0)
-    def _():
-        def block_row_of(a):
-            return a * grid_rows + share * grid_cols + my_col
-
-        solve_strips(
-            x_refs, factor_pairs(factor_refs), pattern_ref, my_row % 4, block_row_of, xs, col_high, col_low, size, None
-        )
-
-    rows = (high_ref[...], low_ref[...])
-    for at in range(0, bcols, 2):
-        piece = slice(at * tile, (at + 2) * tile)
-        update = nt_dot3(rows, (col_high[piece, :], col_low[piece, :]))
-        for k in range(2):
-            for a in range(depth):
-                out_ref[a, at + k, 0] = (
-                    front_ref[a, at + k, 0] - update[a * tile : (a + 1) * tile, k * tile : (k + 1) * tile]
-                )
-
-    def body(k, carry):
-        slot = list_ref[1, k]
-        a, b = slot // bcols - step * depth, slot % bcols
-        out_ref[a, b, 0] = out_ref[a, b, 0] + got_ref[list_ref[0, k]]
+    def child(k):
+        return pltpu.make_async_copy(got_ref.at[list_ref[0, k]], children.at[k], child_sem.at[k])
+
+    def read(step):
+        rows = pl.ds(step * DEPTH, DEPTH)
+        return pltpu.make_async_copy(front_ref.at[rows, :, share], blocks.at[rows], read_sem.at[step])
+
+    def write(step):
+        rows = pl.ds(step * DEPTH, DEPTH)
+        return pltpu.make_async_copy(blocks.at[rows], out_ref.at[rows, :, share], write_sem.at[step])
+
+    own = my_row % grid_cols == my_col
+
+    def strip(m, source):
+        return pltpu.make_async_copy(strip_refs[source], x_refs.at[m], x_sem.at[m])
+
+    pl.when(own)(lambda: strip(0, 4).start())
+    pl.when(jnp.logical_not(own))(lambda: strip(0, 0).start())
+    for m in range(1, 4):
+        strip(m, m).start()
+    for step in range(steps):
+        read(step).start()
+
+    def start(k, carry):
+        child(k).start()
         return carry
 
-    lax.fori_loop(list_ref[2, step], list_ref[2, step + 1], body, 0)
-
-    for a in range(depth):
-        block_row = (step * depth + a) * grid_rows + my_row
-
-        @pl.when(block_row < panel_blocks)
-        def _(a=a):
-            out_ref[a] = jnp.zeros(out_ref.shape[1:], jnp.float32)
-
-        @pl.when((my_col < panel_blocks) & (share == 0))
-        def _(a=a):
-            out_ref[a, 0, 0] = panel_ref[a]
-
-        for i in range(panel_blocks):
-            for j in range(panel_blocks):
-
-                @pl.when((block_row == i) & (my_col == j) & (share == 0))
-                def _(a=a, i=i, j=j):
-                    ref = (l0_ref, None, a_ref, l1_ref)[i // 2 * 2 + j // 2]
-                    rows_at, cols_at = i % 2 * tile, j % 2 * tile
-                    if ref is None:
-                        out_ref[a, 0, 0] = jnp.zeros((tile, tile), jnp.float32)
-                    else:
-                        out_ref[a, 0, 0] = ref[rows_at : rows_at + tile, cols_at : cols_at + tile]
-
-
-def schur_share(depth, listed, pattern, place, before, front, got, rows, panel, corners, strips, factors, panel_blocks):
+    lax.fori_loop(0, list_ref[2, steps], start, 0)
+
+    for m in range(4):
+        strip(m, m).wait()
+        for a in range(bcols):
+            block_row = a * grid_rows + share * grid_cols + my_col
+            first_keep = pattern_ref[0, block_row]
+            keep = jnp.where((my_row ^ m) & 2 == 0, first_keep, jnp.maximum(first_keep, pattern_ref[1, block_row]))
+            high, low = split(x_refs[m, a] * keep.astype(jnp.float32))
+            at = (slice(a * tile, (a + 1) * tile), slice(m * tile, (m + 1) * tile))
+            col_high[at] = high
+            col_low[at] = low
+    for step in range(steps):
+        first = step * DEPTH
+        rows = tuple(ref[first * tile : (first + DEPTH) * tile, :] for ref in (high_ref, low_ref))
+        read(step).wait()
+        for at in range(0, bcols, 2):
+            cols = slice(at * tile, (at + 2) * tile)
+            update = nt_dot3(rows, (col_high[cols, :], col_low[cols, :]))
+            for k in range(2):
+                for a in range(DEPTH):
+                    blocks[first + a, at + k] = (
+                        blocks[first + a, at + k] - update[a * tile : (a + 1) * tile, k * tile : (k + 1) * tile]
+                    )
+
+        def body(k, carry):
+            slot = list_ref[1, k]
+            a, b = slot // bcols, slot % bcols
+            child(k).wait()
+            blocks[a, b] = blocks[a, b] + children[k]
+            return carry
+
+        lax.fori_loop(list_ref[2, step], list_ref[2, step + 1], body, 0)
+
+        for a in range(first, first + DEPTH):
+            block_row = a * grid_rows + my_row
+
+            @pl.when(block_row < panel_blocks)
+            def _(a=a):
+                blocks[a] = jnp.zeros(blocks.shape[1:], jnp.float32)
+
+            @pl.when((my_col < panel_blocks) & (share == 0))
+            def _(a=a):
+                blocks[a, 0] = panel_ref[a]
+
+            for i in range(panel_blocks):
+                for j in range(panel_blocks):
+
+                    @pl.when((block_row == i) & (my_col == j) & (share == 0))
+                    def _(a=a, i=i, j=j):
+                        ref = (l0_ref, None, a_ref, l1_ref)[i // 2 * 2 + j // 2]
+                        if ref is None:
+                            blocks[a, 0] = jnp.zeros((tile, tile), jnp.float32)
+                        else:
+                            part = ref.at[pl.ds(i % 2 * tile, tile), pl.ds(j % 2 * tile, tile)]
+                            copy = pltpu.make_async_copy(part, blocks.at[a, 0], x_sem.at[0])
+                            copy.start()
+                            copy.wait()
+
+        write(step).start()
+    for step in range(steps):
+        write(step).wait()
+
+
+def schur_share(listed, pattern, place, before, front, got, rows, panel, corners, strips, panel_blocks):
     brows, bcols, _, tile, _ = front.shape
-    size = min(brows, 4)
     width = 4 * tile
-    share = pl.BlockSpec((depth, bcols, 1, tile, tile), lambda i, listed, pattern, place: (i, 0, place[4], 0, 0))
-    row_spec = pl.BlockSpec((depth * tile, width), lambda i, *_: (i, 0))
+    blocks = jax.ShapeDtypeStruct((brows, bcols, tile, tile), jnp.float32)
     return pl.pallas_call(
-        functools.partial(schur_kernel, size, panel_blocks),
+        functools.partial(schur_kernel, panel_blocks),
         out_shape=jax.ShapeDtypeStruct(front.shape, jnp.float32),
         grid_spec=pltpu.PrefetchScalarGridSpec(
             num_scalar_prefetch=3,
-            grid=(brows // depth,),
-            in_specs=[HBM, share, WHOLE, row_spec, row_spec, pl.BlockSpec((depth, tile, tile), lambda i, *_: (i, 0, 0))]
-            + [WHOLE] * 13,
-            out_specs=share,
+            grid=(),
+            in_specs=[HBM] * 3 + [WHOLE] * 3 + [ANY] * 8,
+            out_specs=HBM,
             scratch_shapes=[
-                pltpu.VMEM((4, size * tile, tile), jnp.float32),
-                pltpu.VMEM((brows * tile, width), jnp.bfloat16),
-                pltpu.VMEM((brows * tile, width), jnp.bfloat16),
+                pltpu.VMEM((bcols * tile, width), jnp.bfloat16),
+                pltpu.VMEM((bcols * tile, width), jnp.bfloat16),
+                pltpu.VMEM(blocks.shape, jnp.float32),
+                pltpu.VMEM((4, bcols, tile, tile), jnp.float32),
+                pltpu.VMEM(got.shape, jnp.float32),
+                pltpu.SemaphoreType.DMA((got.shape[0],)),
+                pltpu.SemaphoreType.DMA((brows // DEPTH,)),
+                pltpu.SemaphoreType.DMA((brows // DEPTH,)),
+                pltpu.SemaphoreType.DMA((4,)),
             ],
         ),
         input_output_aliases={3: 0} if before is not front else {},
-        compiler_params=pltpu.CompilerParams(vmem_limit_bytes=VMEM_LIMIT),
+        compiler_params=vmem(40, got, blocks),
         name="schur_share",
-    )(listed, pattern, place, before, front, got, *rows, panel, *corners, *strips, *factors)
+    )(listed, pattern, place, before, front, got, *rows, panel, *corners, *strips)
 
 
 def in_slot_order(slots, valid):
@@ -489,14 +553,16 @@
         same = owner[..., :, None] == owner[..., None, :]
         return jnp.sum((same & (index[None, :] < index[:, None])).astype(jnp.int32), axis=-1)
 
-    corner, notes = spread(corner, notes, "prow")
-    corner = jnp.concatenate([corner, notes], axis=0)
-    for bit in reversed(range(1, panel_bits)):
-        corner = gather_bit(corner, "prow", bit)
-    send = after(pack(owner_ids * CAP + ranked(owner_ids), child_blocks, devices * CAP), corner)
+    hops = list(reversed(range(1, row_bits)))
+    every = gather_bits(jnp.concatenate([corner, notes], axis=0), "prow", hops)
+    corner = every[(0,) * (row_bits - panel_bits)][..., :tile, :]
+    notes = every[..., tile:, :].reshape(-1, tile)
+    corner = jnp.concatenate([corner, jnp.broadcast_to(notes, corner.shape[:-2] + notes.shape)], axis=-2)
+    packed = pack(owner_ids * CAP + ranked(owner_ids), child_blocks, devices * CAP)
+    corner = gather_bit(corner, "prow", 0)
+    send = after(packed, corner)
     got = lax.all_to_all(send, ALL, 0, 0, tiled=True)
     corner = after(corner, send)
-    depth = brows // 4
     highs = grid_rows // grid_cols
     my_high = rank_r // grid_cols
     share_cols = bcols // highs
@@ -504,19 +570,18 @@
     ready = owner_ids[0] >= 0
 
     def beside_children(corner):
-        corner = gather_bit(corner, "prow", 0)
         corner, notes = spread(corner[..., :tile, :], corner[..., tile:, :], "pcol")
         corner = jnp.concatenate([corner, notes], axis=-2)
-        for bit in reversed(range(panel_bits)):
-            corner = gather_bit(corner, "pcol", bit)
+        corner = jnp.swapaxes(gather_bits(corner, "pcol", list(reversed(range(panel_bits)))), 0, 1)
         l0, *z0 = factor_panel0(corner)
         a, ah, al, l1, *z1 = factor_panel1(corner, pattern, z0)
 
         bits = row_bits + col_bits
-        noted = corner[..., tile:, :].reshape((2,) * bits + (8, tile))[..., :2, :children].astype(jnp.int32)
-        dims = [("col", bit) for bit in range(panel_bits)] + [("row", bit) for bit in range(panel_bits)]
+        noted = corner[:, :, :, 0, tile:, :]
+        dims = [("col", bit) for bit in range(panel_bits)] + [("row", 0)]
         dims += [("col", bit) for bit in reversed(range(panel_bits, col_bits))]
-        dims += [("row", bit) for bit in reversed(range(panel_bits, row_bits))]
+        dims += [("row", bit) for bit in reversed(range(1, row_bits))]
+        noted = noted.reshape((2,) * bits + (8, tile))[..., :2, :children].astype(jnp.int32)
         linear = [("row", bit) for bit in reversed(range(row_bits))] + [("col", bit) for bit in reversed(range(col_bits))]
         every = jnp.transpose(noted, [dims.index(dim) for dim in linear] + [bits, bits + 1])
         every = every.reshape(devices, 2, children)
@@ -532,13 +597,12 @@
         def listed(share):
             inside = (got_slots > 0) & ~panel_here & (got_slots % bcols % highs == share)
             slot = got_slots // bcols * share_cols + got_slots % bcols // highs
-            return by_slot(slot, inside, depth * share_cols, brows // depth)
+            return by_slot(slot, inside, DEPTH * share_cols, brows // DEPTH)
 
         return (l0, a, l1), (*z0, ah, al, *z1), panel_row, [listed(share) for share in shares]
 
     corners, factors, panel_row, lists = stage(ready, beside_children, corner)
-    strip = add_to_strip(panel_row, front[:, 0, 0, 0], got)
-    strip = spread_high(strip, "pcol", panel_bits)
+    strip = spread_high(add_to_strip(panel_row, front[:, 0, 0, 0], got), "pcol", panel_bits)
 
     def to_column(part, m):
         pairs = [
@@ -547,23 +611,24 @@
             for low in range(grid_cols)
             for c in range(grid_cols)
         ]
-        return lax.ppermute(part, ALL, pairs)
+        return lax.ppermute(part, ALL, [(source, target) for source, target in pairs if source != target])
 
     parts = {0: strip}
     for bit in reversed(range(col_bits, row_bits)):
         parts |= {key | (1 << (bit - col_bits)): xor_send(part, "prow", bit) for key, part in parts.items()}
-    col_strips = [[to_column(parts[high], m) for m in range(panel_blocks)] for high in range(highs)]
+    col_strips = [
+        [to_column(parts[high], m) for m in range(panel_blocks)] + [parts[high]] for high in range(highs)
+    ]
     across, beside = xor_send(strip, "pcol", 1), xor_send(strip, "pcol", 0)
     row_strips = [strip, beside, across, xor_send(across, "pcol", 0)]
     place = jnp.stack([rank_r, rank_c, jnp.int32(grid_rows)])
     row_high, row_low, panel = solve_rows(row_strips, pattern, place, factors)
     blocks = front.reshape(brows, share_cols, highs, tile, tile)
     out = blocks
-    for high, strips in enumerate(col_strips):
-        place = jnp.stack([rank_r, rank_c, jnp.int32(grid_rows), jnp.int32(grid_cols), shares[high]])
+    for listed, share, strips in zip(lists, shares, col_strips):
+        place = jnp.stack([rank_r, rank_c, jnp.int32(grid_rows), jnp.int32(grid_cols), share])
         out = schur_share(
-            depth, lists[high], pattern, place, out, blocks, got, (row_high, row_low), panel, corners, strips, factors,
-            panel_blocks,
+            listed, pattern, place, out, blocks, got, (row_high, row_low), panel, corners, strips, panel_blocks
         )
     return out.reshape(front.shape)
 

time: 205 us -> 198 us (0.966)
  waiting for transfers between devices: 66.1 us -> 78 us
  Pallas kernels: 77.1 us -> 65.6 us
  starting transfers between devices: 44.6 us -> 38.3 us
  other arithmetic: 7.65 us -> 4.23 us
  local copies, waits for them, and re-layouts: 5.62 us -> 8.96 us
    ppermute x8 -> x14, waiting for transfers between devices: 5.57 us -> 47.5 us  [the longest x6 43.6 us: gather_bits(): lax.ppermute(x, axis, [(i, i ^ mask) for i in range(size)])]
    ppermute x9 -> x5, waiting for transfers between devices: 51.8 us -> 19.2 us  [xor_send(): return lax.ppermute(x, axis, [(i, i ^ 1 << bit) for i in range(size)])]
    ppermute x9 -> x5, starting transfers between devices: 17.4 us -> 6.32 us  [xor_send(): return lax.ppermute(x, axis, [(i, i ^ 1 << bit) for i in range(size)])]
    pallas_call x2, Pallas kernels: 26.6 us -> 18.7 us  [schur_share(): pl.pallas_call(functools.partial(schur_kernel, panel_blocks), out_shape=j...]
    ppermute x8 -> x14, starting transfers between devices: 19.2 us -> 24.4 us  [the longest x8 19.5 us: to_column(): lax.ppermute(part, ALL, [(source, target) for source, target in pairs if...]
    unnamed x18 -> x26, local copies, waits for them, and re-layouts: 1.17 us -> 6.33 us
    all_to_all x1, waiting for transfers between devices: 8.76 us -> 11.2 us  [local(): got = lax.all_to_all(send, ALL, 0, 0, tiled=True)]
  transfers between devices with their start and end apart: 18 -> 20, of which waited for: 7 -> 11; matrix products, arithmetic and copies ran while one was open for 4% -> 2% of each run, Pallas kernels for 30% -> 28%
where the time goes in v3:
time: 198 us; the launch traced here: 196 us
  waiting for transfers between devices  78 us (39%)
  Pallas kernels  65.6 us (33%)
  starting transfers between devices  38.3 us (19%)
  local copies, waits for them, and re-layouts  8.96 us (5%)
  other arithmetic  4.23 us (2%)
    ppermute x6, waiting for transfers between devices, gather_bits(): lax.ppermute(x, axis, [(i, i ^ mask) for i in range(size)])  43.6 us
    ppermute x8, starting transfers between devices, to_column(): lax.ppermute(part, ALL, [(source, target) for source, target in pairs if...  19.5 us
    ppermute x5, waiting for transfers between devices, xor_send(): return lax.ppermute(x, axis, [(i, i ^ 1 << bit) for i in range(size)])  19.2 us
    pallas_call x2, Pallas kernels, schur_share(): pl.pallas_call(functools.partial(schur_kernel, panel_blocks), out_shape=j...  18.7 us
    pallas_call x1, Pallas kernels, factor_panel1(): pl.pallas_call(panel1_kernel, out_shape=(full, part, part, full, part, pa...  18.7 us
    pallas_call x1, Pallas kernels, factor_panel0(): pl.pallas_call(panel0_kernel, out_shape=(full, part, part), in_specs=[WHO...  16.2 us
    all_to_all x1, waiting for transfers between devices, local(): got = lax.all_to_all(send, ALL, 0, 0, tiled=True)  11.2 us
    all_to_all x1, starting transfers between devices, local(): got = lax.all_to_all(send, ALL, 0, 0, tiled=True)  7.63 us
  transfers between devices with their start and end apart: 20, of which 11 were waited for; matrix products, arithmetic and copies ran while one was open for 2% of the time, Pallas kernels for 28%

profile of v3, /device:TPU:9, one launch (start us, length us, event | category | flops | bytes accessed | tf_op | source)
XLA Modules:
  0.0 195.7 jit_solution(6748198149814998026)
XLA Ops:
  0.0 0.7 convert_bitcast_fusion
  0.7 0.7 convert_bitcast_fusion.1
  1.3 0.8 slice_bitcast_fusion.4
  2.4 2.4 %collective-permute-start.4 = (f32[136,128]{1,0:T(8,128)S(1)}, f32[136,128]{1,0:T(8,128)S(1)}, u32[]{:S(2)}, u32[]{:S(2)}) collective-permute-start(f32[136,128]{1,0:T(8,128)S(1)} %get-tuple-element.116), channel_id=1, source_target_pairs={{0,16},{4,20},{8,24},{12,28},{16,0},{20,4},{24,8},{28,12},{1,17},{... | collective-permute-start | bytes 208904 | tf_op jit(solution)/shard_map/ppermute | solution.py:48
  5.1 0.9 convert_reduce_fusion.5
  6.0 1.3 collective-permute-done.4
  7.3 1.2 collective-permute-done.3
  8.5 2.1 %collective-permute-done.5 = f32[136,128]{1,0:T(8,128)S(1)} collective-permute-done((f32[136,128]{1,0:T(8,128)S(1)}, f32[136,128]{1,0:T(8,128)S(1)}, u32[]{:S(2)}, u32[]{:S(2)}) %collective-permute-start.5) | collective-permute-done | bytes 69664 | tf_op jit(solution)/shard_map/ppermute | solution.py:48
  10.7 1.3 collective-permute-start.6
  12.2 2.1 %pack_children.1.x_ref = f32[64,128,128]{2,1,0:T(8,128)} custom-call(s32[32]{0:T(128)S(1)} %multiply_add_fusion.1.place_ref, f32[32,128,128]{2,1,0:T(8,128)S(1)} %copy-done), custom_call_target="tpu_custom_call" | custom-call | tf_op jit(solution)/shard_map/pack_children/pallas_call | solution.py:111
  14.3 1.3 collective-permute-done.6
  15.6 7.6 %all-to-all-start = ((f32[64,128,128]{2,1,0:T(8,128)}), f32[64,128,128]{2,1,0:T(8,128)}, u32[]{:S(2)}, u32[]{:S(2)}) async-start(f32[64,128,128]{2,1,0:T(8,128)} %after.2.refs_0_), calls=%async_computation | async-start | bytes 8388608 | tf_op jit(solution)/shard_map/all_to_all | solution.py:564
  23.3 1.1 slice_bitcast_fusion.2.strip_ref
  24.5 0.7 copy-done.9
  25.1 78.3 %conditional.1 = (f32[256,256]{1,0:T(8,128)}, f32[256,256]{1,0:T(8,128)}, f32[256,256]{1,0:T(8,128)S(1)}, bf16[256,256]{1,0:T(8,128)(2,1)}, bf16[256,256]{1,0:T(...) conditional(s32[]{:T(128)} %bitcast.20, () %tuple.22, ...), branch_computations={%region_1.0_spmd, %region_2.14_spmd} | conditional | flops 1880075 | bytes 14755807 | solution.py:92
  25.1 1.4 collective-permute-start.2
  26.5 0.3 collective-permute-start.1
  26.8 0.4 collective-permute-start
  27.3 29.6 %collective-permute-done.2 = f32[2,2,160,128]{3,2,1,0:T(8,128)S(1)} collective-permute-done((f32[2,2,160,128]{3,2,1,0:T(8,128)S(1)}, f32[2,2,160,128]{3,2,1,0:T(8,128)S(1)}, u32[]{:S(2)}, u32[]{:S(2)}) %collective-permute-start.2) | collective-permute-done | bytes 327712 | tf_op jit(solution)/shard_map/cond/branch_1_fun/ppermute | solution.py:48
  56.9 9.4 %collective-permute-done.1 = f32[2,2,160,128]{3,2,1,0:T(8,128)S(1)} collective-permute-done((f32[2,2,160,128]{3,2,1,0:T(8,128)S(1)}, f32[2,2,160,128]{3,2,1,0:T(8,128)S(1)}, u32[]{:S(2)}, u32[]{:S(2)}) %collective-permute-start.1) | collective-permute-done | bytes 327712 | tf_op jit(solution)/shard_map/cond/branch_1_fun/ppermute | solution.py:48
  66.8 16.2 %factor_panel0.1 = (f32[256,256]{1,0:T(8,128)}, bf16[256,256]{1,0:T(8,128)(2,1)}, bf16[256,256]{1,0:T(8,128)(2,1)}) custom-call(f32[2,2,2,2,160,128]{5,4,3,2,1,0:T(8,128)S(1)} %fusion.corner_ref), custom_call_target="tpu_custom_call" | custom-call | tf_op jit(solution)/shard_map/cond/branch_1_fun/factor_panel0/pallas_call | solution.py:274
  83.1 0.8 convert_reduce_fusion
  84.7 18.7 %factor_panel1.1 = (f32[256,256]{1,0:T(8,128)}, bf16[256,256]{1,0:T(8,128)(2,1)}, bf16[256,256]{1,0:T(8,128)(2,1)}, f32[256,256]{1,0:T(8,128)S(1)}, bf16[256,256...) custom-call(s32[2,64]{1,0:T(2,128)S(1)} %get-tuple-element.49.pattern_ref, f32[2,2,2,2,160,128]{5,4,3,2,1,0:T(8,128)S(1)} %fusion.corner_ref, ...), custom_call_target="tpu_custom_call" | custom-call | tf_op jit(solution)/shard_map/cond/branch_1_fun/factor_panel1/pallas_call | solution.py:289
  103.4 11.2 %all-to-all-done.got_ref = f32[64,128,128]{2,1,0:T(8,128)} async-done(((f32[64,128,128]{2,1,0:T(8,128)}), f32[64,128,128]{2,1,0:T(8,128)}, u32[]{:S(2)}, u32[]{:S(2)}) %all-to-all-start) | async-done | bytes 4194336 | tf_op jit(solution)/shard_map/all_to_all | solution.py:564
  114.6 2.3 %add_panel_children.1.refs_0_.refs_4_ = f32[8,128,128]{2,1,0:T(8,128)S(1)} custom-call(s32[64]{0:T(128)S(1)} %get-tuple-element.80.row_ref, f32[8,128,128]{2,1,0:T(8,128)S(1)} %slice_bitcast_fusion.2.strip_ref, f32[64,128,128]{2,1,0:T(8,128)} %all-to-all-done.got_ref), custom_call_target="tpu_custom_call" | custom-call | tf_op jit(solution)/shard_map/add_panel_children/pallas_call | solution.py:144
  116.9 3.1 %collective-permute-start.14 = (f32[8,128,128]{2,1,0:T(8,128)S(1)}, f32[8,128,128]{2,1,0:T(8,128)S(1)}, u32[]{:S(2)}, u32[]{:S(2)}) collective-permute-start(f32[8,128,128]{2,1,0:T(8,128)S(1)} %add_panel_children.1.refs_0_.refs_4_), channel_id=1, source_target_pairs={{0,16},{4,20},{8,24},{12,28},{16,0},{20,4},{24,8},{28,12},{1,17},{... | collective-permute-start | bytes 1572872 | tf_op jit(solution)/shard_map/ppermute | solution.py:30
  120.0 2.2 %collective-permute-start.13 = (f32[8,128,128]{2,1,0:T(8,128)S(1)}, f32[8,128,128]{2,1,0:T(8,128)S(1)}, u32[]{:S(2)}, u32[]{:S(2)}) collective-permute-start(f32[8,128,128]{2,1,0:T(8,128)S(1)} %add_panel_children.1.refs_0_.refs_4_), channel_id=1, source_target_pairs={{0,12},{1,8},{2,4},{3,0},{4,13},{5,9},{6,5},{7,1},{8,14},{9,10},{1... | collective-permute-start | bytes 1572872 | tf_op jit(solution)/shard_map/ppermute | solution.py:614
  122.4 3.4 %collective-permute-start.11 = (f32[8,128,128]{2,1,0:T(8,128)S(1)}, f32[8,128,128]{2,1,0:T(8,128)S(1)}, u32[]{:S(2)}, u32[]{:S(2)}) collective-permute-start(f32[8,128,128]{2,1,0:T(8,128)S(1)} %add_panel_children.1.refs_0_.refs_4_), channel_id=1, source_target_pairs={{0,4},{1,0},{2,12},{3,8},{4,5},{5,1},{6,13},{7,9},{8,6},{9,2},{10,... | collective-permute-start | bytes 1572872 | tf_op jit(solution)/shard_map/ppermute | solution.py:614
  125.8 15.7 %collective-permute-done.14.refs_4_ = f32[8,128,128]{2,1,0:T(8,128)S(1)} collective-permute-done((f32[8,128,128]{2,1,0:T(8,128)S(1)}, f32[8,128,128]{2,1,0:T(8,128)S(1)}, u32[]{:S(2)}, u32[]{:S(2)}) %collective-permute-start.14) | collective-permute-done | bytes 524320 | tf_op jit(solution)/shard_map/ppermute | solution.py:30
  141.5 0.5 collective-permute-start.7
  141.9 2.2 %collective-permute-done.8.refs_2_ = f32[8,128,128]{2,1,0:T(8,128)S(1)} collective-permute-done((f32[8,128,128]{2,1,0:T(8,128)S(1)}, f32[8,128,128]{2,1,0:T(8,128)S(1)}, u32[]{:S(2)}, u32[]{:S(2)}) %collective-permute-start.8) | collective-permute-done | bytes 524320 | tf_op jit(solution)/shard_map/ppermute | solution.py:30
  144.2 1.4 collective-permute-start.9
  145.6 0.8 copy-done.1
  146.4 5.0 %collective-permute-start.10 = (f32[8,128,128]{2,1,0:T(8,128)S(1)}, f32[8,128,128]{2,1,0:T(8,128)}, u32[]{:S(2)}, u32[]{:S(2)}) collective-permute-start(f32[8,128,128]{2,1,0:T(8,128)S(1)} %add_panel_children.1.refs_0_.refs_4_), channel_id=1, source_target_pairs={{1,4},{2,8},{3,12},{4,1},{6,9},{7,13},{8,2},{9,6},{11,14},{12,3},{... | collective-permute-start | bytes 1572872 | tf_op jit(solution)/shard_map/ppermute | solution.py:614
  151.4 3.6 %collective-permute-done.12.refs_2_ = f32[8,128,128]{2,1,0:T(8,128)S(1)} collective-permute-done((f32[8,128,128]{2,1,0:T(8,128)S(1)}, f32[8,128,128]{2,1,0:T(8,128)S(1)}, u32[]{:S(2)}, u32[]{:S(2)}) %collective-permute-start.12) | collective-permute-done | bytes 524320 | tf_op jit(solution)/shard_map/ppermute | solution.py:614
  155.0 1.7 collective-permute-start.18
  156.7 0.9 collective-permute-start.17
  157.6 0.8 copy-done.3
  158.4 1.8 collective-permute-start.16
  160.2 0.8 copy-done.5
  161.0 4.4 %collective-permute-start.15 = (f32[8,128,128]{2,1,0:T(8,128)S(1)}, f32[8,128,128]{2,1,0:T(8,128)}, u32[]{:S(2)}, u32[]{:S(2)}) collective-permute-start(f32[8,128,128]{2,1,0:T(8,128)S(1)} %collective-permute-done.14.refs_4_), channel_id=1, source_target_pairs={{1,4},{2,8},{3,12},{4,1},{6,9},{7,13},{8,2},{9,6},{11,14},{12,3},{... | collective-permute-start | bytes 1572872 | tf_op jit(solution)/shard_map/ppermute | solution.py:614
  165.7 1.0 copy-done.2
  166.7 1.0 copy-done.4
  167.7 1.0 copy-done.6
  168.8 7.6 %solve_rows.1 = (bf16[1024,512]{1,0:T(8,128)(2,1)S(1)}, bf16[1024,512]{1,0:T(8,128)(2,1)S(1)}, f32[8,128,128]{2,1,0:T(8,128)S(1)}) custom-call(s32[2,64]{1,0:T(2,128)S(1)} %copy-done.9, s32[3]{0:T(128)S(1)} %pad_add_fusion.3.place_ref, f32[8,128,128]{2,1,0:T(8,128)S(1)} %add_panel_children.1.refs_0_.refs_4_, f32[8,128,128]{2,1,0:T(8,128)S(1)} %copy-done.4, ...), custom_call_target="tpu_custom_call" | custom-call | tf_op jit(solution)/shard_map/solve_rows/pallas_call | solution.py:360
  176.4 9.5 %schur_share.2.before_ref = f32[8,8,2,128,128]{4,3,2,1,0:T(8,128)} custom-call(s32[3,64]{1,0:T(4,128)S(1)} %copy-done.11, s32[2,64]{1,0:T(2,128)S(1)} %copy-done.9, s32[5]{0:T(128)S(1)} %stack.110.place_ref, f32[8,8,2,128,128]{4,3,2,1,0:T(8,128)} %bitcast.64, f32[8,8,2,128,128]{4,3,2,1,0:T(8,128)} %bitcast.65, f32[64,128,128]{2,1,0:T(8,128)} %all-to-all-done.got_ref, ...), custom_call_target="tpu_custom_call" | custom-call | tf_op jit(solution)/shard_map/schur_share/pallas_call | solution.py:481
  185.9 0.3 collective-permute-done.15.refs_0_
  186.3 9.3 %schur_share.3 = f32[8,8,2,128,128]{4,3,2,1,0:T(8,128)} custom-call(s32[3,64]{1,0:T(4,128)S(1)} %get-tuple-element.78.list_ref, s32[2,64]{1,0:T(2,128)S(1)} %copy-done.9, s32[5]{0:T(128)S(1)} %stack.108.place_ref, f32[8,8,2,128,128]{4,3,2,1,0:T(8,128)} %schur_share.2.before_ref, f32[8,8,2,128,128]{4,3,2,1,0:T(8,128)} %bitcast.66, ...), custom_call_target="tpu_custom_call", output_to_operand_aliasing={{}: (3, {})} | custom-call | tf_op jit(solution)/shard_map/schur_share/pallas_call | solution.py:481
  (72 shorter events, 2.6 us)
Async XLA Ops:
  2.4 5.0 %collective-permute-start.4 = (f32[136,128]{1,0:T(8,128)S(1)}, f32[136,128]{1,0:T(8,128)S(1)}, u32[]{:S(2)}, u32[]{:S(2)}) collective-permute-start(f32[136,128]{1,0:T(8,128)S(1)} %get-tuple-element.116), channel_id=1, source_target_pairs={{0,16},{4,20},{8,24},{12,28},{16,0},{20,4},{24,8},{28,12},{1,17},{... | collective-permute-start | bytes 208904 | tf_op jit(solution)/shard_map/ppermute | solution.py:48
  4.8 3.7 %collective-permute-start.3 = (f32[136,128]{1,0:T(8,128)S(1)}, f32[136,128]{1,0:T(8,128)S(1)}, u32[]{:S(2)}, u32[]{:S(2)}) collective-permute-start(f32[136,128]{1,0:T(8,128)S(1)} %get-tuple-element.116), channel_id=1, source_target_pairs={{0,8},{4,12},{8,0},{12,4},{16,24},{20,28},{24,16},{28,20},{1,9},{5... | collective-permute-start | bytes 208904 | tf_op jit(solution)/shard_map/ppermute | solution.py:48
  4.9 5.6 %collective-permute-start.5 = (f32[136,128]{1,0:T(8,128)S(1)}, f32[136,128]{1,0:T(8,128)S(1)}, u32[]{:S(2)}, u32[]{:S(2)}) collective-permute-start(f32[136,128]{1,0:T(8,128)S(1)} %get-tuple-element.116), channel_id=1, source_target_pairs={{0,24},{4,28},{8,16},{12,20},{16,8},{20,12},{24,0},{28,4},{1,25},{... | collective-permute-start | bytes 208904 | tf_op jit(solution)/shard_map/ppermute | solution.py:48
  10.6 1.5 copy-start.12
  10.6 1.6 copy-start
  10.7 4.8 %collective-permute-start.6 = (f32[2,160,128]{2,1,0:T(8,128)S(1)}, f32[2,160,128]{2,1,0:T(8,128)S(1)}, u32[]{:S(2)}, u32[]{:S(2)}) collective-permute-start(f32[2,160,128]{2,1,0:T(8,128)S(1)} %pad_maximum_fusion.3), channel_id=1, source_target_pairs={{0,4},{4,0},{8,12},{12,8},{16,20},{20,16},{24,28},{28,24},{1,5},{5... | collective-permute-start | bytes 491528 | tf_op jit(solution)/shard_map/ppermute | solution.py:30
  15.6 99.0 %all-to-all-start = ((f32[64,128,128]{2,1,0:T(8,128)}), f32[64,128,128]{2,1,0:T(8,128)}, u32[]{:S(2)}, u32[]{:S(2)}) async-start(f32[64,128,128]{2,1,0:T(8,128)} %after.2.refs_0_), calls=%async_computation | async-start | bytes 8388608 | tf_op jit(solution)/shard_map/all_to_all | solution.py:564
  24.4 0.7 copy-start.9
  25.1 31.8 %collective-permute-start.2 = (f32[2,2,160,128]{3,2,1,0:T(8,128)S(1)}, f32[2,2,160,128]{3,2,1,0:T(8,128)S(1)}, u32[]{:S(2)}, u32[]{:S(2)}) collective-permute-start(f32[2,2,160,128]{3,2,1,0:T(8,128)S(1)} %get-tuple-element.47), channel_id=1, source_target_pairs={{0,3},{1,2},{2,1},{3,0},{4,7},{5,6},{6,5},{7,4},{8,11},{9,10},{10,... | collective-permute-start | bytes 983048 | tf_op jit(solution)/shard_map/cond/branch_1_fun/ppermute | solution.py:48
  26.5 39.8 %collective-permute-start.1 = (f32[2,2,160,128]{3,2,1,0:T(8,128)S(1)}, f32[2,2,160,128]{3,2,1,0:T(8,128)S(1)}, u32[]{:S(2)}, u32[]{:S(2)}) collective-permute-start(f32[2,2,160,128]{3,2,1,0:T(8,128)S(1)} %get-tuple-element.47), channel_id=1, source_target_pairs={{0,2},{1,3},{2,0},{3,1},{4,6},{5,7},{6,4},{7,5},{8,10},{9,11},{10,... | collective-permute-start | bytes 983048 | tf_op jit(solution)/shard_map/cond/branch_1_fun/ppermute | solution.py:48
  26.8 39.5 %collective-permute-start = (f32[2,2,160,128]{3,2,1,0:T(8,128)S(1)}, f32[2,2,160,128]{3,2,1,0:T(8,128)S(1)}, u32[]{:S(2)}, u32[]{:S(2)}) collective-permute-start(f32[2,2,160,128]{3,2,1,0:T(8,128)S(1)} %get-tuple-element.47), channel_id=1, source_target_pairs={{0,1},{1,0},{2,3},{3,2},{4,5},{5,4},{6,7},{7,6},{8,9},{9,8},{10,11... | collective-permute-start | bytes 983048 | tf_op jit(solution)/shard_map/cond/branch_1_fun/ppermute | solution.py:48
  103.4 13.5 %copy-start.10 = (s32[3,64]{1,0:T(4,128)}, s32[3,64]{1,0:T(4,128)S(1)}, u32[]{:S(2)}) copy-start(s32[3,64]{1,0:T(4,128)S(1)} %get-tuple-element.79.list_ref) | copy-start | bytes 2308
  116.9 24.5 %collective-permute-start.14 = (f32[8,128,128]{2,1,0:T(8,128)S(1)}, f32[8,128,128]{2,1,0:T(8,128)S(1)}, u32[]{:S(2)}, u32[]{:S(2)}) collective-permute-start(f32[8,128,128]{2,1,0:T(8,128)S(1)} %add_panel_children.1.refs_0_.refs_4_), channel_id=1, source_target_pairs={{0,16},{4,20},{8,24},{12,28},{16,0},{20,4},{24,8},{28,12},{1,17},{... | collective-permute-start | bytes 1572872 | tf_op jit(solution)/shard_map/ppermute | solution.py:30
  120.0 24.1 %collective-permute-start.8 = (f32[8,128,128]{2,1,0:T(8,128)S(1)}, f32[8,128,128]{2,1,0:T(8,128)S(1)}, u32[]{:S(2)}, u32[]{:S(2)}) collective-permute-start(f32[8,128,128]{2,1,0:T(8,128)S(1)} %add_panel_children.1.refs_0_.refs_4_), channel_id=1, source_target_pairs={{0,2},{1,3},{2,0},{3,1},{4,6},{5,7},{6,4},{7,5},{8,10},{9,11},{10,... | collective-permute-start | bytes 1572872 | tf_op jit(solution)/shard_map/ppermute | solution.py:30
  120.0 26.4 %collective-permute-start.13 = (f32[8,128,128]{2,1,0:T(8,128)S(1)}, f32[8,128,128]{2,1,0:T(8,128)S(1)}, u32[]{:S(2)}, u32[]{:S(2)}) collective-permute-start(f32[8,128,128]{2,1,0:T(8,128)S(1)} %add_panel_children.1.refs_0_.refs_4_), channel_id=1, source_target_pairs={{0,12},{1,8},{2,4},{3,0},{4,13},{5,9},{6,5},{7,1},{8,14},{9,10},{1... | collective-permute-start | bytes 1572872 | tf_op jit(solution)/shard_map/ppermute | solution.py:614
  122.2 32.8 %collective-permute-start.12 = (f32[8,128,128]{2,1,0:T(8,128)S(1)}, f32[8,128,128]{2,1,0:T(8,128)S(1)}, u32[]{:S(2)}, u32[]{:S(2)}) collective-permute-start(f32[8,128,128]{2,1,0:T(8,128)S(1)} %add_panel_children.1.refs_0_.refs_4_), channel_id=1, source_target_pairs={{0,8},{1,12},{2,0},{3,4},{4,9},{5,13},{6,1},{7,5},{8,10},{9,14},{1... | collective-permute-start | bytes 1572872 | tf_op jit(solution)/shard_map/ppermute | solution.py:614
  122.4 34.4 %collective-permute-start.11 = (f32[8,128,128]{2,1,0:T(8,128)S(1)}, f32[8,128,128]{2,1,0:T(8,128)S(1)}, u32[]{:S(2)}, u32[]{:S(2)}) collective-permute-start(f32[8,128,128]{2,1,0:T(8,128)S(1)} %add_panel_children.1.refs_0_.refs_4_), channel_id=1, source_target_pairs={{0,4},{1,0},{2,12},{3,8},{4,5},{5,1},{6,13},{7,9},{8,6},{9,2},{10,... | collective-permute-start | bytes 1572872 | tf_op jit(solution)/shard_map/ppermute | solution.py:614
  141.5 16.2 %collective-permute-start.7 = (f32[8,128,128]{2,1,0:T(8,128)S(1)}, f32[8,128,128]{2,1,0:T(8,128)S(1)}, u32[]{:S(2)}, u32[]{:S(2)}) collective-permute-start(f32[8,128,128]{2,1,0:T(8,128)S(1)} %add_panel_children.1.refs_0_.refs_4_), channel_id=1, source_target_pairs={{0,1},{1,0},{2,3},{3,2},{4,5},{5,4},{6,7},{7,6},{8,9},{9,8},{10,11... | collective-permute-start | bytes 1572872 | tf_op jit(solution)/shard_map/ppermute | solution.py:30
  144.2 16.1 %collective-permute-start.9 = (f32[8,128,128]{2,1,0:T(8,128)S(1)}, f32[8,128,128]{2,1,0:T(8,128)S(1)}, u32[]{:S(2)}, u32[]{:S(2)}) collective-permute-start(f32[8,128,128]{2,1,0:T(8,128)S(1)} %collective-permute-done.8.refs_2_), channel_id=1, source_target_pairs={{0,1},{1,0},{2,3},{3,2},{4,5},{5,4},{6,7},{7,6},{8,9},{9,8},{10,11... | collective-permute-start | bytes 1572872 | tf_op jit(solution)/shard_map/ppermute | solution.py:30
  145.6 0.8 copy-start.1
  146.4 30.0 %collective-permute-start.10 = (f32[8,128,128]{2,1,0:T(8,128)S(1)}, f32[8,128,128]{2,1,0:T(8,128)}, u32[]{:S(2)}, u32[]{:S(2)}) collective-permute-start(f32[8,128,128]{2,1,0:T(8,128)S(1)} %add_panel_children.1.refs_0_.refs_4_), channel_id=1, source_target_pairs={{1,4},{2,8},{3,12},{4,1},{6,9},{7,13},{8,2},{9,6},{11,14},{12,3},{... | collective-permute-start | bytes 1572872 | tf_op jit(solution)/shard_map/ppermute | solution.py:614
  155.0 30.8 %collective-permute-start.18 = (f32[8,128,128]{2,1,0:T(8,128)S(1)}, f32[8,128,128]{2,1,0:T(8,128)S(1)}, u32[]{:S(2)}, u32[]{:S(2)}) collective-permute-start(f32[8,128,128]{2,1,0:T(8,128)S(1)} %collective-permute-done.14.refs_4_), channel_id=1, source_target_pairs={{0,12},{1,8},{2,4},{3,0},{4,13},{5,9},{6,5},{7,1},{8,14},{9,10},{1... | collective-permute-start | bytes 1572872 | tf_op jit(solution)/shard_map/ppermute | solution.py:614
  156.7 29.2 %collective-permute-start.17 = (f32[8,128,128]{2,1,0:T(8,128)S(1)}, f32[8,128,128]{2,1,0:T(8,128)}, u32[]{:S(2)}, u32[]{:S(2)}) collective-permute-start(f32[8,128,128]{2,1,0:T(8,128)S(1)} %collective-permute-done.14.refs_4_), channel_id=1, source_target_pairs={{0,8},{1,12},{2,0},{3,4},{4,9},{5,13},{6,1},{7,5},{8,10},{9,14},{1... | collective-permute-start | bytes 1572872 | tf_op jit(solution)/shard_map/ppermute | solution.py:614
  157.6 0.8 copy-start.3
  158.4 27.5 %collective-permute-start.16 = (f32[8,128,128]{2,1,0:T(8,128)S(1)}, f32[8,128,128]{2,1,0:T(8,128)}, u32[]{:S(2)}, u32[]{:S(2)}) collective-permute-start(f32[8,128,128]{2,1,0:T(8,128)S(1)} %collective-permute-done.14.refs_4_), channel_id=1, source_target_pairs={{0,4},{1,0},{2,12},{3,8},{4,5},{5,1},{6,13},{7,9},{8,6},{9,2},{10,... | collective-permute-start | bytes 1572872 | tf_op jit(solution)/shard_map/ppermute | solution.py:614
  160.2 0.8 copy-start.5
  161.0 25.2 %collective-permute-start.15 = (f32[8,128,128]{2,1,0:T(8,128)S(1)}, f32[8,128,128]{2,1,0:T(8,128)}, u32[]{:S(2)}, u32[]{:S(2)}) collective-permute-start(f32[8,128,128]{2,1,0:T(8,128)S(1)} %collective-permute-done.14.refs_4_), channel_id=1, source_target_pairs={{1,4},{2,8},{3,12},{4,1},{6,9},{7,13},{8,2},{9,6},{11,14},{12,3},{... | collective-permute-start | bytes 1572872 | tf_op jit(solution)/shard_map/ppermute | solution.py:614
  165.7 1.0 copy-start.2
  166.7 1.0 copy-start.4
  167.7 1.0 copy-start.6
  168.8 7.6 %copy-start.7 = (f32[256,256]{1,0:T(8,128)S(1)}, f32[256,256]{1,0:T(8,128)}, u32[]{:S(2)}) copy-start(f32[256,256]{1,0:T(8,128)} %get-tuple-element.91.a_ref) | copy-start | bytes 786436
  168.8 7.6 %copy-start.8 = (f32[256,256]{1,0:T(8,128)S(1)}, f32[256,256]{1,0:T(8,128)}, u32[]{:S(2)}) copy-start(f32[256,256]{1,0:T(8,128)} %get-tuple-element.90.l0_ref) | copy-start | bytes 786436
  168.8 7.6 %copy-start.11 = (s32[3,64]{1,0:T(4,128)S(1)}, s32[3,64]{1,0:T(4,128)}, u32[]{:S(2)}) copy-start(s32[3,64]{1,0:T(4,128)} %copy-done.10) | copy-start | bytes 2308

commit v4 on v3

--- a/solution.py
+++ b/solution.py
@@ -40,14 +40,15 @@
     return jnp.stack([jnp.where(low, x, other), jnp.where(low, other, x)])
 
 
-def gather_bits(x, axis, bits):
-    size = lax.axis_size(axis)
+def gather_bits(x, bits):
+    devices = lax.axis_size("prow") * lax.axis_size("pcol")
+    unit = {"prow": lax.axis_size("pcol"), "pcol": 1}
     masks = [0]
-    for bit in bits:
-        masks = [mask | on for mask in masks for on in (0, 1 << bit)]
-    sent = [lax.ppermute(x, axis, [(i, i ^ mask) for i in range(size)]) if mask else x for mask in masks]
+    for axis, bit in bits:
+        masks = [mask | on for mask in masks for on in (0, unit[axis] << bit)]
+    sent = [lax.ppermute(x, ALL, [(i, i ^ mask) for i in range(devices)]) if mask else x for mask in masks]
     whole = jnp.stack(sent).reshape((2,) * len(bits) + x.shape)
-    for dim, bit in enumerate(bits):
+    for dim, (axis, bit) in enumerate(bits):
         whole = jnp.where(my_bit(axis, bit) == 0, whole, jnp.flip(whole, dim))
     return whole
 
@@ -553,13 +554,12 @@
         same = owner[..., :, None] == owner[..., None, :]
         return jnp.sum((same & (index[None, :] < index[:, None])).astype(jnp.int32), axis=-1)
 
-    hops = list(reversed(range(1, row_bits)))
-    every = gather_bits(jnp.concatenate([corner, notes], axis=0), "prow", hops)
+    hops = [("prow", bit) for bit in reversed(range(1, row_bits))]
+    every = gather_bits(jnp.concatenate([corner, notes], axis=0), hops)
     corner = every[(0,) * (row_bits - panel_bits)][..., :tile, :]
     notes = every[..., tile:, :].reshape(-1, tile)
     corner = jnp.concatenate([corner, jnp.broadcast_to(notes, corner.shape[:-2] + notes.shape)], axis=-2)
     packed = pack(owner_ids * CAP + ranked(owner_ids), child_blocks, devices * CAP)
-    corner = gather_bit(corner, "prow", 0)
     send = after(packed, corner)
     got = lax.all_to_all(send, ALL, 0, 0, tiled=True)
     corner = after(corner, send)
@@ -572,7 +572,8 @@
     def beside_children(corner):
         corner, notes = spread(corner[..., :tile, :], corner[..., tile:, :], "pcol")
         corner = jnp.concatenate([corner, notes], axis=-2)
-        corner = jnp.swapaxes(gather_bits(corner, "pcol", list(reversed(range(panel_bits)))), 0, 1)
+        corner = gather_bits(corner, [("pcol", bit) for bit in range(1, panel_bits)] + [("prow", 0)])
+        corner = gather_bit(corner, "pcol", 0)
         l0, *z0 = factor_panel0(corner)
         a, ah, al, l1, *z1 = factor_panel1(corner, pattern, z0)
 

time: 198 us -> 194 us (0.980)
  waiting for transfers between devices: 78 us -> 70.1 us
  starting transfers between devices: 38.3 us -> 40.8 us
    ppermute x6, waiting for transfers between devices: 43.6 us -> 30.2 us  [gather_bits(): lax.ppermute(x, ALL, [(i, i ^ mask) for i in range(devices)])]
    all_to_all x1, waiting for transfers between devices: 11.2 us -> 17.8 us  [local(): got = lax.all_to_all(send, ALL, 0, 0, tiled=True)]
    unnamed x26 -> x28, local copies, waits for them, and re-layouts: 6.33 us -> 7.15 us
  transfers between devices with their start and end apart: 20 -> 20, of which waited for: 11 -> 7; matrix products, arithmetic and copies ran while one was open for 2% -> 3% of each run, Pallas kernels for 28% -> 28%
where the time goes in v4:
time: 194 us; the launch traced here: 192 us
  waiting for transfers between devices  70.1 us (36%)
  Pallas kernels  65.8 us (34%)
  starting transfers between devices  40.8 us (21%)
  local copies, waits for them, and re-layouts  9.69 us (5%)
  other arithmetic  4.88 us (3%)
    ppermute x6, waiting for transfers between devices, gather_bits(): lax.ppermute(x, ALL, [(i, i ^ mask) for i in range(devices)])  30.2 us
    ppermute x8, starting transfers between devices, to_column(): lax.ppermute(part, ALL, [(source, target) for source, target in pairs if...  20 us
    pallas_call x2, Pallas kernels, schur_share(): pl.pallas_call(functools.partial(schur_kernel, panel_blocks), out_shape=j...  19.3 us
    pallas_call x1, Pallas kernels, factor_panel1(): pl.pallas_call(panel1_kernel, out_shape=(full, part, part, full, part, pa...  18.7 us
    all_to_all x1, waiting for transfers between devices, local(): got = lax.all_to_all(send, ALL, 0, 0, tiled=True)  17.8 us
    ppermute x5, waiting for transfers between devices, xor_send(): return lax.ppermute(x, axis, [(i, i ^ 1 << bit) for i in range(size)])  17.5 us
    pallas_call x1, Pallas kernels, factor_panel0(): pl.pallas_call(panel0_kernel, out_shape=(full, part, part), in_specs=[WHO...  16.2 us
    all_to_all x1, starting transfers between devices, local(): got = lax.all_to_all(send, ALL, 0, 0, tiled=True)  8 us
  transfers between devices with their start and end apart: 20, of which 7 were waited for; matrix products, arithmetic and copies ran while one was open for 3% of the time, Pallas kernels for 28%

profile of v4, /device:TPU:9, one launch (start us, length us, event | category | flops | bytes accessed | tf_op | source)
XLA Modules:
  0.0 192.0 jit_solution(16526203369284857684)
XLA Ops:
  0.0 0.7 convert_bitcast_fusion
  0.7 0.7 convert_bitcast_fusion.1
  1.3 0.8 slice_bitcast_fusion.4
  2.4 2.4 %collective-permute-start.5 = (f32[136,128]{1,0:T(8,128)S(1)}, f32[136,128]{1,0:T(8,128)S(1)}, u32[]{:S(2)}, u32[]{:S(2)}) collective-permute-start(f32[136,128]{1,0:T(8,128)S(1)} %get-tuple-element.116), channel_id=1, source_target_pairs={{0,16},{1,17},{2,18},{3,19},{4,20},{5,21},{6,22},{7,23},{8,24},{9,... | collective-permute-start | bytes 208904 | tf_op jit(solution)/shard_map/ppermute | solution.py:49
  4.9 0.2 collective-permute-start.6
  5.1 0.9 convert_reduce_fusion.5
  6.0 0.7 multiply_add_fusion.1.place_ref
  6.7 1.6 copy-done
  8.3 2.1 %pack_children.1.x_ref = f32[64,128,128]{2,1,0:T(8,128)} custom-call(s32[32]{0:T(128)S(1)} %multiply_add_fusion.1.place_ref, f32[32,128,128]{2,1,0:T(8,128)S(1)} %copy-done), custom_call_target="tpu_custom_call" | custom-call | tf_op jit(solution)/shard_map/pack_children/pallas_call | solution.py:112
  10.8 8.0 %all-to-all-start = ((f32[64,128,128]{2,1,0:T(8,128)}), f32[64,128,128]{2,1,0:T(8,128)}, u32[]{:S(2)}, u32[]{:S(2)}) async-start(f32[64,128,128]{2,1,0:T(8,128)} %after.2.refs_0_), calls=%async_computation | async-start | bytes 8388608 | tf_op jit(solution)/shard_map/all_to_all | solution.py:564
  18.8 1.1 slice_bitcast_fusion.2.strip_ref
  20.0 72.3 %conditional.1 = (f32[256,256]{1,0:T(8,128)S(1)}, f32[256,256]{1,0:T(8,128)S(1)}, f32[256,256]{1,0:T(8,128)S(1)}, bf16[256,256]{1,0:T(8,128)(2,1)}, bf16[256,256...) conditional(s32[]{:T(128)} %bitcast.21, () %tuple.22, ...), branch_computations={%region_1.0_spmd, %region_2.14_spmd} | conditional | flops 1912849 | bytes 15280202 | solution.py:93
  20.0 2.1 %collective-permute-start.2 = (f32[2,160,128]{2,1,0:T(8,128)S(1)}, f32[2,160,128]{2,1,0:T(8,128)S(1)}, u32[]{:S(2)}, u32[]{:S(2)}) collective-permute-start(f32[2,160,128]{2,1,0:T(8,128)S(1)} %get-tuple-element.47), channel_id=1, source_target_pairs={{0,6},{1,7},{2,4},{3,5},{4,2},{5,3},{6,0},{7,1},{8,14},{9,15},{10,... | collective-permute-start | bytes 491528 | tf_op jit(solution)/shard_map/cond/branch_1_fun/ppermute | solution.py:49
  22.1 0.3 collective-permute-start.1
  22.4 0.3 collective-permute-start
  22.7 29.2 %collective-permute-done.2 = f32[2,160,128]{2,1,0:T(8,128)S(1)} collective-permute-done((f32[2,160,128]{2,1,0:T(8,128)S(1)}, f32[2,160,128]{2,1,0:T(8,128)S(1)}, u32[]{:S(2)}, u32[]{:S(2)}) %collective-permute-start.2) | collective-permute-done | bytes 163872 | tf_op jit(solution)/shard_map/cond/branch_1_fun/ppermute | solution.py:49
  51.9 0.8 collective-permute-done.1
  52.9 0.9 collective-permute-start.3
  53.9 1.6 collective-permute-done.3
  55.8 0.8 convert_reduce_fusion
  57.0 16.2 %factor_panel0.1 = (f32[256,256]{1,0:T(8,128)S(1)}, bf16[256,256]{1,0:T(8,128)(2,1)}, bf16[256,256]{1,0:T(8,128)(2,1)}) custom-call(f32[2,2,2,2,160,128]{5,4,3,2,1,0:T(8,128)S(1)} %pad_maximum_fusion.corner_ref), custom_call_target="tpu_custom_call" | custom-call | tf_op jit(solution)/shard_map/cond/branch_1_fun/factor_panel0/pallas_call | solution.py:275
  73.4 0.2 select_reduce_fusion.1
  73.6 18.7 %factor_panel1.1 = (f32[256,256]{1,0:T(8,128)S(1)}, bf16[256,256]{1,0:T(8,128)(2,1)}, bf16[256,256]{1,0:T(8,128)(2,1)}, f32[256,256]{1,0:T(8,128)S(1)}, bf16[256...) custom-call(s32[2,64]{1,0:T(2,128)S(1)} %get-tuple-element.49.pattern_ref, ...), custom_call_target="tpu_custom_call" | custom-call | tf_op jit(solution)/shard_map/cond/branch_1_fun/factor_panel1/pallas_call | solution.py:290
  92.3 17.8 %all-to-all-done.got_ref = f32[64,128,128]{2,1,0:T(8,128)} async-done(((f32[64,128,128]{2,1,0:T(8,128)}), f32[64,128,128]{2,1,0:T(8,128)}, u32[]{:S(2)}, u32[]{:S(2)}) %all-to-all-start) | async-done | bytes 4194336 | tf_op jit(solution)/shard_map/all_to_all | solution.py:564
  110.1 2.0 %add_panel_children.1.refs_0_.refs_4_ = f32[8,128,128]{2,1,0:T(8,128)S(1)} custom-call(s32[64]{0:T(128)S(1)} %get-tuple-element.80.row_ref, f32[8,128,128]{2,1,0:T(8,128)S(1)} %slice_bitcast_fusion.2.strip_ref, f32[64,128,128]{2,1,0:T(8,128)} %all-to-all-done.got_ref), custom_call_target="tpu_custom_call" | custom-call | tf_op jit(solution)/shard_map/add_panel_children/pallas_call | solution.py:145
  112.1 3.2 %collective-permute-start.14 = (f32[8,128,128]{2,1,0:T(8,128)S(1)}, f32[8,128,128]{2,1,0:T(8,128)S(1)}, u32[]{:S(2)}, u32[]{:S(2)}) collective-permute-start(f32[8,128,128]{2,1,0:T(8,128)S(1)} %add_panel_children.1.refs_0_.refs_4_), channel_id=1, source_target_pairs={{0,16},{4,20},{8,24},{12,28},{16,0},{20,4},{24,8},{28,12},{1,17},{... | collective-permute-start | bytes 1572872 | tf_op jit(solution)/shard_map/ppermute | solution.py:30
  115.2 0.5 collective-permute-start.8
  115.7 2.2 %collective-permute-start.13 = (f32[8,128,128]{2,1,0:T(8,128)S(1)}, f32[8,128,128]{2,1,0:T(8,128)S(1)}, u32[]{:S(2)}, u32[]{:S(2)}) collective-permute-start(f32[8,128,128]{2,1,0:T(8,128)S(1)} %add_panel_children.1.refs_0_.refs_4_), channel_id=1, source_target_pairs={{0,12},{1,8},{2,4},{3,0},{4,13},{5,9},{6,5},{7,1},{8,14},{9,10},{1... | collective-permute-start | bytes 1572872 | tf_op jit(solution)/shard_map/ppermute | solution.py:615
  117.9 0.8 collective-permute-start.12
  118.7 3.4 %collective-permute-start.11 = (f32[8,128,128]{2,1,0:T(8,128)S(1)}, f32[8,128,128]{2,1,0:T(8,128)S(1)}, u32[]{:S(2)}, u32[]{:S(2)}) collective-permute-start(f32[8,128,128]{2,1,0:T(8,128)S(1)} %add_panel_children.1.refs_0_.refs_4_), channel_id=1, source_target_pairs={{0,4},{1,0},{2,12},{3,8},{4,5},{5,1},{6,13},{7,9},{8,6},{9,2},{10,... | collective-permute-start | bytes 1572872 | tf_op jit(solution)/shard_map/ppermute | solution.py:615
  122.1 15.9 %collective-permute-done.14.refs_4_ = f32[8,128,128]{2,1,0:T(8,128)S(1)} collective-permute-done((f32[8,128,128]{2,1,0:T(8,128)S(1)}, f32[8,128,128]{2,1,0:T(8,128)S(1)}, u32[]{:S(2)}, u32[]{:S(2)}) %collective-permute-start.14) | collective-permute-done | bytes 524320 | tf_op jit(solution)/shard_map/ppermute | solution.py:30
  138.0 0.7 collective-permute-start.7
  138.7 2.2 %collective-permute-start.9 = (f32[8,128,128]{2,1,0:T(8,128)S(1)}, f32[8,128,128]{2,1,0:T(8,128)S(1)}, u32[]{:S(2)}, u32[]{:S(2)}) collective-permute-start(f32[8,128,128]{2,1,0:T(8,128)S(1)} %collective-permute-done.8.refs_2_), channel_id=1, source_target_pairs={{0,1},{1,0},{2,3},{3,2},{4,5},{5,4},{6,7},{7,6},{8,9},{9,8},{10,11... | collective-permute-start | bytes 1572872 | tf_op jit(solution)/shard_map/ppermute | solution.py:30
  140.8 0.8 copy-done.1
  141.6 4.3 %collective-permute-start.10 = (f32[8,128,128]{2,1,0:T(8,128)S(1)}, f32[8,128,128]{2,1,0:T(8,128)}, u32[]{:S(2)}, u32[]{:S(2)}) collective-permute-start(f32[8,128,128]{2,1,0:T(8,128)S(1)} %add_panel_children.1.refs_0_.refs_4_), channel_id=1, source_target_pairs={{1,4},{2,8},{3,12},{4,1},{6,9},{7,13},{8,2},{9,6},{11,14},{12,3},{... | collective-permute-start | bytes 1572872 | tf_op jit(solution)/shard_map/ppermute | solution.py:615
  145.9 4.6 %collective-permute-done.12.refs_2_ = f32[8,128,128]{2,1,0:T(8,128)S(1)} collective-permute-done((f32[8,128,128]{2,1,0:T(8,128)S(1)}, f32[8,128,128]{2,1,0:T(8,128)S(1)}, u32[]{:S(2)}, u32[]{:S(2)}) %collective-permute-start.12) | collective-permute-done | bytes 524320 | tf_op jit(solution)/shard_map/ppermute | solution.py:615
  150.5 2.0 %collective-permute-start.18 = (f32[8,128,128]{2,1,0:T(8,128)S(1)}, f32[8,128,128]{2,1,0:T(8,128)S(1)}, u32[]{:S(2)}, u32[]{:S(2)}) collective-permute-start(f32[8,128,128]{2,1,0:T(8,128)S(1)} %collective-permute-done.14.refs_4_), channel_id=1, source_target_pairs={{0,12},{1,8},{2,4},{3,0},{4,13},{5,9},{6,5},{7,1},{8,14},{9,10},{1... | collective-permute-start | bytes 1572872 | tf_op jit(solution)/shard_map/ppermute | solution.py:615
  152.4 1.3 collective-permute-start.17
  153.7 0.8 copy-done.3
  154.5 1.9 %collective-permute-start.16 = (f32[8,128,128]{2,1,0:T(8,128)S(1)}, f32[8,128,128]{2,1,0:T(8,128)}, u32[]{:S(2)}, u32[]{:S(2)}) collective-permute-start(f32[8,128,128]{2,1,0:T(8,128)S(1)} %collective-permute-done.14.refs_4_), channel_id=1, source_target_pairs={{0,4},{1,0},{2,12},{3,8},{4,5},{5,1},{6,13},{7,9},{8,6},{9,2},{10,... | collective-permute-start | bytes 1572872 | tf_op jit(solution)/shard_map/ppermute | solution.py:615
  156.5 0.8 copy-done.5
  157.3 4.2 %collective-permute-start.15 = (f32[8,128,128]{2,1,0:T(8,128)S(1)}, f32[8,128,128]{2,1,0:T(8,128)}, u32[]{:S(2)}, u32[]{:S(2)}) collective-permute-start(f32[8,128,128]{2,1,0:T(8,128)S(1)} %collective-permute-done.14.refs_4_), channel_id=1, source_target_pairs={{1,4},{2,8},{3,12},{4,1},{6,9},{7,13},{8,2},{9,6},{11,14},{12,3},{... | collective-permute-start | bytes 1572872 | tf_op jit(solution)/shard_map/ppermute | solution.py:615
  161.7 1.0 copy-done.2
  162.7 1.0 copy-done.4
  163.8 1.0 copy-done.6
  164.8 7.6 %solve_rows.1 = (bf16[1024,512]{1,0:T(8,128)(2,1)S(1)}, bf16[1024,512]{1,0:T(8,128)(2,1)S(1)}, f32[8,128,128]{2,1,0:T(8,128)S(1)}) custom-call(s32[2,64]{1,0:T(2,128)S(1)} %copy-done.11, s32[3]{0:T(128)S(1)} %pad_add_fusion.3.place_ref, f32[8,128,128]{2,1,0:T(8,128)S(1)} %add_panel_children.1.refs_0_.refs_4_, f32[8,128,128]{2,1,0:T(8,128)S(1)} %copy-done.4, ...), custom_call_target="tpu_custom_call" | custom-call | tf_op jit(solution)/shard_map/solve_rows/pallas_call | solution.py:361
  172.4 10.0 %schur_share.2.before_ref = f32[8,8,2,128,128]{4,3,2,1,0:T(8,128)} custom-call(s32[3,64]{1,0:T(4,128)} %copy-done.12, s32[2,64]{1,0:T(2,128)S(1)} %copy-done.11, s32[5]{0:T(128)S(1)} %stack.107.place_ref, f32[8,8,2,128,128]{4,3,2,1,0:T(8,128)} %bitcast.62, f32[8,8,2,128,128]{4,3,2,1,0:T(8,128)} %bitcast.63, f32[64,128,128]{2,1,0:T(8,128)} %all-to-all-done.got_ref, ...), custom_call_target="tpu_custom_call" | custom-call | tf_op jit(solution)/shard_map/schur_share/pallas_call | solution.py:482
  182.5 9.3 %schur_share.3 = f32[8,8,2,128,128]{4,3,2,1,0:T(8,128)} custom-call(s32[3,64]{1,0:T(4,128)S(1)} %get-tuple-element.78.list_ref, s32[2,64]{1,0:T(2,128)S(1)} %copy-done.11, s32[5]{0:T(128)S(1)} %stack.105.place_ref, f32[8,8,2,128,128]{4,3,2,1,0:T(8,128)} %schur_share.2.before_ref, f32[8,8,2,128,128]{4,3,2,1,0:T(8,128)} %bitcast.64, ...), custom_call_target="tpu_custom_call", output_to_operand_aliasing={{}: (3, {})} | custom-call | tf_op jit(solution)/shard_map/schur_share/pallas_call | solution.py:482
  (73 shorter events, 2.0 us)
Async XLA Ops:
  2.4 8.0 %collective-permute-start.5 = (f32[136,128]{1,0:T(8,128)S(1)}, f32[136,128]{1,0:T(8,128)S(1)}, u32[]{:S(2)}, u32[]{:S(2)}) collective-permute-start(f32[136,128]{1,0:T(8,128)S(1)} %get-tuple-element.116), channel_id=1, source_target_pairs={{0,16},{1,17},{2,18},{3,19},{4,20},{5,21},{6,22},{7,23},{8,24},{9,... | collective-permute-start | bytes 208904 | tf_op jit(solution)/shard_map/ppermute | solution.py:49
  4.8 5.7 %collective-permute-start.4 = (f32[136,128]{1,0:T(8,128)S(1)}, f32[136,128]{1,0:T(8,128)S(1)}, u32[]{:S(2)}, u32[]{:S(2)}) collective-permute-start(f32[136,128]{1,0:T(8,128)S(1)} %get-tuple-element.116), channel_id=1, source_target_pairs={{0,8},{1,9},{2,10},{3,11},{4,12},{5,13},{6,14},{7,15},{8,0},{9,1},... | collective-permute-start | bytes 208904 | tf_op jit(solution)/shard_map/ppermute | solution.py:49
  4.9 5.6 %collective-permute-start.6 = (f32[136,128]{1,0:T(8,128)S(1)}, f32[136,128]{1,0:T(8,128)S(1)}, u32[]{:S(2)}, u32[]{:S(2)}) collective-permute-start(f32[136,128]{1,0:T(8,128)S(1)} %get-tuple-element.116), channel_id=1, source_target_pairs={{0,24},{1,25},{2,26},{3,27},{4,28},{5,29},{6,30},{7,31},{8,16},{9,... | collective-permute-start | bytes 208904 | tf_op jit(solution)/shard_map/ppermute | solution.py:49
  6.7 1.6 copy-start
  10.7 8.1 %copy-start.13 = (s32[32,1]{0,1:T(1,128)S(1)}, s32[32,1]{0,1:T(1,128)}, u32[]{:S(2)}) copy-start(s32[32,1]{0,1:T(1,128)} %param.13) | copy-start | bytes 388
  10.8 99.3 %all-to-all-start = ((f32[64,128,128]{2,1,0:T(8,128)}), f32[64,128,128]{2,1,0:T(8,128)}, u32[]{:S(2)}, u32[]{:S(2)}) async-start(f32[64,128,128]{2,1,0:T(8,128)} %after.2.refs_0_), calls=%async_computation | async-start | bytes 8388608 | tf_op jit(solution)/shard_map/all_to_all | solution.py:564
  18.8 1.2 copy-start.11
  20.0 31.9 %collective-permute-start.2 = (f32[2,160,128]{2,1,0:T(8,128)S(1)}, f32[2,160,128]{2,1,0:T(8,128)S(1)}, u32[]{:S(2)}, u32[]{:S(2)}) collective-permute-start(f32[2,160,128]{2,1,0:T(8,128)S(1)} %get-tuple-element.47), channel_id=1, source_target_pairs={{0,6},{1,7},{2,4},{3,5},{4,2},{5,3},{6,0},{7,1},{8,14},{9,15},{10,... | collective-permute-start | bytes 491528 | tf_op jit(solution)/shard_map/cond/branch_1_fun/ppermute | solution.py:49
  22.1 30.6 %collective-permute-start.1 = (f32[2,160,128]{2,1,0:T(8,128)S(1)}, f32[2,160,128]{2,1,0:T(8,128)S(1)}, u32[]{:S(2)}, u32[]{:S(2)}) collective-permute-start(f32[2,160,128]{2,1,0:T(8,128)S(1)} %get-tuple-element.47), channel_id=1, source_target_pairs={{0,2},{1,3},{2,0},{3,1},{4,6},{5,7},{6,4},{7,5},{8,10},{9,11},{10,... | collective-permute-start | bytes 491528 | tf_op jit(solution)/shard_map/cond/branch_1_fun/ppermute | solution.py:49
  22.4 30.3 %collective-permute-start = (f32[2,160,128]{2,1,0:T(8,128)S(1)}, f32[2,160,128]{2,1,0:T(8,128)S(1)}, u32[]{:S(2)}, u32[]{:S(2)}) collective-permute-start(f32[2,160,128]{2,1,0:T(8,128)S(1)} %get-tuple-element.47), channel_id=1, source_target_pairs={{0,4},{1,5},{2,6},{3,7},{4,0},{5,1},{6,2},{7,3},{8,12},{9,13},{10,... | collective-permute-start | bytes 491528 | tf_op jit(solution)/shard_map/cond/branch_1_fun/ppermute | solution.py:49
  52.9 2.7 %collective-permute-start.3 = (f32[2,2,2,160,128]{4,3,2,1,0:T(8,128)S(1)}, f32[2,2,2,160,128]{4,3,2,1,0:T(8,128)S(1)}, u32[]{:S(2)}, u32[]{:S(2)}) collective-permute-start(f32[2,2,2,160,128]{4,3,2,1,0:T(8,128)S(1)} %reverse_select_fusion), channel_id=1, source_target_pairs={{0,1},{1,0},{2,3},{3,2},{4,5},{5,4},{6,7},{7,6},{8,9},{9,8},{10,11... | collective-permute-start | bytes 1966088 | tf_op jit(solution)/shard_map/cond/branch_1_fun/ppermute | solution.py:30
  92.3 23.4 %copy-start.7 = (f32[256,256]{1,0:T(8,128)}, f32[256,256]{1,0:T(8,128)S(1)}, u32[]{:S(2)}) copy-start(f32[256,256]{1,0:T(8,128)S(1)} %get-tuple-element.91.a_ref) | copy-start | bytes 786436
  92.3 25.6 %copy-start.9 = (f32[256,256]{1,0:T(8,128)}, f32[256,256]{1,0:T(8,128)S(1)}, u32[]{:S(2)}) copy-start(f32[256,256]{1,0:T(8,128)S(1)} %get-tuple-element.90.l0_ref) | copy-start | bytes 786436
  92.3 25.6 %copy-start.12 = (s32[3,64]{1,0:T(4,128)}, s32[3,64]{1,0:T(4,128)S(1)}, u32[]{:S(2)}) copy-start(s32[3,64]{1,0:T(4,128)S(1)} %get-tuple-element.79.list_ref) | copy-start | bytes 2308
  112.1 25.9 %collective-permute-start.14 = (f32[8,128,128]{2,1,0:T(8,128)S(1)}, f32[8,128,128]{2,1,0:T(8,128)S(1)}, u32[]{:S(2)}, u32[]{:S(2)}) collective-permute-start(f32[8,128,128]{2,1,0:T(8,128)S(1)} %add_panel_children.1.refs_0_.refs_4_), channel_id=1, source_target_pairs={{0,16},{4,20},{8,24},{12,28},{16,0},{20,4},{24,8},{28,12},{1,17},{... | collective-permute-start | bytes 1572872 | tf_op jit(solution)/shard_map/ppermute | solution.py:30
  115.2 23.4 %collective-permute-start.8 = (f32[8,128,128]{2,1,0:T(8,128)S(1)}, f32[8,128,128]{2,1,0:T(8,128)S(1)}, u32[]{:S(2)}, u32[]{:S(2)}) collective-permute-start(f32[8,128,128]{2,1,0:T(8,128)S(1)} %add_panel_children.1.refs_0_.refs_4_), channel_id=1, source_target_pairs={{0,2},{1,3},{2,0},{3,1},{4,6},{5,7},{6,4},{7,5},{8,10},{9,11},{10,... | collective-permute-start | bytes 1572872 | tf_op jit(solution)/shard_map/ppermute | solution.py:30
  115.7 25.9 %collective-permute-start.13 = (f32[8,128,128]{2,1,0:T(8,128)S(1)}, f32[8,128,128]{2,1,0:T(8,128)S(1)}, u32[]{:S(2)}, u32[]{:S(2)}) collective-permute-start(f32[8,128,128]{2,1,0:T(8,128)S(1)} %add_panel_children.1.refs_0_.refs_4_), channel_id=1, source_target_pairs={{0,12},{1,8},{2,4},{3,0},{4,13},{5,9},{6,5},{7,1},{8,14},{9,10},{1... | collective-permute-start | bytes 1572872 | tf_op jit(solution)/shard_map/ppermute | solution.py:615
  117.9 32.6 %collective-permute-start.12 = (f32[8,128,128]{2,1,0:T(8,128)S(1)}, f32[8,128,128]{2,1,0:T(8,128)S(1)}, u32[]{:S(2)}, u32[]{:S(2)}) collective-permute-start(f32[8,128,128]{2,1,0:T(8,128)S(1)} %add_panel_children.1.refs_0_.refs_4_), channel_id=1, source_target_pairs={{0,8},{1,12},{2,0},{3,4},{4,9},{5,13},{6,1},{7,5},{8,10},{9,14},{1... | collective-permute-start | bytes 1572872 | tf_op jit(solution)/shard_map/ppermute | solution.py:615
  118.7 33.8 %collective-permute-start.11 = (f32[8,128,128]{2,1,0:T(8,128)S(1)}, f32[8,128,128]{2,1,0:T(8,128)S(1)}, u32[]{:S(2)}, u32[]{:S(2)}) collective-permute-start(f32[8,128,128]{2,1,0:T(8,128)S(1)} %add_panel_children.1.refs_0_.refs_4_), channel_id=1, source_target_pairs={{0,4},{1,0},{2,12},{3,8},{4,5},{5,1},{6,13},{7,9},{8,6},{9,2},{10,... | collective-permute-start | bytes 1572872 | tf_op jit(solution)/shard_map/ppermute | solution.py:615
  138.0 15.7 %collective-permute-start.7 = (f32[8,128,128]{2,1,0:T(8,128)S(1)}, f32[8,128,128]{2,1,0:T(8,128)S(1)}, u32[]{:S(2)}, u32[]{:S(2)}) collective-permute-start(f32[8,128,128]{2,1,0:T(8,128)S(1)} %add_panel_children.1.refs_0_.refs_4_), channel_id=1, source_target_pairs={{0,1},{1,0},{2,3},{3,2},{4,5},{5,4},{6,7},{7,6},{8,9},{9,8},{10,11... | collective-permute-start | bytes 1572872 | tf_op jit(solution)/shard_map/ppermute | solution.py:30
  138.7 17.8 %collective-permute-start.9 = (f32[8,128,128]{2,1,0:T(8,128)S(1)}, f32[8,128,128]{2,1,0:T(8,128)S(1)}, u32[]{:S(2)}, u32[]{:S(2)}) collective-permute-start(f32[8,128,128]{2,1,0:T(8,128)S(1)} %collective-permute-done.8.refs_2_), channel_id=1, source_target_pairs={{0,1},{1,0},{2,3},{3,2},{4,5},{5,4},{6,7},{7,6},{8,9},{9,8},{10,11... | collective-permute-start | bytes 1572872 | tf_op jit(solution)/shard_map/ppermute | solution.py:30
  140.8 0.8 copy-start.1
  141.6 30.8 %collective-permute-start.10 = (f32[8,128,128]{2,1,0:T(8,128)S(1)}, f32[8,128,128]{2,1,0:T(8,128)}, u32[]{:S(2)}, u32[]{:S(2)}) collective-permute-start(f32[8,128,128]{2,1,0:T(8,128)S(1)} %add_panel_children.1.refs_0_.refs_4_), channel_id=1, source_target_pairs={{1,4},{2,8},{3,12},{4,1},{6,9},{7,13},{8,2},{9,6},{11,14},{12,3},{... | collective-permute-start | bytes 1572872 | tf_op jit(solution)/shard_map/ppermute | solution.py:615
  150.5 32.0 %collective-permute-start.18 = (f32[8,128,128]{2,1,0:T(8,128)S(1)}, f32[8,128,128]{2,1,0:T(8,128)S(1)}, u32[]{:S(2)}, u32[]{:S(2)}) collective-permute-start(f32[8,128,128]{2,1,0:T(8,128)S(1)} %collective-permute-done.14.refs_4_), channel_id=1, source_target_pairs={{0,12},{1,8},{2,4},{3,0},{4,13},{5,9},{6,5},{7,1},{8,14},{9,10},{1... | collective-permute-start | bytes 1572872 | tf_op jit(solution)/shard_map/ppermute | solution.py:615
  152.4 30.0 %collective-permute-start.17 = (f32[8,128,128]{2,1,0:T(8,128)S(1)}, f32[8,128,128]{2,1,0:T(8,128)}, u32[]{:S(2)}, u32[]{:S(2)}) collective-permute-start(f32[8,128,128]{2,1,0:T(8,128)S(1)} %collective-permute-done.14.refs_4_), channel_id=1, source_target_pairs={{0,8},{1,12},{2,0},{3,4},{4,9},{5,13},{6,1},{7,5},{8,10},{9,14},{1... | collective-permute-start | bytes 1572872 | tf_op jit(solution)/shard_map/ppermute | solution.py:615
  153.7 0.8 copy-start.3
  154.5 28.0 %collective-permute-start.16 = (f32[8,128,128]{2,1,0:T(8,128)S(1)}, f32[8,128,128]{2,1,0:T(8,128)}, u32[]{:S(2)}, u32[]{:S(2)}) collective-permute-start(f32[8,128,128]{2,1,0:T(8,128)S(1)} %collective-permute-done.14.refs_4_), channel_id=1, source_target_pairs={{0,4},{1,0},{2,12},{3,8},{4,5},{5,1},{6,13},{7,9},{8,6},{9,2},{10,... | collective-permute-start | bytes 1572872 | tf_op jit(solution)/shard_map/ppermute | solution.py:615
  156.5 0.8 copy-start.5
  157.3 25.2 %collective-permute-start.15 = (f32[8,128,128]{2,1,0:T(8,128)S(1)}, f32[8,128,128]{2,1,0:T(8,128)}, u32[]{:S(2)}, u32[]{:S(2)}) collective-permute-start(f32[8,128,128]{2,1,0:T(8,128)S(1)} %collective-permute-done.14.refs_4_), channel_id=1, source_target_pairs={{1,4},{2,8},{3,12},{4,1},{6,9},{7,13},{8,2},{9,6},{11,14},{12,3},{... | collective-permute-start | bytes 1572872 | tf_op jit(solution)/shard_map/ppermute | solution.py:615
  161.7 1.0 copy-start.2
  162.7 1.0 copy-start.4
  163.8 1.0 copy-start.6
  172.4 10.1 %copy-start.8 = (f32[256,256]{1,0:T(8,128)S(1)}, f32[256,256]{1,0:T(8,128)}, u32[]{:S(2)}) copy-start(f32[256,256]{1,0:T(8,128)} %copy-done.7) | copy-start | bytes 786436
  172.4 10.1 %copy-start.10 = (f32[256,256]{1,0:T(8,128)S(1)}, f32[256,256]{1,0:T(8,128)}, u32[]{:S(2)}) copy-start(f32[256,256]{1,0:T(8,128)} %copy-done.9) | copy-start | bytes 786436
